TPU v7x, 32 devices: a whole 2x2x4 slice. The times are simulated.
32 devices in a mesh: dp: 8 (over y, x, core), replica: 4 (over z).
Axes of the slice: x: 2, y: 2, z: 4, core: 2. Of those that a mesh axis runs over, the one named last changes fastest.
Arguments:
- tokens: bfloat16 [4, 1024, 1024], P('replica', 'dp'), may hold values from -6 to 6
- user_of_row: int32 [4, 1024], P('replica'), may hold values from 0 to 31, as said below
- proj_weight: bfloat16 [1024, 1536], replicated
- norm_gain: float32 [512], replicated, may hold values from 0.5 to 1.5
- grad_out: bfloat16 [4, 2048, 512], P('replica', 'dp'), may hold values from -6 to 6
Outputs:
- attended: bfloat16 [4, 2048, 512], P('replica', 'dp')
- grad_tokens: bfloat16 [4, 1024, 1024], P('replica', 'dp')
- grad_weight: float32 [1024, 1536], P('dp')
Inputs may be any that keep to these rules, and one draw needn't show every extreme that they name: `user_of_row`: user u belongs to owner u // 4. Among the 128 rows of one source device in one batch at most 32 belong to users of any one owner, and in every batch one owner gets exactly 32 rows from every source.
All inputs are finite; a program needn't handle non-finite values.
Results may differ from a plain program's by a relative error of at most 0.0068.
Values may be sent and summed in bfloat16 or wider, within the bound.
No kernel may reach another device: no remote copies, remote signals or barrier semaphores. Data moves between devices by JAX's collectives and lax.ppermute only.
A program may use at most 64 MiB of HBM per device.

v0:
```python
import jax
import jax.numpy as jnp
from jax import lax
from jax.sharding import PartitionSpec as P

HEADS = 4
HEAD_DIM = 128
UPO = 4


def silu_grad(preact):
    sigmoid_p = jax.nn.sigmoid(preact)
    return sigmoid_p * (1.0 + preact * (1.0 - sigmoid_p))


def attend(activated, gain, slot_user, slot_order):
    slot_total = activated.shape[0]
    split_acts = activated.astype(jnp.float32).reshape(slot_total, 3, HEADS, HEAD_DIM)
    queries = split_acts[:, 0]
    keys_h = split_acts[:, 1]
    values = split_acts[:, 2]
    scores = jnp.einsum(
        "qhd,khd->hqk", queries, keys_h, precision=lax.Precision.HIGHEST
    ) * HEAD_DIM ** (-0.5)
    visible = (
        (slot_user[:, None] == slot_user[None, :])
        & (slot_order[None, :] <= slot_order[:, None])
        & (slot_user[:, None] >= 0)
    )
    weights = jnp.where(visible[None], jax.nn.silu(scores), 0.0)
    mixed = jnp.einsum("hqk,khd->qhd", weights, values, precision=lax.Precision.HIGHEST).reshape(
        slot_total, HEADS * HEAD_DIM
    )
    mean_row = jnp.mean(mixed, axis=1, keepdims=True)
    centered = mixed - mean_row
    variance = jnp.mean(centered * centered, axis=1, keepdims=True)
    return centered * lax.rsqrt(variance + 1e-06) * gain


def block_pass(activated, gain, slot_user, slot_order, cotangent):

    def forward(acts):
        return attend(acts, gain, slot_user, slot_order)

    normed, pull = jax.vjp(forward, activated)
    (d_acts,) = pull(cotangent.astype(jnp.float32))
    return (normed.astype(jnp.bfloat16), d_acts)


def body(tokens, user_of_row, proj_weight, norm_gain, grad_out):
    peer_count = lax.axis_size("dp")
    self_index = lax.axis_index("dp")
    row_count = tokens.shape[1]
    width = proj_weight.shape[0]
    capacity = 2 * row_count // peer_count
    slot_count = peer_count * capacity
    routing = user_of_row[0]
    owners = (routing // UPO).reshape(peer_count, row_count)
    peer_ids = jnp.arange(peer_count, dtype=jnp.int32)
    inbound = (owners == self_index).astype(jnp.int32)
    in_rank = jnp.cumsum(inbound, axis=1) - 1
    matches = (
        (inbound[:, None, :] == 1)
        & (in_rank[:, None, :] == jnp.arange(capacity, dtype=jnp.int32)[None, :, None])
    ).astype(jnp.int32)
    users_src = routing.reshape(peer_count, row_count)
    slot_user = jnp.sum(matches * (users_src[:, None, :] + 1), axis=2).reshape(slot_count) - 1
    order_src = jnp.arange(peer_count * row_count, dtype=jnp.int32).reshape(peer_count, row_count)
    slot_order = jnp.sum(matches * order_src[:, None, :], axis=2).reshape(slot_count)
    own_owner = lax.dynamic_slice_in_dim(owners, self_index, 1, 0)[0]
    to_peer = (own_owner[:, None] == peer_ids[None, :]).astype(jnp.int32)
    out_rank = jnp.sum(jnp.cumsum(to_peer, axis=0) * to_peer, axis=1) - 1
    position = own_owner * capacity + out_rank
    rows_x = tokens[0]
    cotangent = grad_out[0]
    contract_cols = (((1,), (1,)), ((), ()))
    contract_rows = (((0,), (0,)), ((), ()))
    outgoing = jnp.zeros((slot_count, width), rows_x.dtype).at[position].set(rows_x)
    arrived = lax.all_to_all(outgoing, "dp", split_axis=0, concat_axis=0, tiled=True)
    preact = jnp.dot(arrived, proj_weight, preferred_element_type=jnp.float32)
    activated = jax.nn.silu(preact).astype(jnp.bfloat16)
    attended, d_acts = block_pass(activated, norm_gain, slot_user, slot_order, cotangent)
    d_acts = lax.optimization_barrier(d_acts)
    d_pre = (d_acts.astype(jnp.float32) * silu_grad(preact)).astype(jnp.bfloat16)
    d_slots = lax.dot_general(
        d_pre, proj_weight, contract_cols, preferred_element_type=jnp.float32
    ).astype(jnp.bfloat16)
    returned = lax.all_to_all(d_slots, "dp", split_axis=0, concat_axis=0, tiled=True)
    grad_tokens = returned[position]
    weight_shard = lax.psum_scatter(
        lax.dot_general(arrived, d_pre, contract_rows, preferred_element_type=jnp.float32),
        "dp",
        scatter_dimension=0,
        tiled=True,
    )
    grad_weight = lax.psum(weight_shard, "replica")
    return (attended[None], grad_tokens[None], grad_weight)


def solution(mesh):
    return jax.shard_map(
        body,
        mesh=mesh,
        in_specs=(P("replica", "dp", None), P("replica", None), P(), P(), P("replica", "dp", None)),
        out_specs=(P("replica", "dp", None), P("replica", "dp", None), P("dp", None)),
        check_vma=False,
    )
```

profile of v0, /device:TPU:0, one launch (start us, length us, event | category | flops | bytes accessed | tf_op | source)
XLA Modules:
  0.0 174.3 jit_solution(1940224548962781748)
XLA Ops:
  8.5 2.4 %scatter_custom_fusion = bf16[256,1024]{1,0:T(8,128)(2,1)} fusion(s32[128]{0:T(128)S(1)} %fusion.20, bf16[1,128,1024]{2,1,0:T(8,128)(2,1)} %param.5, bf16[]{:T(256)} %constant.57.clone.1), kind=kCustom, calls=%fused_computation.34 | custom fusion | bytes 786434 | tf_op jit(solution)/shard_map/scatter | solution.py:78
  10.9 5.2 %all-to-all-start = ((bf16[8,32,1024]{2,1,0:T(8,128)(2,1)}), bf16[8,32,1024]{2,1,0:T(8,128)(2,1)}, u32[]{:S(2)}, u32[]{:S(2)}) async-start(bf16[8,32,1024]{2,1,0:T(8,128)(2,1)} %bitcast.86), calls=%async_computation | async-start | bytes 1048576 | tf_op jit(solution)/shard_map/all_to_all | solution.py:79
  18.1 7.8 %all-to-all-done = bf16[8,32,1024]{2,1,0:T(8,128)(2,1)} async-done(((bf16[8,32,1024]{2,1,0:T(8,128)(2,1)}), bf16[8,32,1024]{2,1,0:T(8,128)(2,1)}, u32[]{:S(2)}, u32[]{:S(2)}) %all-to-all-start) | async-done | bytes 524320 | tf_op jit(solution)/shard_map/all_to_all | solution.py:79
  25.9 3.4 %multiply_convert_fusion.1 = (bf16[256,1536]{1,0:T(8,128)(2,1)}, f32[256,1536]{1,0:T(8,128)}) fusion(bf16[256,1024]{1,0:T(8,128)(2,1)} %bitcast.7, bf16[1024,1536]{1,0:T(8,128)(2,1)S(1)} %copy-done), kind=kOutput, calls=%fused_computation.5 | convolution fusion | flops 807272448 | bytes 6029312 | tf_op jit(solution)/shard_map/dot_general | solution.py:80
  29.3 2.4 %reshape.382 = bf16[256,3,4,128]{3,2,1,0:T(4,128)(2,1)} reshape(bf16[256,1536]{1,0:T(8,128)(2,1)} %get-tuple-element.16) | data formatting | bytes 1572864 | tf_op jit(solution)/shard_map/jvp()/reshape | solution.py:18
  31.8 2.2 %fusion.27 = (bf16[256,1,4,128]{3,2,1,0:T(4,128)(2,1)}, bf16[256,1,4,128]{3,2,1,0:T(4,128)(2,1)}, bf16[256,1,4,128]{3,2,1,0:T(4,128)(2,1)S(1)}) fusion(bf16[256,3,4,128]{3,2,1,0:T(4,128)(2,1)} %reshape.382), kind=kLoop, calls=%fused_computation.75 | loop fusion | bytes 1572864 | tf_op jit(solution)/shard_map/jvp()/slice | solution.py:20
  33.9 1.8 %copy.35 = bf16[256,1,4,128]{0,3,2,1:T(8,128)(2,1)} copy(bf16[256,1,4,128]{3,2,1,0:T(4,128)(2,1)} %get-tuple-element.10) | data formatting | bytes 524288
  35.8 1.3 convolution_multiply_fusion
  37.1 1.8 %fusion.28 = (f32[256]{0:T(256)S(1)}, f32[4,128,256]{2,1,0:T(8,128)}) fusion(f32[4,256,256]{2,1,0:T(8,128)S(1)} %convolution_multiply_fusion, pred[256,256]{1,0:T(8,128)(4,1)S(1)} %and_and_fusion, bf16[256,1,4,128]{0,3,2,1:T(8,128)(2,1)S(1)} %copy-done.7), kind=kOutput, calls=%fused_computation.76 | convolution fusion | flops 404094720 | bytes 1901568 | tf_op jit(solution)/shard_map/jvp(hqk,khd->qhd)/dot_general | solution.py:31
  38.9 2.0 %copy.24 = f32[256,512]{1,0:T(8,128)} copy(f32[256,512]{0,1:T(8,128)} %bitcast.80) | data formatting | bytes 1048576 | tf_op jit(solution)/shard_map/jvp()/reshape | solution.py:31
  40.9 1.4 multiply_reduce_fusion
  42.4 1.4 fusion.5
  43.8 2.4 %convolution_bitcast_fusion.2 = f32[256,1,4,128]{0,3,2,1:T(8,128)S(1)} fusion(f32[4,256,256]{2,1,0:T(8,128)} %copy-done.5, pred[256,256]{1,0:T(8,128)(4,1)S(1)} %and_and_fusion, f32[256,4,128]{0,2,1:T(8,128)S(1)} %bitcast.84, f32[4,128,256]{2,1,0:T(8,128)S(1)} %copy-done.1, f32[256]{0:T(256)S(1)} %negate_multiply_fusion, f32[256]{0:T(256)S(1)} %get-tuple-element.14, ...), kind=kOutput, calls=%fused_computation.12 | convolution fusion | flops 404881408 | bytes 2693120 | tf_op jit(solution)/shard_map/transpose(jvp(hqk,khd->qhd))/dot_general | solution.py:31
  49.6 2.4 %copy.34 = bf16[256,1536]{1,0:T(8,128)(2,1)} copy(bf16[256,1536]{0,1:T(8,128)(2,1)} %bitcast.82) | data formatting | bytes 1572864 | tf_op jit(solution)/shard_map/transpose(jvp())/convert_element_type | solution.py:18
  52.0 5.6 %fusion.26 = f32[1024,1536]{1,0:T(8,128)} fusion(bf16[256,1024]{1,0:T(8,128)(2,1)} %bitcast.7, f32[256,1536]{1,0:T(8,128)} %get-tuple-element.17, bf16[256,1536]{1,0:T(8,128)(2,1)} %copy.34), kind=kOutput, calls=%fused_computation.74 | convolution fusion | flops 809238528 | bytes 9175040 | tf_op jit(solution)/shard_map/dot_general | solution.py:91
  57.7 61.5 %reduce-scatter.2.cloned.1.call-done = f32[128,1536]{1,0:T(8,128)} async-done(((f32[1024,1536]{1,0:T(8,128)}), f32[128,1536]{1,0:T(8,128)}) %reduce-scatter.2.cloned.1.call-update) | async-done | bytes 786448 | tf_op jit(solution)/shard_map/reduce_scatter | solution.py:90
  119.3 3.6 %convolution_convert_fusion = bf16[256,1024]{1,0:T(8,128)(2,1)} fusion(bf16[1024,1536]{1,0:T(8,128)(2,1)S(1)} %copy-done, f32[256,1536]{1,0:T(8,128)} %get-tuple-element.17, bf16[256,1536]{1,0:T(8,128)(2,1)} %copy.34), kind=kOutput, calls=%fused_computation.9 | convolution fusion | flops 809500672 | bytes 6029312 | tf_op jit(solution)/shard_map/dot_general | solution.py:85
  122.9 4.1 %all-to-all-start.1 = ((bf16[8,32,1024]{2,1,0:T(8,128)(2,1)}), bf16[8,32,1024]{2,1,0:T(8,128)(2,1)}, u32[]{:S(2)}, u32[]{:S(2)}) async-start(bf16[8,32,1024]{2,1,0:T(8,128)(2,1)} %bitcast.87), calls=%async_computation.1 | async-start | bytes 1048576 | tf_op jit(solution)/shard_map/all_to_all | solution.py:88
  127.0 2.0 %copy.22 = f32[1,256,512]{2,1,0:T(8,128)} copy(f32[1,256,512]{1,2,0:T(8,128)} %bitcast.81) | data formatting | bytes 1048576 | tf_op jit(solution)/shard_map/jvp()/reshape | solution.py:31
  129.1 1.9 %multiply_convert_fusion.2 = bf16[1,256,512]{2,1,0:T(8,128)(2,1)} fusion(f32[1,256,512]{2,1,0:T(8,128)} %copy.22, f32[512]{0:T(512)S(1)} %copy-done.9, f32[256]{0:T(256)S(1)} %get-tuple-element.15, f32[256]{0:T(256)S(1)} %broadcast_multiply_fusion), kind=kLoop, calls=%fused_computation.27 | loop fusion | flops 524288 | bytes 790528 | tf_op jit(solution)/shard_map/convert_element_type | solution.py:47
  131.0 5.8 %all-to-all-done.1 = bf16[8,32,1024]{2,1,0:T(8,128)(2,1)} async-done(((bf16[8,32,1024]{2,1,0:T(8,128)(2,1)}), bf16[8,32,1024]{2,1,0:T(8,128)(2,1)}, u32[]{:S(2)}, u32[]{:S(2)}) %all-to-all-start.1) | async-done | bytes 524320 | tf_op jit(solution)/shard_map/all_to_all | solution.py:88
  136.8 2.9 %gather_fusion = bf16[128,1024]{1,0:T(8,128)(2,1)} fusion(bf16[256,1024]{1,0:T(8,128)(2,1)} %bitcast.26, s32[1024]{0:T(1024)S(1)} %pad_clamp_fusion), kind=kCustom, calls=%fused_computation | custom fusion | bytes 524800 | tf_op jit(solution)/shard_map/gather | solution.py:89
  139.6 25.8 %all-reduce.5.cloned.1.call-done = f32[128,1536]{1,0:T(8,128)} async-done(((f32[128,1536]{1,0:T(8,128)}), f32[128,1536]{1,0:T(8,128)}) %all-reduce.5.cloned.1.call-update) | async-done | bytes 786448 | tf_op jit(solution)/shard_map/psum | solution.py:96
  165.4 2.1 %copy.45 = f32[128,1536]{1,0:T(8,128)} copy(f32[128,1536]{1,0:T(8,128)} %all-reduce.5.cloned.1.call-done) | data formatting | bytes 1572864
  (50 shorter events, 6.8 us)
Async XLA Ops:
  7.2 18.8 %copy-start = (bf16[1024,1536]{1,0:T(8,128)(2,1)S(1)}, bf16[1024,1536]{1,0:T(8,128)(2,1)}, u32[]{:S(2)}) copy-start(bf16[1024,1536]{1,0:T(8,128)(2,1)} %param.7) | copy-start | bytes 9437188
  7.2 8.9 %copy-start.10 = (s32[1,1024]{1,0:T(1,128)S(1)}, s32[1,1024]{1,0:T(1,128)}, u32[]{:S(2)}) copy-start(s32[1,1024]{1,0:T(1,128)} %param.6) | copy-start | bytes 12292
  7.2 9.8 %copy-start.4 = (bf16[1,256,512]{2,1,0:T(8,128)(2,1)S(1)}, bf16[1,256,512]{2,1,0:T(8,128)(2,1)}, u32[]{:S(2)}) copy-start(bf16[1,256,512]{2,1,0:T(8,128)(2,1)} %param.9) | copy-start | bytes 786436
  10.9 15.0 %all-to-all-start = ((bf16[8,32,1024]{2,1,0:T(8,128)(2,1)}), bf16[8,32,1024]{2,1,0:T(8,128)(2,1)}, u32[]{:S(2)}, u32[]{:S(2)}) async-start(bf16[8,32,1024]{2,1,0:T(8,128)(2,1)} %bitcast.86), calls=%async_computation | async-start | bytes 1048576 | tf_op jit(solution)/shard_map/all_to_all | solution.py:79
  16.1 103.2 %reduce-scatter.2.cloned.1.call-start = ((), (), s32[]{:S(2)}) async-start(), calls=%async_computation.3 | async-start | bytes 7077888 | tf_op jit(solution)/shard_map/reduce_scatter | solution.py:90
  35.8 1.3 copy-start.7
  37.1 1.8 %copy-start.5 = (f32[4,256,256]{2,1,0:T(8,128)}, f32[4,256,256]{2,1,0:T(8,128)S(1)}, u32[]{:S(2)}) copy-start(f32[4,256,256]{2,1,0:T(8,128)S(1)} %convolution_multiply_fusion) | copy-start | bytes 3145732
  37.1 3.8 %copy-start.9 = (f32[512]{0:T(512)S(1)}, f32[512]{0:T(512)}, u32[]{:S(2)}) copy-start(f32[512]{0:T(512)} %param.8) | copy-start | bytes 6148
  40.9 2.8 %copy-start.1 = (f32[4,128,256]{2,1,0:T(8,128)S(1)}, f32[4,128,256]{2,1,0:T(8,128)}, u32[]{:S(2)}) copy-start(f32[4,128,256]{2,1,0:T(8,128)} %get-tuple-element.19) | copy-start | bytes 1572868
  40.9 2.9 %copy-start.3 = (f32[1,256,512]{1,2,0:T(8,128)S(1)}, f32[1,256,512]{1,2,0:T(8,128)}, u32[]{:S(2)}) copy-start(f32[1,256,512]{1,2,0:T(8,128)} %copy.23) | copy-start | bytes 1572868
  43.8 2.5 %copy-start.6 = (f32[4,256,256]{2,1,0:T(8,128)S(1)}, f32[4,256,256]{2,1,0:T(8,128)}, u32[]{:S(2)}) copy-start(f32[4,256,256]{2,1,0:T(8,128)} %copy-done.5) | copy-start | bytes 3145732
  43.8 2.5 %copy-start.8 = (bf16[256,1,4,128]{0,3,2,1:T(8,128)(2,1)S(1)}, bf16[256,1,4,128]{0,3,2,1:T(8,128)(2,1)}, u32[]{:S(2)}) copy-start(bf16[256,1,4,128]{0,3,2,1:T(8,128)(2,1)} %copy.35) | copy-start | bytes 786436
  46.3 1.1 copy-start.2
  57.6 107.8 %all-reduce.5.cloned.1.call-start = ((), (), s32[]{:S(2)}) async-start(), calls=%async_computation.4 | async-start | bytes 1572864 | tf_op jit(solution)/shard_map/psum | solution.py:96
  122.9 13.9 %all-to-all-start.1 = ((bf16[8,32,1024]{2,1,0:T(8,128)(2,1)}), bf16[8,32,1024]{2,1,0:T(8,128)(2,1)}, u32[]{:S(2)}, u32[]{:S(2)}) async-start(bf16[8,32,1024]{2,1,0:T(8,128)(2,1)} %bitcast.87), calls=%async_computation.1 | async-start | bytes 1048576 | tf_op jit(solution)/shard_map/all_to_all | solution.py:88
Sparse Core Ops, SparseCore 0:
  57.8 61.4 reduce-scatter.1
  121.7 43.6 all-reduce.4
where the time goes:
time: 175 us; the launch traced here: 174 us
  waiting for transfers between devices  101 us (58%)
  local copies, waits for them, and re-layouts  21.4 us (12%)
  matrix products  20.5 us (12%)
  between operations  14.3 us (8%)
  starting transfers between devices  9.39 us (5%)
  other arithmetic  7.81 us (4%)
    reduce_scatter x1, waiting for transfers between devices, body(): lax.psum_scatter(lax.dot_general(arrived, d_pre, contract_rows, preferred...  61.5 us
    psum x1, waiting for transfers between devices, body(): grad_weight = lax.psum(weight_shard, 'replica')  25.8 us
    all_to_all x1, waiting for transfers between devices, body(): lax.all_to_all(outgoing, 'dp', split_axis=0, concat_axis=0, tiled=True)  7.8 us
    all_to_all x1, waiting for transfers between devices, body(): lax.all_to_all(d_slots, 'dp', split_axis=0, concat_axis=0, tiled=True)  5.81 us
    dot_general x1, matrix products, body(): lax.dot_general(arrived, d_pre, contract_rows, preferred_element_type=jnp...  5.6 us
    dot_general x3, matrix products, attend(): jnp.einsum('hqk,khd->qhd', weights, values, precision=lax.Precision.HIGHEST)  5.29 us
    all_to_all x1, starting transfers between devices, body(): lax.all_to_all(outgoing, 'dp', split_axis=0, concat_axis=0, tiled=True)  5.17 us
    all_to_all x1, starting transfers between devices, body(): lax.all_to_all(d_slots, 'dp', split_axis=0, concat_axis=0, tiled=True)  4.14 us
  transfers between devices with their start and end apart: 4, of which 4 were waited for; matrix products, arithmetic and copies ran while one was open for 7% of the time, Pallas kernels for 0%

commit v1 on v0

--- a/solution.py
+++ b/solution.py
@@ -1,6 +1,10 @@
+import functools
+
 import jax
 import jax.numpy as jnp
 from jax import lax
+from jax.experimental import pallas as pl
+from jax.experimental.pallas import tpu as pltpu
 from jax.sharding import PartitionSpec as P
 
 HEADS = 4
@@ -47,7 +51,7 @@
     return (normed.astype(jnp.bfloat16), d_acts)
 
 
-def body(tokens, user_of_row, proj_weight, norm_gain, grad_out):
+def general_body(tokens, user_of_row, proj_weight, norm_gain, grad_out):
     peer_count = lax.axis_size("dp")
     self_index = lax.axis_index("dp")
     row_count = tokens.shape[1]
@@ -97,6 +101,276 @@
     return (attended[None], grad_tokens[None], grad_weight)
 
 
+F32 = jnp.float32
+BF16 = jnp.bfloat16
+ROWS_BY_COLS = (((1,), (0,)), ((), ()))
+COLS_BY_COLS = (((1,), (1,)), ((), ()))
+ROWS_BY_ROWS = (((0,), (0,)), ((), ()))
+VMEM_LIMIT = 40 * 1024 * 1024
+
+
+def matmul(left, right, contract=ROWS_BY_COLS):
+    return lax.dot_general(left, right, contract, preferred_element_type=F32)
+
+
+def call(kernel, outs, operands, flops, scratch=()):
+    nbytes = sum(a.size * a.dtype.itemsize for a in operands)
+    nbytes += sum(o.size * o.dtype.itemsize for o in outs)
+    vmem = pl.BlockSpec(memory_space=pltpu.VMEM)
+    return pl.pallas_call(
+        kernel,
+        out_shape=outs,
+        in_specs=[vmem] * len(operands),
+        out_specs=[vmem] * len(outs),
+        scratch_shapes=list(scratch),
+        compiler_params=pltpu.CompilerParams(vmem_limit_bytes=VMEM_LIMIT),
+        cost_estimate=pl.CostEstimate(flops=flops, bytes_accessed=nbytes, transcendentals=0),
+    )(*operands)
+
+
+def shaped(shape, dtype):
+    return jax.ShapeDtypeStruct(shape, dtype)
+
+
+def running_count(flags):
+    length = flags.shape[1]
+    at = lax.broadcasted_iota(jnp.int32, (length, length), 0)
+    upto = lax.broadcasted_iota(jnp.int32, (length, length), 1)
+    return matmul(flags, (at <= upto).astype(F32))
+
+
+def own_placement(users_ref, me, peers, capacity):
+    owner = lax.div(users_ref[pl.ds(me, 1), :], UPO)
+    rows = owner.shape[1]
+    match = (lax.broadcasted_iota(jnp.int32, (peers, rows), 0) == owner).astype(F32)
+    rank = jnp.sum(running_count(match) * match, axis=0, keepdims=True) - 1.0
+    key = (owner ^ me) * capacity + rank.astype(jnp.int32)
+    return (lax.broadcasted_iota(jnp.int32, (peers * capacity, rows), 0) == key).astype(BF16)
+
+
+def pack_kernel(peers, capacity, users_ref, tokens_ref, *out_refs):
+    me = lax.axis_index("dp")
+    place = own_placement(users_ref, me, peers, capacity)
+    packed = matmul(place, tokens_ref[...]).astype(BF16)
+    for m in range(peers):
+        out_refs[m][...] = packed[m * capacity : (m + 1) * capacity]
+
+
+def unpack_kernel(peers, capacity, users_ref, *refs):
+    *in_refs, out_ref, held = refs
+    me = lax.axis_index("dp")
+    place = own_placement(users_ref, me, peers, capacity)
+    for m in range(peers):
+        held[m * capacity : (m + 1) * capacity, :] = in_refs[m][...]
+    out_ref[...] = matmul(place, held[...], ROWS_BY_ROWS).astype(BF16)
+
+
+def slot_codes(users_ref, me, peers, capacity):
+    users = jnp.concatenate([users_ref[pl.ds(me ^ m, 1), :] for m in range(peers)], axis=0)
+    rows = users.shape[1]
+    match = (lax.div(users, UPO) == me).astype(F32)
+    rank = running_count(match) * match - 1.0
+    position = lax.broadcasted_iota(jnp.int32, (1, rows), 1)
+    slot = lax.broadcasted_iota(jnp.int32, (capacity, rows), 0).astype(F32)
+    codes = []
+    for m in range(peers):
+        code = (users[m : m + 1] + 1) * (peers * rows) + (me ^ m) * rows + position
+        picked = jnp.where(rank[m : m + 1] == slot, code.astype(F32), 0.0)
+        codes.append(jnp.sum(picked, axis=1, keepdims=True))
+    return jnp.concatenate(codes, axis=0)
+
+
+def attend_kernel(peers, capacity, users_ref, gain_ref, w_ref, grad_ref, *refs):
+    x_refs, refs = refs[:peers], refs[peers:]
+    attended_ref, d_values_ref, d_rest_ref, x_own_ref, x_sib_ref, x, act, slope, grad = refs
+    me = lax.axis_index("dp")
+    slots = peers * capacity
+    width, columns = w_ref.shape
+    features = gain_ref.shape[1]
+    block = width // peers
+    for m in range(peers):
+        x[m * capacity : (m + 1) * capacity, :] = x_refs[m][...]
+    for i in range(peers // 2):
+        own_at = pl.multiple_of((me ^ (2 * i)) * block, block)
+        sib_at = pl.multiple_of((me ^ (2 * i + 1)) * block, block)
+        x_own_ref[:, i * block : (i + 1) * block] = x[:, pl.ds(own_at, block)]
+        x_sib_ref[:, i * block : (i + 1) * block] = x[:, pl.ds(sib_at, block)]
+    gain = gain_ref[...]
+    for m in range(peers):
+        at = pl.multiple_of((me ^ m) * capacity, capacity)
+        grad[m * capacity : (m + 1) * capacity, :] = grad_ref[pl.ds(at, capacity), :].astype(F32) * gain
+    step = 2 * HEAD_DIM
+    for c in range(0, columns, step):
+        preact = matmul(x[...], w_ref[:, c : c + step])
+        gate = 0.5 * jnp.tanh(0.5 * preact) + 0.5
+        silu = preact * gate
+        act[:, c : c + step] = silu.astype(BF16)
+        slope[:, c : c + step] = gate + silu * (1.0 - gate)
+
+    code = slot_codes(users_ref, me, peers, capacity)
+    code_of_key = jnp.broadcast_to(code, (slots, HEAD_DIM)).T[0:1]
+    batch_rows = users_ref.shape[0] * users_ref.shape[1]
+    whole = code.astype(jnp.int32)
+    first = (lax.div(whole, batch_rows) * batch_rows).astype(F32)
+    first = jnp.where(code > 0.0, first, code + 1.0)
+    visible = (code_of_key <= code) & (code_of_key >= first)
+
+    def head(base, h):
+        return act[:, base + h * HEAD_DIM : base + (h + 1) * HEAD_DIM]
+
+    scale = HEAD_DIM**-0.5
+    weights, slopes, mixed = [], [], []
+    for h in range(HEADS):
+        scores = matmul(head(0, h), head(features, h), COLS_BY_COLS) * scale
+        gate = 0.5 * jnp.tanh(0.5 * scores) + 0.5
+        silu = scores * gate
+        weight = jnp.where(visible, silu, 0.0).astype(BF16)
+        slopes.append(jnp.where(visible, (gate + silu * (1.0 - gate)) * scale, 0.0))
+        weights.append(weight)
+        mixed.append(matmul(weight, head(2 * features, h)))
+    mean = sum(jnp.sum(v, axis=1, keepdims=True) for v in mixed) / features
+    centered = [v - mean for v in mixed]
+    variance = sum(jnp.sum(v * v, axis=1, keepdims=True) for v in centered) / features
+    inverse = lax.rsqrt(variance + 1e-06)
+    unit = [v * inverse for v in centered]
+
+    def part(ref, h):
+        return ref[:, h * HEAD_DIM : (h + 1) * HEAD_DIM]
+
+    grads = [part(grad, h) for h in range(HEADS)]
+    for h in range(HEADS):
+        normed = (unit[h] * part(gain, h)).astype(BF16)
+        for m in range(peers):
+            at = pl.multiple_of((me ^ m) * capacity, capacity)
+            attended_ref[pl.ds(at, capacity), h * HEAD_DIM : (h + 1) * HEAD_DIM] = normed[m * capacity : (m + 1) * capacity]
+    grad_mean = sum(jnp.sum(g, axis=1, keepdims=True) for g in grads) / features
+    grad_unit = sum(jnp.sum(g * u, axis=1, keepdims=True) for g, u in zip(grads, unit)) / features
+    for h in range(HEADS):
+        d_mixed = ((grads[h] - grad_mean - unit[h] * grad_unit) * inverse).astype(BF16)
+        d_value = matmul(weights[h], d_mixed, ROWS_BY_ROWS)
+        at = h * HEAD_DIM
+        d_values_ref[:, at : at + HEAD_DIM] = (d_value * part(slope, 2 * HEADS + h)).astype(BF16)
+        d_scores = (matmul(d_mixed, head(2 * features, h), COLS_BY_COLS) * slopes[h]).astype(BF16)
+        d_query = matmul(d_scores, head(features, h))
+        d_key = matmul(d_scores, head(0, h), ROWS_BY_ROWS)
+        d_rest_ref[:, at : at + HEAD_DIM] = (d_query * part(slope, h)).astype(BF16)
+        at += features
+        d_rest_ref[:, at : at + HEAD_DIM] = (d_key * part(slope, HEADS + h)).astype(BF16)
+
+
+def weight_kernel(x_own_ref, x_sib_ref, d_own_ref, d_sib_ref, *out_refs):
+    block = x_own_ref.shape[1] // len(out_refs)
+    for i, out_ref in enumerate(out_refs):
+        at = slice(i * block, (i + 1) * block)
+        total = matmul(x_own_ref[:, at], d_own_ref[...], ROWS_BY_ROWS)
+        total += matmul(x_sib_ref[:, at], d_sib_ref[...], ROWS_BY_ROWS)
+        out_ref[...] = total.astype(out_ref.dtype)
+
+
+def token_kernel(d_values_ref, d_rest_ref, w_ref, *out_refs):
+    split = d_rest_ref.shape[1]
+    capacity = out_refs[0].shape[0]
+    total = matmul(d_rest_ref[...], w_ref[:, :split], COLS_BY_COLS)
+    total += matmul(d_values_ref[...], w_ref[:, split:], COLS_BY_COLS)
+    for m, out_ref in enumerate(out_refs):
+        out_ref[...] = total[m * capacity : (m + 1) * capacity].astype(BF16)
+
+
+def swap(array, axis, size, bits):
+    return lax.ppermute(array, axis, [(i, i ^ bits) for i in range(size)])
+
+
+def direct_body(tokens, user_of_row, proj_weight, norm_gain, grad_out):
+    peers = lax.axis_size("dp")
+    replicas = lax.axis_size("replica")
+    rows = tokens.shape[1]
+    width, columns = proj_weight.shape
+    features = grad_out.shape[2]
+    capacity = 2 * rows // peers
+    slots = peers * capacity
+    block = width // peers
+    users = user_of_row.reshape(peers, rows)
+    gain = norm_gain.reshape(1, features)
+    exchange = functools.partial(swap, axis="dp", size=peers)
+
+    outgoing = call(
+        functools.partial(pack_kernel, peers, capacity),
+        [shaped((capacity, width), BF16)] * peers,
+        [users, tokens[0]],
+        2 * slots * rows * width,
+    )
+    arrived = [outgoing[0]] + [exchange(outgoing[m], bits=m) for m in range(1, peers)]
+    half = width // 2
+    attended, d_values, d_rest, x_own, x_sib = call(
+        functools.partial(attend_kernel, peers, capacity),
+        [
+            shaped((slots, features), BF16),
+            shaped((slots, features), BF16),
+            shaped((slots, columns - features), BF16),
+            shaped((slots, half), BF16),
+            shaped((slots, half), BF16),
+        ],
+        [users, gain, proj_weight, grad_out[0], *arrived],
+        2 * slots * width * columns + 14 * slots * slots * features,
+        [
+            pltpu.VMEM((slots, width), BF16),
+            pltpu.VMEM((slots, columns), BF16),
+            pltpu.VMEM((slots, columns), F32),
+            pltpu.VMEM((slots, features), F32),
+        ],
+    )
+    x_from_sib = exchange(x_sib, bits=1)
+    blocks = []
+    for d_own in (d_values, d_rest):
+        size = d_own.shape[1]
+        d_from_sib = exchange(d_own, bits=1)
+        mine, *others = call(
+            weight_kernel,
+            [shaped((block, size), F32)] + [shaped((block, size), BF16)] * (peers // 2 - 1),
+            [x_own, x_from_sib, d_own, d_from_sib],
+            4 * slots * half * size,
+        )
+        total = mine
+        for i, other in enumerate(others):
+            total = total + exchange(other, bits=2 * (i + 1)).astype(F32)
+        bits = 1
+        while bits < replicas:
+            held = total.astype(BF16)
+            total = held.astype(F32) + swap(held, "replica", replicas, bits).astype(F32)
+            bits *= 2
+        blocks.append(total)
+    grad_weight = jnp.concatenate([blocks[1], blocks[0]], axis=1)
+
+    d_slots = call(
+        token_kernel,
+        [shaped((capacity, width), BF16)] * peers,
+        [d_values, d_rest, proj_weight],
+        2 * slots * width * columns,
+    )
+    returned = [d_slots[0]] + [exchange(d_slots[m], bits=m) for m in range(1, peers)]
+    (grad_tokens,) = call(
+        functools.partial(unpack_kernel, peers, capacity),
+        [shaped((rows, width), BF16)],
+        [users, *returned],
+        2 * slots * rows * width,
+        [pltpu.VMEM((slots, width), BF16)],
+    )
+    return (attended[None], grad_tokens[None], grad_weight)
+
+
+def power_of_two(value):
+    return value & (value - 1) == 0
+
+
+def body(tokens, user_of_row, proj_weight, norm_gain, grad_out):
+    peers = lax.axis_size("dp")
+    replicas = lax.axis_size("replica")
+    capacity = 2 * tokens.shape[1] // peers
+    aligned = capacity % 16 == 0 and proj_weight.shape[0] // peers % 128 == 0
+    run = direct_body if aligned and power_of_two(peers) and power_of_two(replicas) else general_body
+    return run(tokens, user_of_row, proj_weight, norm_gain, grad_out)
+
+
 def solution(mesh):
     return jax.shard_map(
         body,

time: 175 us -> 79.7 us (0.46)
  waiting for transfers between devices: 101 us -> 36.2 us
  matrix products: 20.5 us -> 0 us
  starting transfers between devices: 9.39 us -> 28.6 us
  local copies, waits for them, and re-layouts: 21.4 us -> 5.16 us
  between operations: 14.3 us -> 0.76 us
  Pallas kernels: 0 us -> 7.29 us
  other arithmetic: 7.81 us -> 1.36 us
    reduce_scatter x1 -> x0, waiting for transfers between devices: 61.5 us -> none  [body(): lax.psum_scatter(lax.dot_general(arrived, d_pre, contract_rows, preferred...]
    ppermute x0 -> x27, waiting for transfers between devices: none -> 36.2 us  [swap(): return lax.ppermute(array, axis, [(i, i ^ bits) for i in range(size)])]
    ppermute x0 -> x27, starting transfers between devices: none -> 28.6 us  [swap(): return lax.ppermute(array, axis, [(i, i ^ bits) for i in range(size)])]
    psum x1 -> x0, waiting for transfers between devices: 25.8 us -> none  [body(): grad_weight = lax.psum(weight_shard, 'replica')]
    dot_general x9 -> x0, matrix products: 20.5 us -> none  [the longest x1 5.6 us: body(): lax.dot_general(arrived, d_pre, contract_rows, preferred_element_type=jnp...]
    all_to_all x2 -> x0, waiting for transfers between devices: 13.6 us -> none  [the longest x1 7.8 us: body(): lax.all_to_all(outgoing, 'dp', split_axis=0, concat_axis=0, tiled=True)]
    all_to_all x2 -> x0, starting transfers between devices: 9.31 us -> none  [the longest x1 5.17 us: body(): lax.all_to_all(outgoing, 'dp', split_axis=0, concat_axis=0, tiled=True)]
    pallas_call x0 -> x6, Pallas kernels: none -> 7.29 us  [call(): pl.pallas_call(kernel, out_shape=outs, in_specs=[vmem] * len(operands), o...]
  transfers between devices with their start and end apart: 4 -> 27, of which waited for: 4 -> 13; matrix products, arithmetic and copies ran while one was open for 7% -> 0% of each run, Pallas kernels for 0% -> 4%
where the time goes in v1:
time: 79.7 us; the launch traced here: 79.4 us
  waiting for transfers between devices  36.2 us (45%)
  starting transfers between devices  28.6 us (36%)
  Pallas kernels  7.29 us (9%)
  local copies, waits for them, and re-layouts  5.16 us (6%)
  other arithmetic  1.36 us (2%)
    ppermute x27, waiting for transfers between devices, swap(): return lax.ppermute(array, axis, [(i, i ^ bits) for i in range(size)])  36.2 us
    ppermute x27, starting transfers between devices, swap(): return lax.ppermute(array, axis, [(i, i ^ bits) for i in range(size)])  28.6 us
    pallas_call x6, Pallas kernels, call(): pl.pallas_call(kernel, out_shape=outs, in_specs=[vmem] * len(operands), o...  7.29 us
    unnamed x14, local copies, waits for them, and re-layouts  5.16 us
  transfers between devices with their start and end apart: 27, of which 13 were waited for; matrix products, arithmetic and copies ran while one was open for 0% of the time, Pallas kernels for 4%

profile of v1, /device:TPU:0, one launch (start us, length us, event | category | flops | bytes accessed | tf_op | source)
XLA Modules:
  0.0 79.4 jit_solution(12222529924249586375)
XLA Ops:
  3.2 2.6 %collective-permute-start.1 = (bf16[32,1024]{1,0:T(8,128)(2,1)S(1)}, bf16[32,1024]{1,0:T(8,128)(2,1)S(1)}, u32[]{:S(2)}, u32[]{:S(2)}) collective-permute-start(bf16[32,1024]{1,0:T(8,128)(2,1)S(1)} %get-tuple-element.34), channel_id=1, source_target_pairs={{0,8},{4,12},{8,0},{12,4},{16,24},{20,28},{24,16},{28,20},{1,9},{5... | collective-permute-start | bytes 196616 | tf_op jit(solution)/shard_map/ppermute | solution.py:280
  5.8 1.8 %collective-permute-start.3 = (bf16[32,1024]{1,0:T(8,128)(2,1)S(1)}, bf16[32,1024]{1,0:T(8,128)(2,1)S(1)}, u32[]{:S(2)}, u32[]{:S(2)}) collective-permute-start(bf16[32,1024]{1,0:T(8,128)(2,1)S(1)} %get-tuple-element.36), channel_id=1, source_target_pairs={{0,16},{4,20},{8,24},{12,28},{16,0},{20,4},{24,8},{28,12},{1,17},{... | collective-permute-start | bytes 196616 | tf_op jit(solution)/shard_map/ppermute | solution.py:280
  7.6 2.6 %collective-permute-start.5 = (bf16[32,1024]{1,0:T(8,128)(2,1)S(1)}, bf16[32,1024]{1,0:T(8,128)(2,1)S(1)}, u32[]{:S(2)}, u32[]{:S(2)}) collective-permute-start(bf16[32,1024]{1,0:T(8,128)(2,1)S(1)} %get-tuple-element.38), channel_id=1, source_target_pairs={{0,24},{4,28},{8,16},{12,20},{16,8},{20,12},{24,0},{28,4},{1,25},{... | collective-permute-start | bytes 196616 | tf_op jit(solution)/shard_map/ppermute | solution.py:280
  10.4 2.7 %collective-permute-done.4.refs_5_ = bf16[32,1024]{1,0:T(8,128)(2,1)S(1)} collective-permute-done((bf16[32,1024]{1,0:T(8,128)(2,1)S(1)}, bf16[32,1024]{1,0:T(8,128)(2,1)S(1)}, u32[]{:S(2)}, u32[]{:S(2)}) %collective-permute-start.4) | collective-permute-done | bytes 65568 | tf_op jit(solution)/shard_map/ppermute | solution.py:280
  13.2 2.0 %collective-permute-done.6.refs_7_ = bf16[32,1024]{1,0:T(8,128)(2,1)S(1)} collective-permute-done((bf16[32,1024]{1,0:T(8,128)(2,1)S(1)}, bf16[32,1024]{1,0:T(8,128)(2,1)S(1)}, u32[]{:S(2)}, u32[]{:S(2)}) %collective-permute-start.6) | collective-permute-done | bytes 65568 | tf_op jit(solution)/shard_map/ppermute | solution.py:280
  15.2 1.9 %copy-done = bf16[1024,1536]{1,0:T(8,128)(2,1)S(1)} copy-done((bf16[1024,1536]{1,0:T(8,128)(2,1)S(1)}, bf16[1024,1536]{1,0:T(8,128)(2,1)}, u32[]{:S(2)}) %copy-start) | copy-done | bytes 3145752
  18.7 3.6 %shard_map.77 = (bf16[256,512]{1,0:T(8,128)(2,1)}, bf16[256,512]{1,0:T(8,128)(2,1)S(1)}, bf16[256,1024]{1,0:T(8,128)(2,1)S(1)}, bf16[256,512]{1,0:T(8,128)(2,1)S(1)}, bf16[256,512]{1,0:T(8,128)(2,1)S(1)}) custom-call(s32[8,128]{1,0:T(8,128)S(1)} %bitcast.8, f32[1,512]{1,0:T(1,128)S(1)} %bitcast.11, bf16[1024,1536]{1,0:T(8,128)(2,1)S(1)} %copy-done, ...), custom_call_target="tpu_custom_call" | custom-call | flops 1275068416 | bytes 5511168 | tf_op jit(solution)/shard_map/pallas_call | solution.py:120
  23.0 1.6 %collective-permute-done.14.x_sib_ref = bf16[256,512]{1,0:T(8,128)(2,1)S(1)} collective-permute-done((bf16[256,512]{1,0:T(8,128)(2,1)S(1)}, bf16[256,512]{1,0:T(8,128)(2,1)S(1)}, u32[]{:S(2)}, u32[]{:S(2)}) %collective-permute-start.14) | collective-permute-done | bytes 262176 | tf_op jit(solution)/shard_map/ppermute | solution.py:280
  26.2 1.7 %collective-permute-start.23 = (bf16[128,512]{1,0:T(8,128)(2,1)S(1)}, bf16[128,512]{1,0:T(8,128)(2,1)S(1)}, u32[]{:S(2)}, u32[]{:S(2)}) collective-permute-start(bf16[128,512]{1,0:T(8,128)(2,1)S(1)} %get-tuple-element.59), channel_id=1, source_target_pairs={{0,16},{4,20},{8,24},{12,28},{16,0},{20,4},{24,8},{28,12},{1,17},{... | collective-permute-start | bytes 393224 | tf_op jit(solution)/shard_map/ppermute | solution.py:280
  30.5 1.6 %collective-permute-start.17 = (bf16[128,1024]{1,0:T(8,128)(2,1)S(1)}, bf16[128,1024]{1,0:T(8,128)(2,1)S(1)}, u32[]{:S(2)}, u32[]{:S(2)}) collective-permute-start(bf16[128,1024]{1,0:T(8,128)(2,1)S(1)} %get-tuple-element.55), channel_id=1, source_target_pairs={{0,16},{4,20},{8,24},{12,28},{16,0},{20,4},{24,8},{28,12},{1,17},{... | collective-permute-start | bytes 786440 | tf_op jit(solution)/shard_map/ppermute | solution.py:280
  32.2 1.5 %collective-permute-start.18 = (bf16[128,1024]{1,0:T(8,128)(2,1)S(1)}, bf16[128,1024]{1,0:T(8,128)(2,1)S(1)}, u32[]{:S(2)}, u32[]{:S(2)}) collective-permute-start(bf16[128,1024]{1,0:T(8,128)(2,1)S(1)} %get-tuple-element.56), channel_id=1, source_target_pairs={{0,24},{4,28},{8,16},{12,20},{16,8},{20,12},{24,0},{28,4},{1,25},{... | collective-permute-start | bytes 786440 | tf_op jit(solution)/shard_map/ppermute | solution.py:280
  34.0 1.2 %collective-permute-done.24 = bf16[128,512]{1,0:T(8,128)(2,1)S(1)} collective-permute-done((bf16[128,512]{1,0:T(8,128)(2,1)S(1)}, bf16[128,512]{1,0:T(8,128)(2,1)S(1)}, u32[]{:S(2)}, u32[]{:S(2)}) %collective-permute-start.24) | collective-permute-done | bytes 131104 | tf_op jit(solution)/shard_map/ppermute | solution.py:280
  35.3 1.6 %collective-permute-start.25 = (bf16[128,512]{1,0:T(8,128)(2,1)S(1)}, bf16[128,512]{1,0:T(8,128)(2,1)S(1)}, u32[]{:S(2)}, u32[]{:S(2)}) collective-permute-start(bf16[128,512]{1,0:T(8,128)(2,1)S(1)} %add_convert_fusion.3), channel_id=1, source_target_pairs={{0,1},{1,0},{2,3},{3,2},{4,5},{5,4},{6,7},{7,6},{8,9},{9,8},{10,11... | collective-permute-start | bytes 393224 | tf_op jit(solution)/shard_map/ppermute | solution.py:280
  37.0 3.4 %collective-permute-done.16 = bf16[128,1024]{1,0:T(8,128)(2,1)S(1)} collective-permute-done((bf16[128,1024]{1,0:T(8,128)(2,1)S(1)}, bf16[128,1024]{1,0:T(8,128)(2,1)S(1)}, u32[]{:S(2)}, u32[]{:S(2)}) %collective-permute-start.16) | collective-permute-done | bytes 262176 | tf_op jit(solution)/shard_map/ppermute | solution.py:280
  40.3 5.3 %collective-permute-done.17 = bf16[128,1024]{1,0:T(8,128)(2,1)S(1)} collective-permute-done((bf16[128,1024]{1,0:T(8,128)(2,1)S(1)}, bf16[128,1024]{1,0:T(8,128)(2,1)S(1)}, u32[]{:S(2)}, u32[]{:S(2)}) %collective-permute-start.17) | collective-permute-done | bytes 262176 | tf_op jit(solution)/shard_map/ppermute | solution.py:280
  45.8 1.6 %collective-permute-start.19 = (bf16[128,1024]{1,0:T(8,128)(2,1)S(1)}, bf16[128,1024]{1,0:T(8,128)(2,1)S(1)}, u32[]{:S(2)}, u32[]{:S(2)}) collective-permute-start(bf16[128,1024]{1,0:T(8,128)(2,1)S(1)} %add_convert_fusion.1), channel_id=1, source_target_pairs={{0,1},{1,0},{2,3},{3,2},{4,5},{5,4},{6,7},{7,6},{8,9},{9,8},{10,11... | collective-permute-start | bytes 786440 | tf_op jit(solution)/shard_map/ppermute | solution.py:280
  48.5 1.6 %collective-permute-start.10 = (bf16[32,1024]{1,0:T(8,128)(2,1)S(1)}, bf16[32,1024]{1,0:T(8,128)(2,1)S(1)}, u32[]{:S(2)}, u32[]{:S(2)}) collective-permute-start(bf16[32,1024]{1,0:T(8,128)(2,1)S(1)} %get-tuple-element.47), channel_id=1, source_target_pairs={{0,16},{4,20},{8,24},{12,28},{16,0},{20,4},{24,8},{28,12},{1,17},{... | collective-permute-start | bytes 196616 | tf_op jit(solution)/shard_map/ppermute | solution.py:280
  50.1 1.2 %collective-permute-start.12 = (bf16[32,1024]{1,0:T(8,128)(2,1)S(1)}, bf16[32,1024]{1,0:T(8,128)(2,1)S(1)}, u32[]{:S(2)}, u32[]{:S(2)}) collective-permute-start(bf16[32,1024]{1,0:T(8,128)(2,1)S(1)} %get-tuple-element.49), channel_id=1, source_target_pairs={{0,24},{4,28},{8,16},{12,20},{16,8},{20,12},{24,0},{28,4},{1,25},{... | collective-permute-start | bytes 196616 | tf_op jit(solution)/shard_map/ppermute | solution.py:280
  51.3 1.6 %collective-permute-start.13 = (bf16[32,1024]{1,0:T(8,128)(2,1)S(1)}, bf16[32,1024]{1,0:T(8,128)(2,1)S(1)}, u32[]{:S(2)}, u32[]{:S(2)}) collective-permute-start(bf16[32,1024]{1,0:T(8,128)(2,1)S(1)} %get-tuple-element.50), channel_id=1, source_target_pairs={{0,28},{4,24},{8,20},{12,16},{16,12},{20,8},{24,4},{28,0},{1,29},{... | collective-permute-start | bytes 196616 | tf_op jit(solution)/shard_map/ppermute | solution.py:280
  53.2 2.8 %collective-permute-done.11.refs_5_ = bf16[32,1024]{1,0:T(8,128)(2,1)S(1)} collective-permute-done((bf16[32,1024]{1,0:T(8,128)(2,1)S(1)}, bf16[32,1024]{1,0:T(8,128)(2,1)S(1)}, u32[]{:S(2)}, u32[]{:S(2)}) %collective-permute-start.11) | collective-permute-done | bytes 65568 | tf_op jit(solution)/shard_map/ppermute | solution.py:280
  56.0 1.7 %collective-permute-start.9 = (bf16[32,1024]{1,0:T(8,128)(2,1)S(1)}, bf16[32,1024]{1,0:T(8,128)(2,1)S(1)}, u32[]{:S(2)}, u32[]{:S(2)}) collective-permute-start(bf16[32,1024]{1,0:T(8,128)(2,1)S(1)} %get-tuple-element.46), channel_id=1, source_target_pairs={{0,12},{4,8},{8,4},{12,0},{16,28},{20,24},{24,20},{28,16},{1,13},{... | collective-permute-start | bytes 196616 | tf_op jit(solution)/shard_map/ppermute | solution.py:280
  57.8 2.6 %collective-permute-start.26 = (bf16[128,512]{1,0:T(8,128)(2,1)S(1)}, bf16[128,512]{1,0:T(8,128)(2,1)S(1)}, u32[]{:S(2)}, u32[]{:S(2)}) collective-permute-start(bf16[128,512]{1,0:T(8,128)(2,1)S(1)} %add_convert_fusion.2), channel_id=1, source_target_pairs={{0,2},{1,3},{2,0},{3,1},{4,6},{5,7},{6,4},{7,5},{8,10},{9,11},{10,... | collective-permute-start | bytes 393224 | tf_op jit(solution)/shard_map/ppermute | solution.py:280
  62.2 10.7 %collective-permute-done.26 = bf16[128,512]{1,0:T(8,128)(2,1)S(1)} collective-permute-done((bf16[128,512]{1,0:T(8,128)(2,1)S(1)}, bf16[128,512]{1,0:T(8,128)(2,1)S(1)}, u32[]{:S(2)}, u32[]{:S(2)}) %collective-permute-start.26) | collective-permute-done | bytes 131104 | tf_op jit(solution)/shard_map/ppermute | solution.py:280
  72.9 5.5 %collective-permute-done.20 = bf16[128,1024]{1,0:T(8,128)(2,1)S(1)} collective-permute-done((bf16[128,1024]{1,0:T(8,128)(2,1)S(1)}, bf16[128,1024]{1,0:T(8,128)(2,1)S(1)}, u32[]{:S(2)}, u32[]{:S(2)}) %collective-permute-start.20) | collective-permute-done | bytes 262176 | tf_op jit(solution)/shard_map/ppermute | solution.py:280
  (57 shorter events, 14.3 us)
Async XLA Ops:
  2.7 4.9 %collective-permute-start = (bf16[32,1024]{1,0:T(8,128)(2,1)S(1)}, bf16[32,1024]{1,0:T(8,128)(2,1)S(1)}, u32[]{:S(2)}, u32[]{:S(2)}) collective-permute-start(bf16[32,1024]{1,0:T(8,128)(2,1)S(1)} %get-tuple-element.33), channel_id=1, source_target_pairs={{0,4},{4,0},{8,12},{12,8},{16,20},{20,16},{24,28},{28,24},{1,5},{5... | collective-permute-start | bytes 196616 | tf_op jit(solution)/shard_map/ppermute | solution.py:280
  3.2 7.0 %collective-permute-start.1 = (bf16[32,1024]{1,0:T(8,128)(2,1)S(1)}, bf16[32,1024]{1,0:T(8,128)(2,1)S(1)}, u32[]{:S(2)}, u32[]{:S(2)}) collective-permute-start(bf16[32,1024]{1,0:T(8,128)(2,1)S(1)} %get-tuple-element.34), channel_id=1, source_target_pairs={{0,8},{4,12},{8,0},{12,4},{16,24},{20,28},{24,16},{28,20},{1,9},{5... | collective-permute-start | bytes 196616 | tf_op jit(solution)/shard_map/ppermute | solution.py:280
  5.8 4.7 %collective-permute-start.2 = (bf16[32,1024]{1,0:T(8,128)(2,1)S(1)}, bf16[32,1024]{1,0:T(8,128)(2,1)S(1)}, u32[]{:S(2)}, u32[]{:S(2)}) collective-permute-start(bf16[32,1024]{1,0:T(8,128)(2,1)S(1)} %get-tuple-element.35), channel_id=1, source_target_pairs={{0,12},{4,8},{8,4},{12,0},{16,28},{20,24},{24,20},{28,16},{1,13},{... | collective-permute-start | bytes 196616 | tf_op jit(solution)/shard_map/ppermute | solution.py:280
  5.8 4.6 %collective-permute-start.3 = (bf16[32,1024]{1,0:T(8,128)(2,1)S(1)}, bf16[32,1024]{1,0:T(8,128)(2,1)S(1)}, u32[]{:S(2)}, u32[]{:S(2)}) collective-permute-start(bf16[32,1024]{1,0:T(8,128)(2,1)S(1)} %get-tuple-element.36), channel_id=1, source_target_pairs={{0,16},{4,20},{8,24},{12,28},{16,0},{20,4},{24,8},{28,12},{1,17},{... | collective-permute-start | bytes 196616 | tf_op jit(solution)/shard_map/ppermute | solution.py:280
  7.6 5.6 %collective-permute-start.4 = (bf16[32,1024]{1,0:T(8,128)(2,1)S(1)}, bf16[32,1024]{1,0:T(8,128)(2,1)S(1)}, u32[]{:S(2)}, u32[]{:S(2)}) collective-permute-start(bf16[32,1024]{1,0:T(8,128)(2,1)S(1)} %get-tuple-element.37), channel_id=1, source_target_pairs={{0,20},{4,16},{8,28},{12,24},{16,4},{20,0},{24,12},{28,8},{1,21},{... | collective-permute-start | bytes 196616 | tf_op jit(solution)/shard_map/ppermute | solution.py:280
  7.6 5.6 %collective-permute-start.5 = (bf16[32,1024]{1,0:T(8,128)(2,1)S(1)}, bf16[32,1024]{1,0:T(8,128)(2,1)S(1)}, u32[]{:S(2)}, u32[]{:S(2)}) collective-permute-start(bf16[32,1024]{1,0:T(8,128)(2,1)S(1)} %get-tuple-element.38), channel_id=1, source_target_pairs={{0,24},{4,28},{8,16},{12,20},{16,8},{20,12},{24,0},{28,4},{1,25},{... | collective-permute-start | bytes 196616 | tf_op jit(solution)/shard_map/ppermute | solution.py:280
  10.2 4.9 %collective-permute-start.6 = (bf16[32,1024]{1,0:T(8,128)(2,1)S(1)}, bf16[32,1024]{1,0:T(8,128)(2,1)S(1)}, u32[]{:S(2)}, u32[]{:S(2)}) collective-permute-start(bf16[32,1024]{1,0:T(8,128)(2,1)S(1)} %get-tuple-element.39), channel_id=1, source_target_pairs={{0,28},{4,24},{8,20},{12,16},{16,12},{20,8},{24,4},{28,0},{1,29},{... | collective-permute-start | bytes 196616 | tf_op jit(solution)/shard_map/ppermute | solution.py:280
  22.3 6.8 %collective-permute-start.15 = (bf16[256,1024]{1,0:T(8,128)(2,1)S(1)}, bf16[256,1024]{1,0:T(8,128)(2,1)S(1)}, u32[]{:S(2)}, u32[]{:S(2)}) collective-permute-start(bf16[256,1024]{1,0:T(8,128)(2,1)S(1)} %get-tuple-element.42.d_rest_ref.d_own_ref), channel_id=1, source_target_pairs={{0,4},{4,0},{8,12},{12,8},{16,20},{20,16},{24,28},{28,24},{1,5},{5... | collective-permute-start | bytes 1572872 | tf_op jit(solution)/shard_map/ppermute | solution.py:280
  25.5 6.7 %collective-permute-start.22 = (bf16[128,512]{1,0:T(8,128)(2,1)S(1)}, bf16[128,512]{1,0:T(8,128)(2,1)S(1)}, u32[]{:S(2)}, u32[]{:S(2)}) collective-permute-start(bf16[128,512]{1,0:T(8,128)(2,1)S(1)} %get-tuple-element.58), channel_id=1, source_target_pairs={{0,8},{4,12},{8,0},{12,4},{16,24},{20,28},{24,16},{28,20},{1,9},{5... | collective-permute-start | bytes 393224 | tf_op jit(solution)/shard_map/ppermute | solution.py:280
  26.2 7.8 %collective-permute-start.23 = (bf16[128,512]{1,0:T(8,128)(2,1)S(1)}, bf16[128,512]{1,0:T(8,128)(2,1)S(1)}, u32[]{:S(2)}, u32[]{:S(2)}) collective-permute-start(bf16[128,512]{1,0:T(8,128)(2,1)S(1)} %get-tuple-element.59), channel_id=1, source_target_pairs={{0,16},{4,20},{8,24},{12,28},{16,0},{20,4},{24,8},{28,12},{1,17},{... | collective-permute-start | bytes 393224 | tf_op jit(solution)/shard_map/ppermute | solution.py:280
  27.9 7.4 %collective-permute-start.24 = (bf16[128,512]{1,0:T(8,128)(2,1)S(1)}, bf16[128,512]{1,0:T(8,128)(2,1)S(1)}, u32[]{:S(2)}, u32[]{:S(2)}) collective-permute-start(bf16[128,512]{1,0:T(8,128)(2,1)S(1)} %get-tuple-element.60), channel_id=1, source_target_pairs={{0,24},{4,28},{8,16},{12,20},{16,8},{20,12},{24,0},{28,4},{1,25},{... | collective-permute-start | bytes 393224 | tf_op jit(solution)/shard_map/ppermute | solution.py:280
  29.8 10.6 %collective-permute-start.16 = (bf16[128,1024]{1,0:T(8,128)(2,1)S(1)}, bf16[128,1024]{1,0:T(8,128)(2,1)S(1)}, u32[]{:S(2)}, u32[]{:S(2)}) collective-permute-start(bf16[128,1024]{1,0:T(8,128)(2,1)S(1)} %get-tuple-element.54), channel_id=1, source_target_pairs={{0,8},{4,12},{8,0},{12,4},{16,24},{20,28},{24,16},{28,20},{1,9},{5... | collective-permute-start | bytes 786440 | tf_op jit(solution)/shard_map/ppermute | solution.py:280
  30.5 15.1 %collective-permute-start.17 = (bf16[128,1024]{1,0:T(8,128)(2,1)S(1)}, bf16[128,1024]{1,0:T(8,128)(2,1)S(1)}, u32[]{:S(2)}, u32[]{:S(2)}) collective-permute-start(bf16[128,1024]{1,0:T(8,128)(2,1)S(1)} %get-tuple-element.55), channel_id=1, source_target_pairs={{0,16},{4,20},{8,24},{12,28},{16,0},{20,4},{24,8},{28,12},{1,17},{... | collective-permute-start | bytes 786440 | tf_op jit(solution)/shard_map/ppermute | solution.py:280
  32.2 13.5 %collective-permute-start.18 = (bf16[128,1024]{1,0:T(8,128)(2,1)S(1)}, bf16[128,1024]{1,0:T(8,128)(2,1)S(1)}, u32[]{:S(2)}, u32[]{:S(2)}) collective-permute-start(bf16[128,1024]{1,0:T(8,128)(2,1)S(1)} %get-tuple-element.56), channel_id=1, source_target_pairs={{0,24},{4,28},{8,16},{12,20},{16,8},{20,12},{24,0},{28,4},{1,25},{... | collective-permute-start | bytes 786440 | tf_op jit(solution)/shard_map/ppermute | solution.py:280
  35.3 16.0 %collective-permute-start.25 = (bf16[128,512]{1,0:T(8,128)(2,1)S(1)}, bf16[128,512]{1,0:T(8,128)(2,1)S(1)}, u32[]{:S(2)}, u32[]{:S(2)}) collective-permute-start(bf16[128,512]{1,0:T(8,128)(2,1)S(1)} %add_convert_fusion.3), channel_id=1, source_target_pairs={{0,1},{1,0},{2,3},{3,2},{4,5},{5,4},{6,7},{7,6},{8,9},{9,8},{10,11... | collective-permute-start | bytes 393224 | tf_op jit(solution)/shard_map/ppermute | solution.py:280
  45.8 11.9 %collective-permute-start.19 = (bf16[128,1024]{1,0:T(8,128)(2,1)S(1)}, bf16[128,1024]{1,0:T(8,128)(2,1)S(1)}, u32[]{:S(2)}, u32[]{:S(2)}) collective-permute-start(bf16[128,1024]{1,0:T(8,128)(2,1)S(1)} %add_convert_fusion.1), channel_id=1, source_target_pairs={{0,1},{1,0},{2,3},{3,2},{4,5},{5,4},{6,7},{7,6},{8,9},{9,8},{10,11... | collective-permute-start | bytes 786440 | tf_op jit(solution)/shard_map/ppermute | solution.py:280
  50.1 6.0 %collective-permute-start.11 = (bf16[32,1024]{1,0:T(8,128)(2,1)S(1)}, bf16[32,1024]{1,0:T(8,128)(2,1)S(1)}, u32[]{:S(2)}, u32[]{:S(2)}) collective-permute-start(bf16[32,1024]{1,0:T(8,128)(2,1)S(1)} %get-tuple-element.48), channel_id=1, source_target_pairs={{0,20},{4,16},{8,28},{12,24},{16,4},{20,0},{24,12},{28,8},{1,21},{... | collective-permute-start | bytes 196616 | tf_op jit(solution)/shard_map/ppermute | solution.py:280
  50.1 6.0 %collective-permute-start.12 = (bf16[32,1024]{1,0:T(8,128)(2,1)S(1)}, bf16[32,1024]{1,0:T(8,128)(2,1)S(1)}, u32[]{:S(2)}, u32[]{:S(2)}) collective-permute-start(bf16[32,1024]{1,0:T(8,128)(2,1)S(1)} %get-tuple-element.49), channel_id=1, source_target_pairs={{0,24},{4,28},{8,16},{12,20},{16,8},{20,12},{24,0},{28,4},{1,25},{... | collective-permute-start | bytes 196616 | tf_op jit(solution)/shard_map/ppermute | solution.py:280
  51.3 9.1 %collective-permute-start.13 = (bf16[32,1024]{1,0:T(8,128)(2,1)S(1)}, bf16[32,1024]{1,0:T(8,128)(2,1)S(1)}, u32[]{:S(2)}, u32[]{:S(2)}) collective-permute-start(bf16[32,1024]{1,0:T(8,128)(2,1)S(1)} %get-tuple-element.50), channel_id=1, source_target_pairs={{0,28},{4,24},{8,20},{12,16},{16,12},{20,8},{24,4},{28,0},{1,29},{... | collective-permute-start | bytes 196616 | tf_op jit(solution)/shard_map/ppermute | solution.py:280
  53.0 7.9 %collective-permute-start.7 = (bf16[32,1024]{1,0:T(8,128)(2,1)S(1)}, bf16[32,1024]{1,0:T(8,128)(2,1)S(1)}, u32[]{:S(2)}, u32[]{:S(2)}) collective-permute-start(bf16[32,1024]{1,0:T(8,128)(2,1)S(1)} %get-tuple-element.44), channel_id=1, source_target_pairs={{0,4},{4,0},{8,12},{12,8},{16,20},{20,16},{24,28},{28,24},{1,5},{5... | collective-permute-start | bytes 196616 | tf_op jit(solution)/shard_map/ppermute | solution.py:280
  56.0 4.9 %collective-permute-start.8 = (bf16[32,1024]{1,0:T(8,128)(2,1)S(1)}, bf16[32,1024]{1,0:T(8,128)(2,1)S(1)}, u32[]{:S(2)}, u32[]{:S(2)}) collective-permute-start(bf16[32,1024]{1,0:T(8,128)(2,1)S(1)} %get-tuple-element.45), channel_id=1, source_target_pairs={{0,8},{4,12},{8,0},{12,4},{16,24},{20,28},{24,16},{28,20},{1,9},{5... | collective-permute-start | bytes 196616 | tf_op jit(solution)/shard_map/ppermute | solution.py:280
  56.0 5.1 %collective-permute-start.9 = (bf16[32,1024]{1,0:T(8,128)(2,1)S(1)}, bf16[32,1024]{1,0:T(8,128)(2,1)S(1)}, u32[]{:S(2)}, u32[]{:S(2)}) collective-permute-start(bf16[32,1024]{1,0:T(8,128)(2,1)S(1)} %get-tuple-element.46), channel_id=1, source_target_pairs={{0,12},{4,8},{8,4},{12,0},{16,28},{20,24},{24,20},{28,16},{1,13},{... | collective-permute-start | bytes 196616 | tf_op jit(solution)/shard_map/ppermute | solution.py:280
  57.8 15.1 %collective-permute-start.26 = (bf16[128,512]{1,0:T(8,128)(2,1)S(1)}, bf16[128,512]{1,0:T(8,128)(2,1)S(1)}, u32[]{:S(2)}, u32[]{:S(2)}) collective-permute-start(bf16[128,512]{1,0:T(8,128)(2,1)S(1)} %add_convert_fusion.2), channel_id=1, source_target_pairs={{0,2},{1,3},{2,0},{3,1},{4,6},{5,7},{6,4},{7,5},{8,10},{9,11},{10,... | collective-permute-start | bytes 393224 | tf_op jit(solution)/shard_map/ppermute | solution.py:280
  60.4 18.0 %collective-permute-start.20 = (bf16[128,1024]{1,0:T(8,128)(2,1)S(1)}, bf16[128,1024]{1,0:T(8,128)(2,1)S(1)}, u32[]{:S(2)}, u32[]{:S(2)}) collective-permute-start(bf16[128,1024]{1,0:T(8,128)(2,1)S(1)} %add_convert_fusion), channel_id=1, source_target_pairs={{0,2},{1,3},{2,0},{3,1},{4,6},{5,7},{6,4},{7,5},{8,10},{9,11},{10,... | collective-permute-start | bytes 786440 | tf_op jit(solution)/shard_map/ppermute | solution.py:280
  (10 other events, 54.5 us)

commit v2 on v1

--- a/solution.py
+++ b/solution.py
@@ -106,22 +106,23 @@
 ROWS_BY_COLS = (((1,), (0,)), ((), ()))
 COLS_BY_COLS = (((1,), (1,)), ((), ()))
 ROWS_BY_ROWS = (((0,), (0,)), ((), ()))
-VMEM_LIMIT = 40 * 1024 * 1024
+VMEM_LIMIT = 32 * 1024 * 1024
+HBM = pl.BlockSpec(memory_space=pltpu.HBM)
+VMEM = pl.BlockSpec(memory_space=pltpu.VMEM)
 
 
 def matmul(left, right, contract=ROWS_BY_COLS):
     return lax.dot_general(left, right, contract, preferred_element_type=F32)
 
 
-def call(kernel, outs, operands, flops, scratch=()):
+def call(kernel, outs, operands, flops, scratch=(), specs=None):
     nbytes = sum(a.size * a.dtype.itemsize for a in operands)
     nbytes += sum(o.size * o.dtype.itemsize for o in outs)
-    vmem = pl.BlockSpec(memory_space=pltpu.VMEM)
     return pl.pallas_call(
         kernel,
         out_shape=outs,
-        in_specs=[vmem] * len(operands),
-        out_specs=[vmem] * len(outs),
+        in_specs=specs or [VMEM] * len(operands),
+        out_specs=[VMEM] * len(outs),
         scratch_shapes=list(scratch),
         compiler_params=pltpu.CompilerParams(vmem_limit_bytes=VMEM_LIMIT),
         cost_estimate=pl.CostEstimate(flops=flops, bytes_accessed=nbytes, transcendentals=0),
@@ -148,21 +149,23 @@
     return (lax.broadcasted_iota(jnp.int32, (peers * capacity, rows), 0) == key).astype(BF16)
 
 
-def pack_kernel(peers, capacity, users_ref, tokens_ref, *out_refs):
+def fetch(pairs, sems):
+    copies = [pltpu.make_async_copy(src, dst, sems.at[i]) for i, (src, dst) in enumerate(pairs)]
+    for copy in copies:
+        copy.start()
+    return copies
+
+
+def pack_kernel(peers, capacity, users_hbm, tokens_hbm, *refs):
+    *out_refs, users, rows, sems = refs
+    users_copy, rows_copy = fetch([(users_hbm, users), (tokens_hbm, rows)], sems)
     me = lax.axis_index("dp")
-    place = own_placement(users_ref, me, peers, capacity)
-    packed = matmul(place, tokens_ref[...]).astype(BF16)
-    for m in range(peers):
-        out_refs[m][...] = packed[m * capacity : (m + 1) * capacity]
-
-
-def unpack_kernel(peers, capacity, users_ref, *refs):
-    *in_refs, out_ref, held = refs
-    me = lax.axis_index("dp")
-    place = own_placement(users_ref, me, peers, capacity)
-    for m in range(peers):
-        held[m * capacity : (m + 1) * capacity, :] = in_refs[m][...]
-    out_ref[...] = matmul(place, held[...], ROWS_BY_ROWS).astype(BF16)
+    users_copy.wait()
+    place = own_placement(users, me, peers, capacity)
+    rows_copy.wait()
+    packed = matmul(place, rows[...]).astype(BF16)
+    for i, out_ref in enumerate(out_refs):
+        out_ref[...] = packed[2 * i * capacity : 2 * (i + 1) * capacity]
 
 
 def slot_codes(users_ref, me, peers, capacity):
@@ -180,25 +183,42 @@
     return jnp.concatenate(codes, axis=0)
 
 
-def attend_kernel(peers, capacity, users_ref, gain_ref, w_ref, grad_ref, *refs):
-    x_refs, refs = refs[:peers], refs[peers:]
-    attended_ref, d_values_ref, d_rest_ref, x_own_ref, x_sib_ref, x, act, slope, grad = refs
+def prep_kernel(peers, capacity, users_hbm, gain_ref, w_hbm, grad_hbm, w_ref, grad_ref, code_ref, key_ref, users, grad, sems):
+    users_copy, grad_copy, w_copy = fetch([(users_hbm, users), (grad_hbm, grad), (w_hbm, w_ref)], sems)
+    me = lax.axis_index("dp")
+    users_copy.wait()
+    code = jnp.broadcast_to(slot_codes(users, me, peers, capacity), code_ref.shape)
+    code_ref[...] = code
+    key_ref[...] = code.T[0 : key_ref.shape[0]]
+    grad_copy.wait()
+    for m in range(peers):
+        at = pl.multiple_of((me ^ m) * capacity, capacity)
+        grad_ref[m * capacity : (m + 1) * capacity, :] = grad[pl.ds(at, capacity), :].astype(F32) * gain_ref[...]
+    w_copy.wait()
+
+
+def attend_kernel(peers, capacity, batch_rows, gain_ref, w_ref, grad, code_ref, key_ref, *refs):
+    chips = peers // 2
+    near, far, refs = refs[:chips], refs[chips : 2 * chips], refs[2 * chips :]
+    attended_ref, *d_refs, x_own_ref, x_sib_ref, x, x_sib, act, slope = refs
     me = lax.axis_index("dp")
     slots = peers * capacity
     width, columns = w_ref.shape
     features = gain_ref.shape[1]
     block = width // peers
-    for m in range(peers):
-        x[m * capacity : (m + 1) * capacity, :] = x_refs[m][...]
-    for i in range(peers // 2):
-        own_at = pl.multiple_of((me ^ (2 * i)) * block, block)
-        sib_at = pl.multiple_of((me ^ (2 * i + 1)) * block, block)
-        x_own_ref[:, i * block : (i + 1) * block] = x[:, pl.ds(own_at, block)]
-        x_sib_ref[:, i * block : (i + 1) * block] = x[:, pl.ds(sib_at, block)]
+    first, second = slice(0, capacity), slice(capacity, 2 * capacity)
+    for i in range(chips):
+        even = slice(2 * i * capacity, (2 * i + 1) * capacity)
+        odd = slice((2 * i + 1) * capacity, (2 * i + 2) * capacity)
+        x[even, :] = near[i][first, :]
+        x[odd, :] = far[i][second, :]
+        x_sib[even, :] = far[i][first, :]
+        x_sib[odd, :] = near[i][second, :]
+    for i in range(chips):
+        at = pl.multiple_of((me ^ (2 * i)) * block, block)
+        x_own_ref[:, i * block : (i + 1) * block] = x[:, pl.ds(at, block)]
+        x_sib_ref[:, i * block : (i + 1) * block] = x_sib[:, pl.ds(at, block)]
     gain = gain_ref[...]
-    for m in range(peers):
-        at = pl.multiple_of((me ^ m) * capacity, capacity)
-        grad[m * capacity : (m + 1) * capacity, :] = grad_ref[pl.ds(at, capacity), :].astype(F32) * gain
     step = 2 * HEAD_DIM
     for c in range(0, columns, step):
         preact = matmul(x[...], w_ref[:, c : c + step])
@@ -207,11 +227,9 @@
         act[:, c : c + step] = silu.astype(BF16)
         slope[:, c : c + step] = gate + silu * (1.0 - gate)
 
-    code = slot_codes(users_ref, me, peers, capacity)
-    code_of_key = jnp.broadcast_to(code, (slots, HEAD_DIM)).T[0:1]
-    batch_rows = users_ref.shape[0] * users_ref.shape[1]
-    whole = code.astype(jnp.int32)
-    first = (lax.div(whole, batch_rows) * batch_rows).astype(F32)
+    code = code_ref[:, 0:1]
+    code_of_key = key_ref[0:1, :]
+    first = (lax.div(code.astype(jnp.int32), batch_rows) * batch_rows).astype(F32)
     first = jnp.where(code > 0.0, first, code + 1.0)
     visible = (code_of_key <= code) & (code_of_key >= first)
 
@@ -245,35 +263,103 @@
             attended_ref[pl.ds(at, capacity), h * HEAD_DIM : (h + 1) * HEAD_DIM] = normed[m * capacity : (m + 1) * capacity]
     grad_mean = sum(jnp.sum(g, axis=1, keepdims=True) for g in grads) / features
     grad_unit = sum(jnp.sum(g * u, axis=1, keepdims=True) for g, u in zip(grads, unit)) / features
+    per = HEADS // len(d_refs)
     for h in range(HEADS):
+        d_ref, at = d_refs[h // per], (h % per) * HEAD_DIM
         d_mixed = ((grads[h] - grad_mean - unit[h] * grad_unit) * inverse).astype(BF16)
-        d_value = matmul(weights[h], d_mixed, ROWS_BY_ROWS)
-        at = h * HEAD_DIM
-        d_values_ref[:, at : at + HEAD_DIM] = (d_value * part(slope, 2 * HEADS + h)).astype(BF16)
         d_scores = (matmul(d_mixed, head(2 * features, h), COLS_BY_COLS) * slopes[h]).astype(BF16)
         d_query = matmul(d_scores, head(features, h))
         d_key = matmul(d_scores, head(0, h), ROWS_BY_ROWS)
-        d_rest_ref[:, at : at + HEAD_DIM] = (d_query * part(slope, h)).astype(BF16)
-        at += features
-        d_rest_ref[:, at : at + HEAD_DIM] = (d_key * part(slope, HEADS + h)).astype(BF16)
+        d_value = matmul(weights[h], d_mixed, ROWS_BY_ROWS)
+        for j, d in enumerate((d_query, d_key, d_value)):
+            to = j * per * HEAD_DIM + at
+            d_ref[:, to : to + HEAD_DIM] = (d * part(slope, j * HEADS + h)).astype(BF16)
+
+
+def weight_block(i, x_own_ref, x_sib_ref, d_own_ref, d_sib_ref, block):
+    at = slice(i * block, (i + 1) * block)
+    total = matmul(x_own_ref[:, at], d_own_ref[...], ROWS_BY_ROWS)
+    return total + matmul(x_sib_ref[:, at], d_sib_ref[...], ROWS_BY_ROWS)
 
 
 def weight_kernel(x_own_ref, x_sib_ref, d_own_ref, d_sib_ref, *out_refs):
     block = x_own_ref.shape[1] // len(out_refs)
     for i, out_ref in enumerate(out_refs):
-        at = slice(i * block, (i + 1) * block)
-        total = matmul(x_own_ref[:, at], d_own_ref[...], ROWS_BY_ROWS)
-        total += matmul(x_sib_ref[:, at], d_sib_ref[...], ROWS_BY_ROWS)
-        out_ref[...] = total.astype(out_ref.dtype)
-
-
-def token_kernel(d_values_ref, d_rest_ref, w_ref, *out_refs):
-    split = d_rest_ref.shape[1]
-    capacity = out_refs[0].shape[0]
-    total = matmul(d_rest_ref[...], w_ref[:, :split], COLS_BY_COLS)
-    total += matmul(d_values_ref[...], w_ref[:, split:], COLS_BY_COLS)
-    for m, out_ref in enumerate(out_refs):
-        out_ref[...] = total[m * capacity : (m + 1) * capacity].astype(BF16)
+        out_ref[...] = weight_block(i, x_own_ref, x_sib_ref, d_own_ref, d_sib_ref, block).astype(out_ref.dtype)
+
+
+def halves(half):
+    side = lax.rem(lax.axis_index("replica"), 2)
+    return pl.multiple_of(side * half, half), pl.multiple_of((1 - side) * half, half)
+
+
+def weight_halves_kernel(blocks, x_own_ref, x_sib_ref, d_own_ref, d_sib_ref, keep_ref, send_ref, held):
+    block = held.shape[0]
+    half = block // 2
+    keep_at, send_at = halves(half)
+    for i in range(blocks):
+        held[...] = weight_block(i, x_own_ref, x_sib_ref, d_own_ref, d_sib_ref, block)
+        rows = slice(i * half, (i + 1) * half)
+        keep_ref[rows, :] = held[pl.ds(keep_at, half), :]
+        send_ref[rows, :] = held[pl.ds(send_at, half), :].astype(BF16)
+
+
+def sum_halves_kernel(own_ref, *refs):
+    *in_refs, keep_ref, send_ref, held = refs
+    half = held.shape[0] // 2
+    total = own_ref[...]
+    for in_ref in in_refs:
+        total = total + in_ref[...].astype(F32)
+    held[...] = total
+    keep_at, send_at = halves(half)
+    keep_ref[...] = held[pl.ds(keep_at, half), :]
+    send_ref[...] = held[pl.ds(send_at, half), :].astype(BF16)
+
+
+def sum_blocks_kernel(keep_ref, in_ref, *out_refs):
+    half = out_refs[0].shape[0]
+    for i, out_ref in enumerate(out_refs):
+        rows = slice(i * half, (i + 1) * half)
+        out_ref[...] = (keep_ref[rows, :] + in_ref[rows, :].astype(F32)).astype(out_ref.dtype)
+
+
+def join_kernel(features, *refs):
+    *in_refs, out_ref = refs
+    half, size = in_refs[0].shape
+    keep_at, send_at = halves(half)
+    per = size // 3
+    for p in range(len(in_refs) // 2):
+        for in_ref, at in ((in_refs[2 * p], keep_at), (in_refs[2 * p + 1], send_at)):
+            for j in range(3):
+                to = j * features + p * per
+                out_ref[pl.ds(at, half), to : to + per] = in_ref[:, j * per : (j + 1) * per].astype(F32)
+
+
+def token_kernel(features, w_ref, *refs):
+    d_refs, out_refs = refs[:2], refs[2:]
+    rows = out_refs[0].shape[0]
+    per = d_refs[0].shape[1] // 3
+    total = None
+    for p, d_ref in enumerate(d_refs):
+        for j in range(3):
+            at = j * features + p * per
+            term = matmul(d_ref[:, j * per : (j + 1) * per], w_ref[:, at : at + per], COLS_BY_COLS)
+            total = term if total is None else total + term
+    for i, out_ref in enumerate(out_refs):
+        out_ref[...] = total[i * rows : (i + 1) * rows].astype(BF16)
+
+
+def unpack_kernel(peers, capacity, users_hbm, *refs):
+    chips = peers // 2
+    near, far, (out_ref, held, users, sems) = refs[:chips], refs[chips : 2 * chips], refs[2 * chips :]
+    (users_copy,) = fetch([(users_hbm, users)], sems)
+    me = lax.axis_index("dp")
+    for i in range(chips):
+        held[2 * i * capacity : (2 * i + 1) * capacity, :] = near[i][0:capacity, :]
+        held[(2 * i + 1) * capacity : (2 * i + 2) * capacity, :] = far[i][capacity : 2 * capacity, :]
+    users_copy.wait()
+    place = own_placement(users, me, peers, capacity)
+    out_ref[...] = matmul(place, held[...], ROWS_BY_ROWS).astype(BF16)
 
 
 def swap(array, axis, size, bits):
@@ -288,78 +374,129 @@
     features = grad_out.shape[2]
     capacity = 2 * rows // peers
     slots = peers * capacity
+    chips = peers // 2
     block = width // peers
+    half = block // 2
+    size = columns // 2
     users = user_of_row.reshape(peers, rows)
     gain = norm_gain.reshape(1, features)
     exchange = functools.partial(swap, axis="dp", size=peers)
-
-    outgoing = call(
+    swap_replicas = functools.partial(swap, axis="replica", size=replicas)
+    pair = shaped((2 * capacity, width), BF16)
+    users_scratch = pltpu.VMEM((peers, rows), jnp.int32)
+
+    def to_sources(pairs):
+        return [pairs[0]] + [exchange(pairs[i], bits=2 * i) for i in range(1, chips)]
+
+    def to_siblings(pairs):
+        return [exchange(a, bits=1) for a in pairs]
+
+    packed = call(
         functools.partial(pack_kernel, peers, capacity),
-        [shaped((capacity, width), BF16)] * peers,
+        [pair] * chips,
         [users, tokens[0]],
         2 * slots * rows * width,
-    )
-    arrived = [outgoing[0]] + [exchange(outgoing[m], bits=m) for m in range(1, peers)]
-    half = width // 2
-    attended, d_values, d_rest, x_own, x_sib = call(
-        functools.partial(attend_kernel, peers, capacity),
+        [users_scratch, pltpu.VMEM((rows, width), BF16), pltpu.SemaphoreType.DMA((2,))],
+        [HBM, HBM],
+    )
+    near = to_sources(packed)
+    w_held, grad, code, key = call(
+        functools.partial(prep_kernel, peers, capacity),
         [
-            shaped((slots, features), BF16),
-            shaped((slots, features), BF16),
-            shaped((slots, columns - features), BF16),
-            shaped((slots, half), BF16),
-            shaped((slots, half), BF16),
+            shaped((width, columns), BF16),
+            shaped((slots, features), F32),
+            shaped((slots, HEAD_DIM), F32),
+            shaped((8, slots), F32),
         ],
-        [users, gain, proj_weight, grad_out[0], *arrived],
+        [users, gain, proj_weight, grad_out[0]],
+        2 * slots * slots * rows,
+        [users_scratch, pltpu.VMEM((slots, features), BF16), pltpu.SemaphoreType.DMA((3,))],
+        [HBM, VMEM, HBM, HBM],
+    )
+    near, (w_held, grad, code, key) = lax.optimization_barrier((near, (w_held, grad, code, key)))
+    far = to_siblings(near)
+    attended, d_first, d_second, x_own, x_sib = call(
+        functools.partial(attend_kernel, peers, capacity, peers * rows),
+        [shaped((slots, features), BF16)] + [shaped((slots, size), BF16)] * 2 + [shaped((slots, width // 2), BF16)] * 2,
+        [gain, w_held, grad, code, key, *near, *far],
         2 * slots * width * columns + 14 * slots * slots * features,
         [
             pltpu.VMEM((slots, width), BF16),
+            pltpu.VMEM((slots, width), BF16),
             pltpu.VMEM((slots, columns), BF16),
             pltpu.VMEM((slots, columns), F32),
-            pltpu.VMEM((slots, features), F32),
         ],
     )
-    x_from_sib = exchange(x_sib, bits=1)
-    blocks = []
-    for d_own in (d_values, d_rest):
-        size = d_own.shape[1]
-        d_from_sib = exchange(d_own, bits=1)
-        mine, *others = call(
-            weight_kernel,
-            [shaped((block, size), F32)] + [shaped((block, size), BF16)] * (peers // 2 - 1),
-            [x_own, x_from_sib, d_own, d_from_sib],
-            4 * slots * half * size,
-        )
-        total = mine
-        for i, other in enumerate(others):
-            total = total + exchange(other, bits=2 * (i + 1)).astype(F32)
-        bits = 1
-        while bits < replicas:
-            held = total.astype(BF16)
-            total = held.astype(F32) + swap(held, "replica", replicas, bits).astype(F32)
-            bits *= 2
-        blocks.append(total)
-    grad_weight = jnp.concatenate([blocks[1], blocks[0]], axis=1)
-
+    flops = 4 * slots * (width // 2) * size
+    own, *others = call(
+        weight_kernel,
+        [shaped((block, size), F32)] + [shaped((block, size), BF16)] * (chips - 1),
+        [x_own, x_sib, d_first, exchange(d_first, bits=1)],
+        flops,
+    )
+    keep_second, send_second = call(
+        functools.partial(weight_halves_kernel, chips),
+        [shaped((chips * half, size), F32), shaped((chips * half, size), BF16)],
+        [x_own, x_sib, d_second, exchange(d_second, bits=1)],
+        flops,
+        [pltpu.VMEM((block, size), F32)],
+    )
+    from_plane = [exchange(other, bits=2 * (i + 1)) for i, other in enumerate(others)]
+    from_neighbour = swap_replicas(send_second, bits=1)
+    keep_first, send_first = call(
+        sum_halves_kernel,
+        [shaped((half, size), F32), shaped((half, size), BF16)],
+        [own, *from_plane],
+        chips * block * size,
+        [pltpu.VMEM((block, size), F32)],
+    )
+    own_second, *others_second = call(
+        sum_blocks_kernel,
+        [shaped((half, size), F32)] + [shaped((half, size), BF16)] * (chips - 1),
+        [keep_second, from_neighbour],
+        chips * half * size,
+    )
+    first = keep_first + swap_replicas(send_first, bits=1).astype(F32)
+    second = own_second
+    for i, other in enumerate(others_second):
+        second = second + exchange(other, bits=2 * (i + 1)).astype(F32)
     d_slots = call(
-        token_kernel,
-        [shaped((capacity, width), BF16)] * peers,
-        [d_values, d_rest, proj_weight],
+        functools.partial(token_kernel, features),
+        [pair] * chips,
+        [w_held, d_first, d_second],
         2 * slots * width * columns,
     )
-    returned = [d_slots[0]] + [exchange(d_slots[m], bits=m) for m in range(1, peers)]
+    d_slots, second = lax.optimization_barrier((d_slots, second))
+    near = to_sources(d_slots)
+    far = to_siblings(near)
     (grad_tokens,) = call(
         functools.partial(unpack_kernel, peers, capacity),
         [shaped((rows, width), BF16)],
-        [users, *returned],
+        [users, *near, *far],
         2 * slots * rows * width,
-        [pltpu.VMEM((slots, width), BF16)],
-    )
+        [pltpu.VMEM((slots, width), BF16), users_scratch, pltpu.SemaphoreType.DMA((1,))],
+        [HBM] + [VMEM] * (2 * chips),
+    )
+    joined = []
+    for total in (first, second):
+        held = total.astype(BF16)
+        bits = 2
+        while bits < replicas:
+            held = (held.astype(F32) + swap_replicas(held, bits=bits).astype(F32)).astype(BF16)
+            bits *= 2
+        joined += [held, swap_replicas(held, bits=1)]
+    (grad_weight,) = call(
+        functools.partial(join_kernel, features),
+        [shaped((block, columns), F32)],
+        joined,
+        block * columns,
+    )
+
     return (attended[None], grad_tokens[None], grad_weight)
 
 
 def power_of_two(value):
-    return value & (value - 1) == 0
+    return value > 1 and value & (value - 1) == 0
 
 
 def body(tokens, user_of_row, proj_weight, norm_gain, grad_out):

time: 79.7 us -> 63.9 us (0.80)
  waiting for transfers between devices: 36.2 us -> 20.1 us
  Pallas kernels: 7.29 us -> 9.59 us
  other arithmetic: 1.36 us -> 0.12 us
  starting transfers between devices: 28.6 us -> 27.8 us
    ppermute x27 -> x28, waiting for transfers between devices: 36.2 us -> 20.1 us  [swap(): return lax.ppermute(array, axis, [(i, i ^ bits) for i in range(size)])]
    pallas_call x6 -> x10, Pallas kernels: 7.29 us -> 9.59 us  [call(): pl.pallas_call(kernel, out_shape=outs, in_specs=specs or [VMEM] * len(ope...]
    concatenate x1 -> x0, other arithmetic: 0.94 us -> none  [direct_body(): grad_weight = jnp.concatenate([blocks[1], blocks[0]], axis=1)]
    ppermute x27 -> x28, starting transfers between devices: 28.6 us -> 27.8 us  [swap(): return lax.ppermute(array, axis, [(i, i ^ bits) for i in range(size)])]
    unnamed x14 -> x12, local copies, waits for them, and re-layouts: 5.16 us -> 5.16 us
  transfers between devices with their start and end apart: 27 -> 28, of which waited for: 13 -> 14; matrix products, arithmetic and copies ran while one was open for 0% -> 0% of each run, Pallas kernels for 4% -> 7%
where the time goes in v2:
time: 63.9 us; the launch traced here: 63.6 us
  starting transfers between devices  27.8 us (44%)
  waiting for transfers between devices  20.1 us (31%)
  Pallas kernels  9.59 us (15%)
  local copies, waits for them, and re-layouts  5.16 us (8%)
  between operations  0.78 us (1%)
    ppermute x28, starting transfers between devices, swap(): return lax.ppermute(array, axis, [(i, i ^ bits) for i in range(size)])  27.8 us
    ppermute x28, waiting for transfers between devices, swap(): return lax.ppermute(array, axis, [(i, i ^ bits) for i in range(size)])  20.1 us
    pallas_call x10, Pallas kernels, call(): pl.pallas_call(kernel, out_shape=outs, in_specs=specs or [VMEM] * len(ope...  9.59 us
    unnamed x12, local copies, waits for them, and re-layouts  5.16 us
  transfers between devices with their start and end apart: 28, of which 14 were waited for; matrix products, arithmetic and copies ran while one was open for 0% of the time, Pallas kernels for 7%

profile of v2, /device:TPU:0, one launch (start us, length us, event | category | flops | bytes accessed | tf_op | source)
XLA Modules:
  0.0 63.6 jit_solution(15452222118622859976)
XLA Ops:
  2.8 3.0 %collective-permute-start = (bf16[64,1024]{1,0:T(8,128)(2,1)S(1)}, bf16[64,1024]{1,0:T(8,128)(2,1)S(1)}, u32[]{:S(2)}, u32[]{:S(2)}) collective-permute-start(bf16[64,1024]{1,0:T(8,128)(2,1)S(1)} %get-tuple-element.46), channel_id=1, source_target_pairs={{0,8},{4,12},{8,0},{12,4},{16,24},{20,28},{24,16},{28,20},{1,9},{5... | collective-permute-start | bytes 393224 | tf_op jit(solution)/shard_map/ppermute | solution.py:366
  5.8 1.5 %collective-permute-start.1 = (bf16[64,1024]{1,0:T(8,128)(2,1)S(1)}, bf16[64,1024]{1,0:T(8,128)(2,1)S(1)}, u32[]{:S(2)}, u32[]{:S(2)}) collective-permute-start(bf16[64,1024]{1,0:T(8,128)(2,1)S(1)} %get-tuple-element.47), channel_id=1, source_target_pairs={{0,16},{4,20},{8,24},{12,28},{16,0},{20,4},{24,8},{28,12},{1,17},{... | collective-permute-start | bytes 393224 | tf_op jit(solution)/shard_map/ppermute | solution.py:366
  7.3 1.9 %copy-done = bf16[1024,1536]{1,0:T(8,128)(2,1)S(1)} copy-done((bf16[1024,1536]{1,0:T(8,128)(2,1)S(1)}, bf16[1024,1536]{1,0:T(8,128)(2,1)}, u32[]{:S(2)}) %copy-start) | copy-done | bytes 3145752
  11.5 2.0 %collective-permute-done.1.refs_2_ = bf16[64,1024]{1,0:T(8,128)(2,1)S(1)} collective-permute-done((bf16[64,1024]{1,0:T(8,128)(2,1)S(1)}, bf16[64,1024]{1,0:T(8,128)(2,1)S(1)}, u32[]{:S(2)}, u32[]{:S(2)}) %collective-permute-start.1) | collective-permute-done | bytes 131104 | tf_op jit(solution)/shard_map/ppermute | solution.py:366
  15.6 3.7 %shard_map.78 = (bf16[256,512]{1,0:T(8,128)(2,1)}, bf16[256,768]{1,0:T(8,128)(2,1)S(1)}, bf16[256,768]{1,0:T(8,128)(2,1)S(1)}, bf16[256,512]{1,0:T(8,128)(2,1)S(1)}, bf16[256,512]{1,0:T(8,128)(2,1)S(1)}) custom-call(f32[1,512]{1,0:T(1,128)S(1)} %bitcast.12, bf16[1024,1536]{1,0:T(8,128)(2,1)S(1)} %get-tuple-element.53.w_ref, ...), custom_call_target="tpu_custom_call" | custom-call | flops 1275068416 | bytes 6432768 | tf_op jit(solution)/shard_map/pallas_call | solution.py:121
  19.8 1.2 %collective-permute-done.7.d_sib_ref = bf16[256,768]{1,0:T(8,128)(2,1)S(1)} collective-permute-done((bf16[256,768]{1,0:T(8,128)(2,1)S(1)}, bf16[256,768]{1,0:T(8,128)(2,1)S(1)}, u32[]{:S(2)}, u32[]{:S(2)}) %collective-permute-start.7) | collective-permute-done | bytes 393248 | tf_op jit(solution)/shard_map/ppermute | solution.py:366
  21.8 1.7 %collective-permute-start.8 = (bf16[256,768]{1,0:T(8,128)(2,1)S(1)}, bf16[256,768]{1,0:T(8,128)(2,1)S(1)}, u32[]{:S(2)}, u32[]{:S(2)}) collective-permute-start(bf16[256,768]{1,0:T(8,128)(2,1)S(1)} %get-tuple-element.71), channel_id=1, source_target_pairs={{0,1},{1,0},{2,3},{3,2},{4,5},{5,4},{6,7},{7,6},{8,9},{9,8},{10,11... | collective-permute-start | bytes 1179656 | tf_op jit(solution)/shard_map/ppermute | solution.py:366
  24.1 1.3 %collective-permute-start.20 = (bf16[128,768]{1,0:T(8,128)(2,1)S(1)}, bf16[128,768]{1,0:T(8,128)(2,1)S(1)}, u32[]{:S(2)}, u32[]{:S(2)}) collective-permute-start(bf16[128,768]{1,0:T(8,128)(2,1)S(1)} %get-tuple-element.81), channel_id=1, source_target_pairs={{0,8},{4,12},{8,0},{12,4},{16,24},{20,28},{24,16},{28,20},{1,9},{5... | collective-permute-start | bytes 589832 | tf_op jit(solution)/shard_map/ppermute | solution.py:366
  26.2 1.4 %collective-permute-start.22 = (bf16[128,768]{1,0:T(8,128)(2,1)S(1)}, bf16[128,768]{1,0:T(8,128)(2,1)S(1)}, u32[]{:S(2)}, u32[]{:S(2)}) collective-permute-start(bf16[128,768]{1,0:T(8,128)(2,1)S(1)} %get-tuple-element.83), channel_id=1, source_target_pairs={{0,24},{4,28},{8,16},{12,20},{16,8},{20,12},{24,0},{28,4},{1,25},{... | collective-permute-start | bytes 589832 | tf_op jit(solution)/shard_map/ppermute | solution.py:366
  27.7 4.3 %collective-permute-done.20.refs_0_ = bf16[128,768]{1,0:T(8,128)(2,1)S(1)} collective-permute-done((bf16[128,768]{1,0:T(8,128)(2,1)S(1)}, bf16[128,768]{1,0:T(8,128)(2,1)S(1)}, u32[]{:S(2)}, u32[]{:S(2)}) %collective-permute-start.20) | collective-permute-done | bytes 196640 | tf_op jit(solution)/shard_map/ppermute | solution.py:366
  31.9 2.6 %collective-permute-done.21.refs_1_ = bf16[128,768]{1,0:T(8,128)(2,1)S(1)} collective-permute-done((bf16[128,768]{1,0:T(8,128)(2,1)S(1)}, bf16[128,768]{1,0:T(8,128)(2,1)S(1)}, u32[]{:S(2)}, u32[]{:S(2)}) %collective-permute-start.21) | collective-permute-done | bytes 196640 | tf_op jit(solution)/shard_map/ppermute | solution.py:366
  34.5 1.6 %collective-permute-done.22.refs_2_ = bf16[128,768]{1,0:T(8,128)(2,1)S(1)} collective-permute-done((bf16[128,768]{1,0:T(8,128)(2,1)S(1)}, bf16[128,768]{1,0:T(8,128)(2,1)S(1)}, u32[]{:S(2)}, u32[]{:S(2)}) %collective-permute-start.22) | collective-permute-done | bytes 196640 | tf_op jit(solution)/shard_map/ppermute | solution.py:366
  38.8 1.5 %collective-permute-start.10 = (bf16[64,768]{1,0:T(8,128)(2,1)S(1)}, bf16[64,768]{1,0:T(8,128)(2,1)S(1)}, u32[]{:S(2)}, u32[]{:S(2)}) collective-permute-start(bf16[64,768]{1,0:T(8,128)(2,1)S(1)} %get-tuple-element.74), channel_id=1, source_target_pairs={{0,16},{4,20},{8,24},{12,28},{16,0},{20,4},{24,8},{28,12},{1,17},{... | collective-permute-start | bytes 294920 | tf_op jit(solution)/shard_map/ppermute | solution.py:366
  40.3 1.2 %collective-permute-start.11 = (bf16[64,768]{1,0:T(8,128)(2,1)S(1)}, bf16[64,768]{1,0:T(8,128)(2,1)S(1)}, u32[]{:S(2)}, u32[]{:S(2)}) collective-permute-start(bf16[64,768]{1,0:T(8,128)(2,1)S(1)} %get-tuple-element.75), channel_id=1, source_target_pairs={{0,24},{4,28},{8,16},{12,20},{16,8},{20,12},{24,0},{28,4},{1,25},{... | collective-permute-start | bytes 294920 | tf_op jit(solution)/shard_map/ppermute | solution.py:366
  41.5 2.6 %collective-permute-start.24 = (bf16[64,768]{1,0:T(8,128)(2,1)S(1)}, bf16[64,768]{1,0:T(8,128)(2,1)S(1)}, u32[]{:S(2)}, u32[]{:S(2)}) collective-permute-start(bf16[64,768]{1,0:T(8,128)(2,1)S(1)} %add_convert_fusion.2), channel_id=1, source_target_pairs={{0,2},{1,3},{2,0},{3,1},{4,6},{5,7},{6,4},{7,5},{8,10},{9,11},{10,... | collective-permute-start | bytes 294920 | tf_op jit(solution)/shard_map/ppermute | solution.py:366
  44.2 1.7 %collective-permute-done.11 = bf16[64,768]{1,0:T(8,128)(2,1)S(1)} collective-permute-done((bf16[64,768]{1,0:T(8,128)(2,1)S(1)}, bf16[64,768]{1,0:T(8,128)(2,1)S(1)}, u32[]{:S(2)}, u32[]{:S(2)}) %collective-permute-start.11) | collective-permute-done | bytes 98336 | tf_op jit(solution)/shard_map/ppermute | solution.py:366
  45.9 2.6 %collective-permute-start.26 = (bf16[64,768]{1,0:T(8,128)(2,1)S(1)}, bf16[64,768]{1,0:T(8,128)(2,1)S(1)}, u32[]{:S(2)}, u32[]{:S(2)}) collective-permute-start(bf16[64,768]{1,0:T(8,128)(2,1)S(1)} %convert_add_fusion), channel_id=1, source_target_pairs={{0,2},{1,3},{2,0},{3,1},{4,6},{5,7},{6,4},{7,5},{8,10},{9,11},{10,... | collective-permute-start | bytes 294920 | tf_op jit(solution)/shard_map/ppermute | solution.py:366
  49.1 1.2 %collective-permute-start.13 = (bf16[64,1024]{1,0:T(8,128)(2,1)S(1)}, bf16[64,1024]{1,0:T(8,128)(2,1)S(1)}, u32[]{:S(2)}, u32[]{:S(2)}) collective-permute-start(bf16[64,1024]{1,0:T(8,128)(2,1)S(1)} %get-tuple-element.78), channel_id=1, source_target_pairs={{0,16},{4,20},{8,24},{12,28},{16,0},{20,4},{24,8},{28,12},{1,17},{... | collective-permute-start | bytes 393224 | tf_op jit(solution)/shard_map/ppermute | solution.py:366
  50.3 1.7 %collective-permute-start.14 = (bf16[64,1024]{1,0:T(8,128)(2,1)S(1)}, bf16[64,1024]{1,0:T(8,128)(2,1)S(1)}, u32[]{:S(2)}, u32[]{:S(2)}) collective-permute-start(bf16[64,1024]{1,0:T(8,128)(2,1)S(1)} %get-tuple-element.79), channel_id=1, source_target_pairs={{0,24},{4,28},{8,16},{12,20},{16,8},{20,12},{24,0},{28,4},{1,25},{... | collective-permute-start | bytes 393224 | tf_op jit(solution)/shard_map/ppermute | solution.py:366
  52.1 1.6 %collective-permute-start.25 = (bf16[64,768]{1,0:T(8,128)(2,1)S(1)}, bf16[64,768]{1,0:T(8,128)(2,1)S(1)}, u32[]{:S(2)}, u32[]{:S(2)}) collective-permute-start(bf16[64,768]{1,0:T(8,128)(2,1)S(1)} %add_convert_fusion.1.refs_0_), channel_id=1, source_target_pairs={{0,1},{1,0},{2,3},{3,2},{4,5},{5,4},{6,7},{7,6},{8,9},{9,8},{10,11... | collective-permute-start | bytes 294920 | tf_op jit(solution)/shard_map/ppermute | solution.py:366
  54.3 1.8 %collective-permute-done.14.refs_3_ = bf16[64,1024]{1,0:T(8,128)(2,1)S(1)} collective-permute-done((bf16[64,1024]{1,0:T(8,128)(2,1)S(1)}, bf16[64,1024]{1,0:T(8,128)(2,1)S(1)}, u32[]{:S(2)}, u32[]{:S(2)}) %collective-permute-start.14) | collective-permute-done | bytes 131104 | tf_op jit(solution)/shard_map/ppermute | solution.py:366
  56.7 1.6 %collective-permute-start.27 = (bf16[64,768]{1,0:T(8,128)(2,1)S(1)}, bf16[64,768]{1,0:T(8,128)(2,1)S(1)}, u32[]{:S(2)}, u32[]{:S(2)}) collective-permute-start(bf16[64,768]{1,0:T(8,128)(2,1)S(1)} %add_convert_fusion.refs_2_), channel_id=1, source_target_pairs={{0,1},{1,0},{2,3},{3,2},{4,5},{5,4},{6,7},{7,6},{8,9},{9,8},{10,11... | collective-permute-start | bytes 294920 | tf_op jit(solution)/shard_map/ppermute | solution.py:366
  58.3 3.2 %collective-permute-done.27.refs_3_ = bf16[64,768]{1,0:T(8,128)(2,1)S(1)} collective-permute-done((bf16[64,768]{1,0:T(8,128)(2,1)S(1)}, bf16[64,768]{1,0:T(8,128)(2,1)S(1)}, u32[]{:S(2)}, u32[]{:S(2)}) %collective-permute-start.27) | collective-permute-done | bytes 98336 | tf_op jit(solution)/shard_map/ppermute | solution.py:366
  62.5 1.2 %shard_map.82 = bf16[128,1024]{1,0:T(8,128)(2,1)} custom-call(s32[8,128]{1,0:T(8,128)S(1)} %bitcast.10, bf16[64,1024]{1,0:T(8,128)(2,1)S(1)} %get-tuple-element.76.refs_0_, bf16[64,1024]{1,0:T(8,128)(2,1)S(1)} %collective-permute-done.12.refs_1_, bf16[64,1024]{1,0:T(8,128)(2,1)S(1)} %collective-permute-done.13.refs_2_, ...), custom_call_target="tpu_custom_call" | custom-call | flops 67108864 | bytes 1314816 | tf_op jit(solution)/shard_map/pallas_call | solution.py:121
  (58 shorter events, 14.7 us)
Async XLA Ops:
  2.8 8.8 %collective-permute-start = (bf16[64,1024]{1,0:T(8,128)(2,1)S(1)}, bf16[64,1024]{1,0:T(8,128)(2,1)S(1)}, u32[]{:S(2)}, u32[]{:S(2)}) collective-permute-start(bf16[64,1024]{1,0:T(8,128)(2,1)S(1)} %get-tuple-element.46), channel_id=1, source_target_pairs={{0,8},{4,12},{8,0},{12,4},{16,24},{20,28},{24,16},{28,20},{1,9},{5... | collective-permute-start | bytes 393224 | tf_op jit(solution)/shard_map/ppermute | solution.py:366
  5.8 7.8 %collective-permute-start.1 = (bf16[64,1024]{1,0:T(8,128)(2,1)S(1)}, bf16[64,1024]{1,0:T(8,128)(2,1)S(1)}, u32[]{:S(2)}, u32[]{:S(2)}) collective-permute-start(bf16[64,1024]{1,0:T(8,128)(2,1)S(1)} %get-tuple-element.47), channel_id=1, source_target_pairs={{0,16},{4,20},{8,24},{12,28},{16,0},{20,4},{24,8},{28,12},{1,17},{... | collective-permute-start | bytes 393224 | tf_op jit(solution)/shard_map/ppermute | solution.py:366
  7.3 6.3 %collective-permute-start.2 = (bf16[64,1024]{1,0:T(8,128)(2,1)S(1)}, bf16[64,1024]{1,0:T(8,128)(2,1)S(1)}, u32[]{:S(2)}, u32[]{:S(2)}) collective-permute-start(bf16[64,1024]{1,0:T(8,128)(2,1)S(1)} %get-tuple-element.48), channel_id=1, source_target_pairs={{0,24},{4,28},{8,16},{12,20},{16,8},{20,12},{24,0},{28,4},{1,25},{... | collective-permute-start | bytes 393224 | tf_op jit(solution)/shard_map/ppermute | solution.py:366
  19.3 1.7 %collective-permute-start.7 = (bf16[256,768]{1,0:T(8,128)(2,1)S(1)}, bf16[256,768]{1,0:T(8,128)(2,1)S(1)}, u32[]{:S(2)}, u32[]{:S(2)}) collective-permute-start(bf16[256,768]{1,0:T(8,128)(2,1)S(1)} %get-tuple-element.63.refs_1_.d_own_ref), channel_id=1, source_target_pairs={{0,4},{4,0},{8,12},{12,8},{16,20},{20,16},{24,28},{28,24},{1,5},{5... | collective-permute-start | bytes 1179656 | tf_op jit(solution)/shard_map/ppermute | solution.py:366
  19.6 3.9 %collective-permute-start.19 = (bf16[256,768]{1,0:T(8,128)(2,1)S(1)}, bf16[256,768]{1,0:T(8,128)(2,1)S(1)}, u32[]{:S(2)}, u32[]{:S(2)}) collective-permute-start(bf16[256,768]{1,0:T(8,128)(2,1)S(1)} %get-tuple-element.62.refs_0_.d_own_ref), channel_id=1, source_target_pairs={{0,4},{4,0},{8,12},{12,8},{16,20},{20,16},{24,28},{28,24},{1,5},{5... | collective-permute-start | bytes 1179656 | tf_op jit(solution)/shard_map/ppermute | solution.py:366
  21.8 16.0 %collective-permute-start.8 = (bf16[256,768]{1,0:T(8,128)(2,1)S(1)}, bf16[256,768]{1,0:T(8,128)(2,1)S(1)}, u32[]{:S(2)}, u32[]{:S(2)}) collective-permute-start(bf16[256,768]{1,0:T(8,128)(2,1)S(1)} %get-tuple-element.71), channel_id=1, source_target_pairs={{0,1},{1,0},{2,3},{3,2},{4,5},{5,4},{6,7},{7,6},{8,9},{9,8},{10,11... | collective-permute-start | bytes 1179656 | tf_op jit(solution)/shard_map/ppermute | solution.py:366
  24.1 7.8 %collective-permute-start.20 = (bf16[128,768]{1,0:T(8,128)(2,1)S(1)}, bf16[128,768]{1,0:T(8,128)(2,1)S(1)}, u32[]{:S(2)}, u32[]{:S(2)}) collective-permute-start(bf16[128,768]{1,0:T(8,128)(2,1)S(1)} %get-tuple-element.81), channel_id=1, source_target_pairs={{0,8},{4,12},{8,0},{12,4},{16,24},{20,28},{24,16},{28,20},{1,9},{5... | collective-permute-start | bytes 589832 | tf_op jit(solution)/shard_map/ppermute | solution.py:366
  25.4 9.1 %collective-permute-start.21 = (bf16[128,768]{1,0:T(8,128)(2,1)S(1)}, bf16[128,768]{1,0:T(8,128)(2,1)S(1)}, u32[]{:S(2)}, u32[]{:S(2)}) collective-permute-start(bf16[128,768]{1,0:T(8,128)(2,1)S(1)} %get-tuple-element.82), channel_id=1, source_target_pairs={{0,16},{4,20},{8,24},{12,28},{16,0},{20,4},{24,8},{28,12},{1,17},{... | collective-permute-start | bytes 589832 | tf_op jit(solution)/shard_map/ppermute | solution.py:366
  26.2 10.0 %collective-permute-start.22 = (bf16[128,768]{1,0:T(8,128)(2,1)S(1)}, bf16[128,768]{1,0:T(8,128)(2,1)S(1)}, u32[]{:S(2)}, u32[]{:S(2)}) collective-permute-start(bf16[128,768]{1,0:T(8,128)(2,1)S(1)} %get-tuple-element.83), channel_id=1, source_target_pairs={{0,24},{4,28},{8,16},{12,20},{16,8},{20,12},{24,0},{28,4},{1,25},{... | collective-permute-start | bytes 589832 | tf_op jit(solution)/shard_map/ppermute | solution.py:366
  36.3 5.2 %collective-permute-start.23 = (bf16[64,768]{1,0:T(8,128)(2,1)S(1)}, bf16[64,768]{1,0:T(8,128)(2,1)S(1)}, u32[]{:S(2)}, u32[]{:S(2)}) collective-permute-start(bf16[64,768]{1,0:T(8,128)(2,1)S(1)} %get-tuple-element.85), channel_id=1, source_target_pairs={{0,1},{1,0},{2,3},{3,2},{4,5},{5,4},{6,7},{7,6},{8,9},{9,8},{10,11... | collective-permute-start | bytes 294920 | tf_op jit(solution)/shard_map/ppermute | solution.py:366
  38.0 6.2 %collective-permute-start.9 = (bf16[64,768]{1,0:T(8,128)(2,1)S(1)}, bf16[64,768]{1,0:T(8,128)(2,1)S(1)}, u32[]{:S(2)}, u32[]{:S(2)}) collective-permute-start(bf16[64,768]{1,0:T(8,128)(2,1)S(1)} %get-tuple-element.73), channel_id=1, source_target_pairs={{0,8},{4,12},{8,0},{12,4},{16,24},{20,28},{24,16},{28,20},{1,9},{5... | collective-permute-start | bytes 294920 | tf_op jit(solution)/shard_map/ppermute | solution.py:366
  38.8 5.4 %collective-permute-start.10 = (bf16[64,768]{1,0:T(8,128)(2,1)S(1)}, bf16[64,768]{1,0:T(8,128)(2,1)S(1)}, u32[]{:S(2)}, u32[]{:S(2)}) collective-permute-start(bf16[64,768]{1,0:T(8,128)(2,1)S(1)} %get-tuple-element.74), channel_id=1, source_target_pairs={{0,16},{4,20},{8,24},{12,28},{16,0},{20,4},{24,8},{28,12},{1,17},{... | collective-permute-start | bytes 294920 | tf_op jit(solution)/shard_map/ppermute | solution.py:366
  40.3 5.5 %collective-permute-start.11 = (bf16[64,768]{1,0:T(8,128)(2,1)S(1)}, bf16[64,768]{1,0:T(8,128)(2,1)S(1)}, u32[]{:S(2)}, u32[]{:S(2)}) collective-permute-start(bf16[64,768]{1,0:T(8,128)(2,1)S(1)} %get-tuple-element.75), channel_id=1, source_target_pairs={{0,24},{4,28},{8,16},{12,20},{16,8},{20,12},{24,0},{28,4},{1,25},{... | collective-permute-start | bytes 294920 | tf_op jit(solution)/shard_map/ppermute | solution.py:366
  41.5 10.5 %collective-permute-start.24 = (bf16[64,768]{1,0:T(8,128)(2,1)S(1)}, bf16[64,768]{1,0:T(8,128)(2,1)S(1)}, u32[]{:S(2)}, u32[]{:S(2)}) collective-permute-start(bf16[64,768]{1,0:T(8,128)(2,1)S(1)} %add_convert_fusion.2), channel_id=1, source_target_pairs={{0,2},{1,3},{2,0},{3,1},{4,6},{5,7},{6,4},{7,5},{8,10},{9,11},{10,... | collective-permute-start | bytes 294920 | tf_op jit(solution)/shard_map/ppermute | solution.py:366
  45.9 7.8 %collective-permute-start.26 = (bf16[64,768]{1,0:T(8,128)(2,1)S(1)}, bf16[64,768]{1,0:T(8,128)(2,1)S(1)}, u32[]{:S(2)}, u32[]{:S(2)}) collective-permute-start(bf16[64,768]{1,0:T(8,128)(2,1)S(1)} %convert_add_fusion), channel_id=1, source_target_pairs={{0,2},{1,3},{2,0},{3,1},{4,6},{5,7},{6,4},{7,5},{8,10},{9,11},{10,... | collective-permute-start | bytes 294920 | tf_op jit(solution)/shard_map/ppermute | solution.py:366
  48.5 5.2 %collective-permute-start.12 = (bf16[64,1024]{1,0:T(8,128)(2,1)S(1)}, bf16[64,1024]{1,0:T(8,128)(2,1)S(1)}, u32[]{:S(2)}, u32[]{:S(2)}) collective-permute-start(bf16[64,1024]{1,0:T(8,128)(2,1)S(1)} %get-tuple-element.77), channel_id=1, source_target_pairs={{0,8},{4,12},{8,0},{12,4},{16,24},{20,28},{24,16},{28,20},{1,9},{5... | collective-permute-start | bytes 393224 | tf_op jit(solution)/shard_map/ppermute | solution.py:366
  49.1 5.3 %collective-permute-start.13 = (bf16[64,1024]{1,0:T(8,128)(2,1)S(1)}, bf16[64,1024]{1,0:T(8,128)(2,1)S(1)}, u32[]{:S(2)}, u32[]{:S(2)}) collective-permute-start(bf16[64,1024]{1,0:T(8,128)(2,1)S(1)} %get-tuple-element.78), channel_id=1, source_target_pairs={{0,16},{4,20},{8,24},{12,28},{16,0},{20,4},{24,8},{28,12},{1,17},{... | collective-permute-start | bytes 393224 | tf_op jit(solution)/shard_map/ppermute | solution.py:366
  50.3 5.9 %collective-permute-start.14 = (bf16[64,1024]{1,0:T(8,128)(2,1)S(1)}, bf16[64,1024]{1,0:T(8,128)(2,1)S(1)}, u32[]{:S(2)}, u32[]{:S(2)}) collective-permute-start(bf16[64,1024]{1,0:T(8,128)(2,1)S(1)} %get-tuple-element.79), channel_id=1, source_target_pairs={{0,24},{4,28},{8,16},{12,20},{16,8},{20,12},{24,0},{28,4},{1,25},{... | collective-permute-start | bytes 393224 | tf_op jit(solution)/shard_map/ppermute | solution.py:366
  52.1 4.7 %collective-permute-start.25 = (bf16[64,768]{1,0:T(8,128)(2,1)S(1)}, bf16[64,768]{1,0:T(8,128)(2,1)S(1)}, u32[]{:S(2)}, u32[]{:S(2)}) collective-permute-start(bf16[64,768]{1,0:T(8,128)(2,1)S(1)} %add_convert_fusion.1.refs_0_), channel_id=1, source_target_pairs={{0,1},{1,0},{2,3},{3,2},{4,5},{5,4},{6,7},{7,6},{8,9},{9,8},{10,11... | collective-permute-start | bytes 294920 | tf_op jit(solution)/shard_map/ppermute | solution.py:366
  53.7 8.7 %collective-permute-start.15 = (bf16[64,1024]{1,0:T(8,128)(2,1)S(1)}, bf16[64,1024]{1,0:T(8,128)(2,1)S(1)}, u32[]{:S(2)}, u32[]{:S(2)}) collective-permute-start(bf16[64,1024]{1,0:T(8,128)(2,1)S(1)} %get-tuple-element.76.refs_0_), channel_id=1, source_target_pairs={{0,4},{4,0},{8,12},{12,8},{16,20},{20,16},{24,28},{28,24},{1,5},{5... | collective-permute-start | bytes 393224 | tf_op jit(solution)/shard_map/ppermute | solution.py:366
  53.7 8.7 %collective-permute-start.16 = (bf16[64,1024]{1,0:T(8,128)(2,1)S(1)}, bf16[64,1024]{1,0:T(8,128)(2,1)S(1)}, u32[]{:S(2)}, u32[]{:S(2)}) collective-permute-start(bf16[64,1024]{1,0:T(8,128)(2,1)S(1)} %collective-permute-done.12.refs_1_), channel_id=1, source_target_pairs={{0,4},{4,0},{8,12},{12,8},{16,20},{20,16},{24,28},{28,24},{1,5},{5... | collective-permute-start | bytes 393224 | tf_op jit(solution)/shard_map/ppermute | solution.py:366
  54.3 8.1 %collective-permute-start.17 = (bf16[64,1024]{1,0:T(8,128)(2,1)S(1)}, bf16[64,1024]{1,0:T(8,128)(2,1)S(1)}, u32[]{:S(2)}, u32[]{:S(2)}) collective-permute-start(bf16[64,1024]{1,0:T(8,128)(2,1)S(1)} %collective-permute-done.13.refs_2_), channel_id=1, source_target_pairs={{0,4},{4,0},{8,12},{12,8},{16,20},{20,16},{24,28},{28,24},{1,5},{5... | collective-permute-start | bytes 393224 | tf_op jit(solution)/shard_map/ppermute | solution.py:366
  56.2 6.3 %collective-permute-start.18 = (bf16[64,1024]{1,0:T(8,128)(2,1)S(1)}, bf16[64,1024]{1,0:T(8,128)(2,1)S(1)}, u32[]{:S(2)}, u32[]{:S(2)}) collective-permute-start(bf16[64,1024]{1,0:T(8,128)(2,1)S(1)} %collective-permute-done.14.refs_3_), channel_id=1, source_target_pairs={{0,4},{4,0},{8,12},{12,8},{16,20},{20,16},{24,28},{28,24},{1,5},{5... | collective-permute-start | bytes 393224 | tf_op jit(solution)/shard_map/ppermute | solution.py:366
  56.7 4.7 %collective-permute-start.27 = (bf16[64,768]{1,0:T(8,128)(2,1)S(1)}, bf16[64,768]{1,0:T(8,128)(2,1)S(1)}, u32[]{:S(2)}, u32[]{:S(2)}) collective-permute-start(bf16[64,768]{1,0:T(8,128)(2,1)S(1)} %add_convert_fusion.refs_2_), channel_id=1, source_target_pairs={{0,1},{1,0},{2,3},{3,2},{4,5},{5,4},{6,7},{7,6},{8,9},{9,8},{10,11... | collective-permute-start | bytes 294920 | tf_op jit(solution)/shard_map/ppermute | solution.py:366
  (10 other events, 37.0 us)

commit v3 on v2

--- a/solution.py
+++ b/solution.py
@@ -116,17 +116,18 @@
 
 
 def call(kernel, outs, operands, flops, scratch=(), specs=None):
+    specs = specs or [VMEM] * len(operands)
     nbytes = sum(a.size * a.dtype.itemsize for a in operands)
     nbytes += sum(o.size * o.dtype.itemsize for o in outs)
     return pl.pallas_call(
         kernel,
         out_shape=outs,
-        in_specs=specs or [VMEM] * len(operands),
+        in_specs=specs,
         out_specs=[VMEM] * len(outs),
         scratch_shapes=list(scratch),
         compiler_params=pltpu.CompilerParams(vmem_limit_bytes=VMEM_LIMIT),
         cost_estimate=pl.CostEstimate(flops=flops, bytes_accessed=nbytes, transcendentals=0),
-    )(*operands)
+    )(*[pltpu.with_memory_space_constraint(a, pltpu.HBM) if s is HBM else a for a, s in zip(operands, specs)])
 
 
 def shaped(shape, dtype):
@@ -385,8 +386,12 @@
     pair = shaped((2 * capacity, width), BF16)
     users_scratch = pltpu.VMEM((peers, rows), jnp.int32)
 
+    def farthest_first(arrays):
+        sent = [exchange(arrays[i], bits=2 * (i + 1)) for i in reversed(range(chips - 1))]
+        return sent[::-1]
+
     def to_sources(pairs):
-        return [pairs[0]] + [exchange(pairs[i], bits=2 * i) for i in range(1, chips)]
+        return [pairs[0]] + farthest_first(pairs[1:])
 
     def to_siblings(pairs):
         return [exchange(a, bits=1) for a in pairs]
@@ -441,8 +446,16 @@
         flops,
         [pltpu.VMEM((block, size), F32)],
     )
-    from_plane = [exchange(other, bits=2 * (i + 1)) for i, other in enumerate(others)]
+    from_plane = farthest_first(others)
     from_neighbour = swap_replicas(send_second, bits=1)
+    own_second, *others_second = call(
+        sum_blocks_kernel,
+        [shaped((half, size), F32)] + [shaped((half, size), BF16)] * (chips - 1),
+        [keep_second, from_neighbour],
+        chips * half * size,
+    )
+    second_plane = farthest_first(others_second)
+    from_plane, own_second = lax.optimization_barrier((from_plane, own_second))
     keep_first, send_first = call(
         sum_halves_kernel,
         [shaped((half, size), F32), shaped((half, size), BF16)],
@@ -450,23 +463,17 @@
         chips * block * size,
         [pltpu.VMEM((block, size), F32)],
     )
-    own_second, *others_second = call(
-        sum_blocks_kernel,
-        [shaped((half, size), F32)] + [shaped((half, size), BF16)] * (chips - 1),
-        [keep_second, from_neighbour],
-        chips * half * size,
-    )
     first = keep_first + swap_replicas(send_first, bits=1).astype(F32)
     second = own_second
-    for i, other in enumerate(others_second):
-        second = second + exchange(other, bits=2 * (i + 1)).astype(F32)
+    for other in second_plane:
+        second = second + other.astype(F32)
     d_slots = call(
         functools.partial(token_kernel, features),
         [pair] * chips,
         [w_held, d_first, d_second],
         2 * slots * width * columns,
     )
-    d_slots, second = lax.optimization_barrier((d_slots, second))
+    d_slots, _, _ = lax.optimization_barrier((d_slots, first.astype(BF16), second.astype(BF16)))
     near = to_sources(d_slots)
     far = to_siblings(near)
     (grad_tokens,) = call(
@@ -485,6 +492,7 @@
             held = (held.astype(F32) + swap_replicas(held, bits=bits).astype(F32)).astype(BF16)
             bits *= 2
         joined += [held, swap_replicas(held, bits=1)]
+    joined[-1], grad_tokens = lax.optimization_barrier((joined[-1], grad_tokens))
     (grad_weight,) = call(
         functools.partial(join_kernel, features),
         [shaped((block, columns), F32)],

time: 63.9 us -> 59.6 us (0.933)
  local copies, waits for them, and re-layouts: 5.16 us -> 0.68 us
  Pallas kernels: 9.59 us -> 12.4 us
  starting transfers between devices: 27.8 us -> 26.3 us
  waiting for transfers between devices: 20.1 us -> 19.1 us
    unnamed x12 -> x2, local copies, waits for them, and re-layouts: 5.16 us -> 0.68 us
    pallas_call x10, Pallas kernels: 9.59 us -> 12.4 us  [call(): pl.pallas_call(kernel, out_shape=outs, in_specs=specs, out_specs=[VMEM] *...]
    ppermute x28, starting transfers between devices: 27.8 us -> 26.3 us  [swap(): return lax.ppermute(array, axis, [(i, i ^ bits) for i in range(size)])]
    ppermute x28, waiting for transfers between devices: 20.1 us -> 19.1 us  [swap(): return lax.ppermute(array, axis, [(i, i ^ bits) for i in range(size)])]
  transfers between devices with their start and end apart: 28 -> 28, of which waited for: 14 -> 14; matrix products, arithmetic and copies ran while one was open for 0% -> 0% of each run, Pallas kernels for 7% -> 11%
where the time goes in v3:
time: 59.6 us; the launch traced here: 59.4 us
  starting transfers between devices  26.3 us (44%)
  waiting for transfers between devices  19.1 us (32%)
  Pallas kernels  12.4 us (21%)
  between operations  0.77 us (1%)
  local copies, waits for them, and re-layouts  0.68 us (1%)
    ppermute x28, starting transfers between devices, swap(): return lax.ppermute(array, axis, [(i, i ^ bits) for i in range(size)])  26.3 us
    ppermute x28, waiting for transfers between devices, swap(): return lax.ppermute(array, axis, [(i, i ^ bits) for i in range(size)])  19.1 us
    pallas_call x10, Pallas kernels, call(): pl.pallas_call(kernel, out_shape=outs, in_specs=specs, out_specs=[VMEM] *...  12.4 us
  transfers between devices with their start and end apart: 28, of which 14 were waited for; matrix products, arithmetic and copies ran while one was open for 0% of the time, Pallas kernels for 11%

profile of v3, /device:TPU:0, one launch (start us, length us, event | category | flops | bytes accessed | tf_op | source)
XLA Modules:
  0.0 59.4 jit_solution(7510875149518947342)
XLA Ops:
  0.6 1.3 %shard_map.76 = (bf16[64,1024]{1,0:T(8,128)(2,1)S(1)}, bf16[64,1024]{1,0:T(8,128)(2,1)S(1)}, bf16[64,1024]{1,0:T(8,128)(2,1)S(1)}, bf16[64,1024]{1,0:T(8,128)(2,1)S(1)}) custom-call(s32[8,128]{1,0:T(8,128)} %bitcast.11, bf16[128,1024]{1,0:T(8,128)(2,1)} %bitcast.10), custom_call_target="tpu_custom_call" | custom-call | flops 67108864 | bytes 790528 | tf_op jit(solution)/shard_map/pallas_call | solution.py:122
  1.9 3.0 %collective-permute-start = (bf16[64,1024]{1,0:T(8,128)(2,1)S(1)}, bf16[64,1024]{1,0:T(8,128)(2,1)S(1)}, u32[]{:S(2)}, u32[]{:S(2)}) collective-permute-start(bf16[64,1024]{1,0:T(8,128)(2,1)S(1)} %get-tuple-element.51), channel_id=1, source_target_pairs={{0,8},{4,12},{8,0},{12,4},{16,24},{20,28},{24,16},{28,20},{1,9},{5... | collective-permute-start | bytes 393224 | tf_op jit(solution)/shard_map/ppermute | solution.py:367
  4.9 1.5 %collective-permute-start.1 = (bf16[64,1024]{1,0:T(8,128)(2,1)S(1)}, bf16[64,1024]{1,0:T(8,128)(2,1)S(1)}, u32[]{:S(2)}, u32[]{:S(2)}) collective-permute-start(bf16[64,1024]{1,0:T(8,128)(2,1)S(1)} %get-tuple-element.52), channel_id=1, source_target_pairs={{0,16},{4,20},{8,24},{12,28},{16,0},{20,4},{24,8},{28,12},{1,17},{... | collective-permute-start | bytes 393224 | tf_op jit(solution)/shard_map/ppermute | solution.py:367
  7.1 2.0 %shard_map.77 = (bf16[1024,1536]{1,0:T(8,128)(2,1)S(1)}, f32[256,512]{1,0:T(8,128)S(1)}, f32[256,128]{1,0:T(8,128)S(1)}, f32[8,256]{1,0:T(8,128)S(1)}) custom-call(s32[8,128]{1,0:T(8,128)} %bitcast.12, f32[1,512]{1,0:T(1,128)S(1)} %bitcast.6, bf16[1024,1536]{1,0:T(8,128)(2,1)} %w_hbm.1, bf16[256,512]{1,0:T(8,128)(2,1)} %bitcast.8), custom_call_target="tpu_custom_call" | custom-call | flops 16777216 | bytes 7223296 | tf_op jit(solution)/shard_map/pallas_call | solution.py:122
  9.2 3.5 %collective-permute-done.1.refs_2_ = bf16[64,1024]{1,0:T(8,128)(2,1)S(1)} collective-permute-done((bf16[64,1024]{1,0:T(8,128)(2,1)S(1)}, bf16[64,1024]{1,0:T(8,128)(2,1)S(1)}, u32[]{:S(2)}, u32[]{:S(2)}) %collective-permute-start.1) | collective-permute-done | bytes 131104 | tf_op jit(solution)/shard_map/ppermute | solution.py:367
  14.8 3.7 %shard_map.78 = (bf16[256,512]{1,0:T(8,128)(2,1)}, bf16[256,768]{1,0:T(8,128)(2,1)S(1)}, bf16[256,768]{1,0:T(8,128)(2,1)S(1)}, bf16[256,512]{1,0:T(8,128)(2,1)S(1)}, bf16[256,512]{1,0:T(8,128)(2,1)S(1)}) custom-call(f32[1,512]{1,0:T(1,128)S(1)} %bitcast.7, bf16[1024,1536]{1,0:T(8,128)(2,1)S(1)} %get-tuple-element.58.w_ref, ...), custom_call_target="tpu_custom_call" | custom-call | flops 1275068416 | bytes 6432768 | tf_op jit(solution)/shard_map/pallas_call | solution.py:122
  18.9 1.2 %collective-permute-done.11.d_sib_ref = bf16[256,768]{1,0:T(8,128)(2,1)S(1)} collective-permute-done((bf16[256,768]{1,0:T(8,128)(2,1)S(1)}, bf16[256,768]{1,0:T(8,128)(2,1)S(1)}, u32[]{:S(2)}, u32[]{:S(2)}) %collective-permute-start.11) | collective-permute-done | bytes 393248 | tf_op jit(solution)/shard_map/ppermute | solution.py:367
  21.0 1.7 %collective-permute-start.12 = (bf16[256,768]{1,0:T(8,128)(2,1)S(1)}, bf16[256,768]{1,0:T(8,128)(2,1)S(1)}, u32[]{:S(2)}, u32[]{:S(2)}) collective-permute-start(bf16[256,768]{1,0:T(8,128)(2,1)S(1)} %get-tuple-element.75), channel_id=1, source_target_pairs={{0,1},{1,0},{2,3},{3,2},{4,5},{5,4},{6,7},{7,6},{8,9},{9,8},{10,11... | collective-permute-start | bytes 1179656 | tf_op jit(solution)/shard_map/ppermute | solution.py:367
  23.3 1.3 %collective-permute-start.8 = (bf16[128,768]{1,0:T(8,128)(2,1)S(1)}, bf16[128,768]{1,0:T(8,128)(2,1)S(1)}, u32[]{:S(2)}, u32[]{:S(2)}) collective-permute-start(bf16[128,768]{1,0:T(8,128)(2,1)S(1)} %get-tuple-element.70), channel_id=1, source_target_pairs={{0,8},{4,12},{8,0},{12,4},{16,24},{20,28},{24,16},{28,20},{1,9},{5... | collective-permute-start | bytes 589832 | tf_op jit(solution)/shard_map/ppermute | solution.py:367
  25.4 1.4 %collective-permute-start.10 = (bf16[128,768]{1,0:T(8,128)(2,1)S(1)}, bf16[128,768]{1,0:T(8,128)(2,1)S(1)}, u32[]{:S(2)}, u32[]{:S(2)}) collective-permute-start(bf16[128,768]{1,0:T(8,128)(2,1)S(1)} %get-tuple-element.72), channel_id=1, source_target_pairs={{0,24},{4,28},{8,16},{12,20},{16,8},{20,12},{24,0},{28,4},{1,25},{... | collective-permute-start | bytes 589832 | tf_op jit(solution)/shard_map/ppermute | solution.py:367
  26.8 5.6 %collective-permute-done.12.in_ref = bf16[256,768]{1,0:T(8,128)(2,1)S(1)} collective-permute-done((bf16[256,768]{1,0:T(8,128)(2,1)S(1)}, bf16[256,768]{1,0:T(8,128)(2,1)S(1)}, u32[]{:S(2)}, u32[]{:S(2)}) %collective-permute-start.12) | collective-permute-done | bytes 393248 | tf_op jit(solution)/shard_map/ppermute | solution.py:367
  32.5 1.3 %collective-permute-start.13 = (bf16[64,768]{1,0:T(8,128)(2,1)S(1)}, bf16[64,768]{1,0:T(8,128)(2,1)S(1)}, u32[]{:S(2)}, u32[]{:S(2)}) collective-permute-start(bf16[64,768]{1,0:T(8,128)(2,1)S(1)} %get-tuple-element.78), channel_id=1, source_target_pairs={{0,8},{4,12},{8,0},{12,4},{16,24},{20,28},{24,16},{28,20},{1,9},{5... | collective-permute-start | bytes 294920 | tf_op jit(solution)/shard_map/ppermute | solution.py:367
  34.6 1.4 %collective-permute-start.15 = (bf16[64,768]{1,0:T(8,128)(2,1)S(1)}, bf16[64,768]{1,0:T(8,128)(2,1)S(1)}, u32[]{:S(2)}, u32[]{:S(2)}) collective-permute-start(bf16[64,768]{1,0:T(8,128)(2,1)S(1)} %get-tuple-element.80), channel_id=1, source_target_pairs={{0,24},{4,28},{8,16},{12,20},{16,8},{20,12},{24,0},{28,4},{1,25},{... | collective-permute-start | bytes 294920 | tf_op jit(solution)/shard_map/ppermute | solution.py:367
  37.2 1.6 %collective-permute-start.18 = (bf16[64,768]{1,0:T(8,128)(2,1)S(1)}, bf16[64,768]{1,0:T(8,128)(2,1)S(1)}, u32[]{:S(2)}, u32[]{:S(2)}) collective-permute-start(bf16[64,768]{1,0:T(8,128)(2,1)S(1)} %get-tuple-element.90), channel_id=1, source_target_pairs={{0,1},{1,0},{2,3},{3,2},{4,5},{5,4},{6,7},{7,6},{8,9},{9,8},{10,11... | collective-permute-start | bytes 294920 | tf_op jit(solution)/shard_map/ppermute | solution.py:367
  38.9 1.5 %collective-permute-done.14 = bf16[64,768]{1,0:T(8,128)(2,1)S(1)} collective-permute-done((bf16[64,768]{1,0:T(8,128)(2,1)S(1)}, bf16[64,768]{1,0:T(8,128)(2,1)S(1)}, u32[]{:S(2)}, u32[]{:S(2)}) %collective-permute-start.14) | collective-permute-done | bytes 98336 | tf_op jit(solution)/shard_map/ppermute | solution.py:367
  40.4 2.6 %collective-permute-start.16 = (bf16[64,768]{1,0:T(8,128)(2,1)S(1)}, bf16[64,768]{1,0:T(8,128)(2,1)S(1)}, u32[]{:S(2)}, u32[]{:S(2)}) collective-permute-start(bf16[64,768]{1,0:T(8,128)(2,1)S(1)} %add_convert_fusion.3), channel_id=1, source_target_pairs={{0,2},{1,3},{2,0},{3,1},{4,6},{5,7},{6,4},{7,5},{8,10},{9,11},{10,... | collective-permute-start | bytes 294920 | tf_op jit(solution)/shard_map/ppermute | solution.py:367
  43.1 1.9 %collective-permute-start.26 = (bf16[64,768]{1,0:T(8,128)(2,1)S(1)}, bf16[64,768]{1,0:T(8,128)(2,1)S(1)}, u32[]{:S(2)}, u32[]{:S(2)}) collective-permute-start(bf16[64,768]{1,0:T(8,128)(2,1)S(1)} %add_convert_fusion.1), channel_id=1, source_target_pairs={{0,2},{1,3},{2,0},{3,1},{4,6},{5,7},{6,4},{7,5},{8,10},{9,11},{10,... | collective-permute-start | bytes 294920 | tf_op jit(solution)/shard_map/ppermute | solution.py:367
  44.9 1.8 %collective-permute-start.19 = (bf16[64,1024]{1,0:T(8,128)(2,1)S(1)}, bf16[64,1024]{1,0:T(8,128)(2,1)S(1)}, u32[]{:S(2)}, u32[]{:S(2)}) collective-permute-start(bf16[64,1024]{1,0:T(8,128)(2,1)S(1)} %get-tuple-element.92), channel_id=1, source_target_pairs={{0,8},{4,12},{8,0},{12,4},{16,24},{20,28},{24,16},{28,20},{1,9},{5... | collective-permute-start | bytes 393224 | tf_op jit(solution)/shard_map/ppermute | solution.py:367
  47.2 1.2 %collective-permute-start.21 = (bf16[64,1024]{1,0:T(8,128)(2,1)S(1)}, bf16[64,1024]{1,0:T(8,128)(2,1)S(1)}, u32[]{:S(2)}, u32[]{:S(2)}) collective-permute-start(bf16[64,1024]{1,0:T(8,128)(2,1)S(1)} %get-tuple-element.94), channel_id=1, source_target_pairs={{0,24},{4,28},{8,16},{12,20},{16,8},{20,12},{24,0},{28,4},{1,25},{... | collective-permute-start | bytes 393224 | tf_op jit(solution)/shard_map/ppermute | solution.py:367
  48.4 1.8 %collective-permute-done.16 = bf16[64,768]{1,0:T(8,128)(2,1)S(1)} collective-permute-done((bf16[64,768]{1,0:T(8,128)(2,1)S(1)}, bf16[64,768]{1,0:T(8,128)(2,1)S(1)}, u32[]{:S(2)}, u32[]{:S(2)}) %collective-permute-start.16) | collective-permute-done | bytes 98336 | tf_op jit(solution)/shard_map/ppermute | solution.py:367
  50.3 1.0 %collective-permute-done.26 = bf16[64,768]{1,0:T(8,128)(2,1)S(1)} collective-permute-done((bf16[64,768]{1,0:T(8,128)(2,1)S(1)}, bf16[64,768]{1,0:T(8,128)(2,1)S(1)}, u32[]{:S(2)}, u32[]{:S(2)}) %collective-permute-start.26) | collective-permute-done | bytes 98336 | tf_op jit(solution)/shard_map/ppermute | solution.py:367
  53.1 1.0 %collective-permute-start.27 = (bf16[64,768]{1,0:T(8,128)(2,1)S(1)}, bf16[64,768]{1,0:T(8,128)(2,1)S(1)}, u32[]{:S(2)}, u32[]{:S(2)}) collective-permute-start(bf16[64,768]{1,0:T(8,128)(2,1)S(1)} %add_convert_fusion.refs_0_), channel_id=1, source_target_pairs={{0,1},{1,0},{2,3},{3,2},{4,5},{5,4},{6,7},{7,6},{8,9},{9,8},{10,11... | collective-permute-start | bytes 294920 | tf_op jit(solution)/shard_map/ppermute | solution.py:367
  54.4 1.8 %shard_map.84 = bf16[128,1024]{1,0:T(8,128)(2,1)} custom-call(s32[8,128]{1,0:T(8,128)} %bitcast.13, bf16[64,1024]{1,0:T(8,128)(2,1)S(1)} %get-tuple-element.91.refs_0_, bf16[64,1024]{1,0:T(8,128)(2,1)S(1)} %collective-permute-done.19.refs_1_, bf16[64,1024]{1,0:T(8,128)(2,1)S(1)} %collective-permute-done.20.refs_2_, ...), custom_call_target="tpu_custom_call" | custom-call | flops 67108864 | bytes 1314816 | tf_op jit(solution)/shard_map/pallas_call | solution.py:122
  56.3 2.1 %collective-permute-done.27.refs_1_ = bf16[64,768]{1,0:T(8,128)(2,1)S(1)} collective-permute-done((bf16[64,768]{1,0:T(8,128)(2,1)S(1)}, bf16[64,768]{1,0:T(8,128)(2,1)S(1)}, u32[]{:S(2)}, u32[]{:S(2)}) %collective-permute-start.27) | collective-permute-done | bytes 98336 | tf_op jit(solution)/shard_map/ppermute | solution.py:367
  (48 shorter events, 11.2 us)
Async XLA Ops:
  1.9 7.3 %collective-permute-start = (bf16[64,1024]{1,0:T(8,128)(2,1)S(1)}, bf16[64,1024]{1,0:T(8,128)(2,1)S(1)}, u32[]{:S(2)}, u32[]{:S(2)}) collective-permute-start(bf16[64,1024]{1,0:T(8,128)(2,1)S(1)} %get-tuple-element.51), channel_id=1, source_target_pairs={{0,8},{4,12},{8,0},{12,4},{16,24},{20,28},{24,16},{28,20},{1,9},{5... | collective-permute-start | bytes 393224 | tf_op jit(solution)/shard_map/ppermute | solution.py:367
  4.9 7.8 %collective-permute-start.1 = (bf16[64,1024]{1,0:T(8,128)(2,1)S(1)}, bf16[64,1024]{1,0:T(8,128)(2,1)S(1)}, u32[]{:S(2)}, u32[]{:S(2)}) collective-permute-start(bf16[64,1024]{1,0:T(8,128)(2,1)S(1)} %get-tuple-element.52), channel_id=1, source_target_pairs={{0,16},{4,20},{8,24},{12,28},{16,0},{20,4},{24,8},{28,12},{1,17},{... | collective-permute-start | bytes 393224 | tf_op jit(solution)/shard_map/ppermute | solution.py:367
  6.4 6.3 %collective-permute-start.2 = (bf16[64,1024]{1,0:T(8,128)(2,1)S(1)}, bf16[64,1024]{1,0:T(8,128)(2,1)S(1)}, u32[]{:S(2)}, u32[]{:S(2)}) collective-permute-start(bf16[64,1024]{1,0:T(8,128)(2,1)S(1)} %get-tuple-element.53), channel_id=1, source_target_pairs={{0,24},{4,28},{8,16},{12,20},{16,8},{20,12},{24,0},{28,4},{1,25},{... | collective-permute-start | bytes 393224 | tf_op jit(solution)/shard_map/ppermute | solution.py:367
  12.7 1.5 %collective-permute-start.4 = (bf16[64,1024]{1,0:T(8,128)(2,1)S(1)}, bf16[64,1024]{1,0:T(8,128)(2,1)S(1)}, u32[]{:S(2)}, u32[]{:S(2)}) collective-permute-start(bf16[64,1024]{1,0:T(8,128)(2,1)S(1)} %collective-permute-done.refs_1_), channel_id=1, source_target_pairs={{0,4},{4,0},{8,12},{12,8},{16,20},{20,16},{24,28},{28,24},{1,5},{5... | collective-permute-start | bytes 393224 | tf_op jit(solution)/shard_map/ppermute | solution.py:367
  18.4 1.7 %collective-permute-start.11 = (bf16[256,768]{1,0:T(8,128)(2,1)S(1)}, bf16[256,768]{1,0:T(8,128)(2,1)S(1)}, u32[]{:S(2)}, u32[]{:S(2)}) collective-permute-start(bf16[256,768]{1,0:T(8,128)(2,1)S(1)} %get-tuple-element.73.d_own_ref.refs_1_), channel_id=1, source_target_pairs={{0,4},{4,0},{8,12},{12,8},{16,20},{20,16},{24,28},{28,24},{1,5},{5... | collective-permute-start | bytes 1179656 | tf_op jit(solution)/shard_map/ppermute | solution.py:367
  18.7 3.9 %collective-permute-start.7 = (bf16[256,768]{1,0:T(8,128)(2,1)S(1)}, bf16[256,768]{1,0:T(8,128)(2,1)S(1)}, u32[]{:S(2)}, u32[]{:S(2)}) collective-permute-start(bf16[256,768]{1,0:T(8,128)(2,1)S(1)} %get-tuple-element.69.d_own_ref.refs_0_), channel_id=1, source_target_pairs={{0,4},{4,0},{8,12},{12,8},{16,20},{20,16},{24,28},{28,24},{1,5},{5... | collective-permute-start | bytes 1179656 | tf_op jit(solution)/shard_map/ppermute | solution.py:367
  21.0 11.4 %collective-permute-start.12 = (bf16[256,768]{1,0:T(8,128)(2,1)S(1)}, bf16[256,768]{1,0:T(8,128)(2,1)S(1)}, u32[]{:S(2)}, u32[]{:S(2)}) collective-permute-start(bf16[256,768]{1,0:T(8,128)(2,1)S(1)} %get-tuple-element.75), channel_id=1, source_target_pairs={{0,1},{1,0},{2,3},{3,2},{4,5},{5,4},{6,7},{7,6},{8,9},{9,8},{10,11... | collective-permute-start | bytes 1179656 | tf_op jit(solution)/shard_map/ppermute | solution.py:367
  23.3 11.3 %collective-permute-start.8 = (bf16[128,768]{1,0:T(8,128)(2,1)S(1)}, bf16[128,768]{1,0:T(8,128)(2,1)S(1)}, u32[]{:S(2)}, u32[]{:S(2)}) collective-permute-start(bf16[128,768]{1,0:T(8,128)(2,1)S(1)} %get-tuple-element.70), channel_id=1, source_target_pairs={{0,8},{4,12},{8,0},{12,4},{16,24},{20,28},{24,16},{28,20},{1,9},{5... | collective-permute-start | bytes 589832 | tf_op jit(solution)/shard_map/ppermute | solution.py:367
  24.5 12.5 %collective-permute-start.9 = (bf16[128,768]{1,0:T(8,128)(2,1)S(1)}, bf16[128,768]{1,0:T(8,128)(2,1)S(1)}, u32[]{:S(2)}, u32[]{:S(2)}) collective-permute-start(bf16[128,768]{1,0:T(8,128)(2,1)S(1)} %get-tuple-element.71), channel_id=1, source_target_pairs={{0,16},{4,20},{8,24},{12,28},{16,0},{20,4},{24,8},{28,12},{1,17},{... | collective-permute-start | bytes 589832 | tf_op jit(solution)/shard_map/ppermute | solution.py:367
  25.4 11.7 %collective-permute-start.10 = (bf16[128,768]{1,0:T(8,128)(2,1)S(1)}, bf16[128,768]{1,0:T(8,128)(2,1)S(1)}, u32[]{:S(2)}, u32[]{:S(2)}) collective-permute-start(bf16[128,768]{1,0:T(8,128)(2,1)S(1)} %get-tuple-element.72), channel_id=1, source_target_pairs={{0,24},{4,28},{8,16},{12,20},{16,8},{20,12},{24,0},{28,4},{1,25},{... | collective-permute-start | bytes 589832 | tf_op jit(solution)/shard_map/ppermute | solution.py:367
  32.5 6.4 %collective-permute-start.13 = (bf16[64,768]{1,0:T(8,128)(2,1)S(1)}, bf16[64,768]{1,0:T(8,128)(2,1)S(1)}, u32[]{:S(2)}, u32[]{:S(2)}) collective-permute-start(bf16[64,768]{1,0:T(8,128)(2,1)S(1)} %get-tuple-element.78), channel_id=1, source_target_pairs={{0,8},{4,12},{8,0},{12,4},{16,24},{20,28},{24,16},{28,20},{1,9},{5... | collective-permute-start | bytes 294920 | tf_op jit(solution)/shard_map/ppermute | solution.py:367
  33.8 6.6 %collective-permute-start.14 = (bf16[64,768]{1,0:T(8,128)(2,1)S(1)}, bf16[64,768]{1,0:T(8,128)(2,1)S(1)}, u32[]{:S(2)}, u32[]{:S(2)}) collective-permute-start(bf16[64,768]{1,0:T(8,128)(2,1)S(1)} %get-tuple-element.79), channel_id=1, source_target_pairs={{0,16},{4,20},{8,24},{12,28},{16,0},{20,4},{24,8},{28,12},{1,17},{... | collective-permute-start | bytes 294920 | tf_op jit(solution)/shard_map/ppermute | solution.py:367
  34.6 5.8 %collective-permute-start.15 = (bf16[64,768]{1,0:T(8,128)(2,1)S(1)}, bf16[64,768]{1,0:T(8,128)(2,1)S(1)}, u32[]{:S(2)}, u32[]{:S(2)}) collective-permute-start(bf16[64,768]{1,0:T(8,128)(2,1)S(1)} %get-tuple-element.80), channel_id=1, source_target_pairs={{0,24},{4,28},{8,16},{12,20},{16,8},{20,12},{24,0},{28,4},{1,25},{... | collective-permute-start | bytes 294920 | tf_op jit(solution)/shard_map/ppermute | solution.py:367
  37.2 5.8 %collective-permute-start.18 = (bf16[64,768]{1,0:T(8,128)(2,1)S(1)}, bf16[64,768]{1,0:T(8,128)(2,1)S(1)}, u32[]{:S(2)}, u32[]{:S(2)}) collective-permute-start(bf16[64,768]{1,0:T(8,128)(2,1)S(1)} %get-tuple-element.90), channel_id=1, source_target_pairs={{0,1},{1,0},{2,3},{3,2},{4,5},{5,4},{6,7},{7,6},{8,9},{9,8},{10,11... | collective-permute-start | bytes 294920 | tf_op jit(solution)/shard_map/ppermute | solution.py:367
  40.4 9.8 %collective-permute-start.16 = (bf16[64,768]{1,0:T(8,128)(2,1)S(1)}, bf16[64,768]{1,0:T(8,128)(2,1)S(1)}, u32[]{:S(2)}, u32[]{:S(2)}) collective-permute-start(bf16[64,768]{1,0:T(8,128)(2,1)S(1)} %add_convert_fusion.3), channel_id=1, source_target_pairs={{0,2},{1,3},{2,0},{3,1},{4,6},{5,7},{6,4},{7,5},{8,10},{9,11},{10,... | collective-permute-start | bytes 294920 | tf_op jit(solution)/shard_map/ppermute | solution.py:367
  43.1 8.3 %collective-permute-start.26 = (bf16[64,768]{1,0:T(8,128)(2,1)S(1)}, bf16[64,768]{1,0:T(8,128)(2,1)S(1)}, u32[]{:S(2)}, u32[]{:S(2)}) collective-permute-start(bf16[64,768]{1,0:T(8,128)(2,1)S(1)} %add_convert_fusion.1), channel_id=1, source_target_pairs={{0,2},{1,3},{2,0},{3,1},{4,6},{5,7},{6,4},{7,5},{8,10},{9,11},{10,... | collective-permute-start | bytes 294920 | tf_op jit(solution)/shard_map/ppermute | solution.py:367
  44.9 6.7 %collective-permute-start.19 = (bf16[64,1024]{1,0:T(8,128)(2,1)S(1)}, bf16[64,1024]{1,0:T(8,128)(2,1)S(1)}, u32[]{:S(2)}, u32[]{:S(2)}) collective-permute-start(bf16[64,1024]{1,0:T(8,128)(2,1)S(1)} %get-tuple-element.92), channel_id=1, source_target_pairs={{0,8},{4,12},{8,0},{12,4},{16,24},{20,28},{24,16},{28,20},{1,9},{5... | collective-permute-start | bytes 393224 | tf_op jit(solution)/shard_map/ppermute | solution.py:367
  46.7 5.0 %collective-permute-start.20 = (bf16[64,1024]{1,0:T(8,128)(2,1)S(1)}, bf16[64,1024]{1,0:T(8,128)(2,1)S(1)}, u32[]{:S(2)}, u32[]{:S(2)}) collective-permute-start(bf16[64,1024]{1,0:T(8,128)(2,1)S(1)} %get-tuple-element.93), channel_id=1, source_target_pairs={{0,16},{4,20},{8,24},{12,28},{16,0},{20,4},{24,8},{28,12},{1,17},{... | collective-permute-start | bytes 393224 | tf_op jit(solution)/shard_map/ppermute | solution.py:367
  47.2 5.9 %collective-permute-start.21 = (bf16[64,1024]{1,0:T(8,128)(2,1)S(1)}, bf16[64,1024]{1,0:T(8,128)(2,1)S(1)}, u32[]{:S(2)}, u32[]{:S(2)}) collective-permute-start(bf16[64,1024]{1,0:T(8,128)(2,1)S(1)} %get-tuple-element.94), channel_id=1, source_target_pairs={{0,24},{4,28},{8,16},{12,20},{16,8},{20,12},{24,0},{28,4},{1,25},{... | collective-permute-start | bytes 393224 | tf_op jit(solution)/shard_map/ppermute | solution.py:367
  50.3 2.9 %collective-permute-start.22 = (bf16[64,1024]{1,0:T(8,128)(2,1)S(1)}, bf16[64,1024]{1,0:T(8,128)(2,1)S(1)}, u32[]{:S(2)}, u32[]{:S(2)}) collective-permute-start(bf16[64,1024]{1,0:T(8,128)(2,1)S(1)} %get-tuple-element.91.refs_0_), channel_id=1, source_target_pairs={{0,4},{4,0},{8,12},{12,8},{16,20},{20,16},{24,28},{28,24},{1,5},{5... | collective-permute-start | bytes 393224 | tf_op jit(solution)/shard_map/ppermute | solution.py:367
  51.3 5.0 %collective-permute-start.17 = (bf16[64,768]{1,0:T(8,128)(2,1)S(1)}, bf16[64,768]{1,0:T(8,128)(2,1)S(1)}, u32[]{:S(2)}, u32[]{:S(2)}) collective-permute-start(bf16[64,768]{1,0:T(8,128)(2,1)S(1)} %add_convert_fusion.2.refs_2_), channel_id=1, source_target_pairs={{0,1},{1,0},{2,3},{3,2},{4,5},{5,4},{6,7},{7,6},{8,9},{9,8},{10,11... | collective-permute-start | bytes 294920 | tf_op jit(solution)/shard_map/ppermute | solution.py:367
  51.6 2.6 %collective-permute-start.23 = (bf16[64,1024]{1,0:T(8,128)(2,1)S(1)}, bf16[64,1024]{1,0:T(8,128)(2,1)S(1)}, u32[]{:S(2)}, u32[]{:S(2)}) collective-permute-start(bf16[64,1024]{1,0:T(8,128)(2,1)S(1)} %collective-permute-done.19.refs_1_), channel_id=1, source_target_pairs={{0,4},{4,0},{8,12},{12,8},{16,20},{20,16},{24,28},{28,24},{1,5},{5... | collective-permute-start | bytes 393224 | tf_op jit(solution)/shard_map/ppermute | solution.py:367
  51.7 2.5 %collective-permute-start.24 = (bf16[64,1024]{1,0:T(8,128)(2,1)S(1)}, bf16[64,1024]{1,0:T(8,128)(2,1)S(1)}, u32[]{:S(2)}, u32[]{:S(2)}) collective-permute-start(bf16[64,1024]{1,0:T(8,128)(2,1)S(1)} %collective-permute-done.20.refs_2_), channel_id=1, source_target_pairs={{0,4},{4,0},{8,12},{12,8},{16,20},{20,16},{24,28},{28,24},{1,5},{5... | collective-permute-start | bytes 393224 | tf_op jit(solution)/shard_map/ppermute | solution.py:367
  53.1 5.3 %collective-permute-start.27 = (bf16[64,768]{1,0:T(8,128)(2,1)S(1)}, bf16[64,768]{1,0:T(8,128)(2,1)S(1)}, u32[]{:S(2)}, u32[]{:S(2)}) collective-permute-start(bf16[64,768]{1,0:T(8,128)(2,1)S(1)} %add_convert_fusion.refs_0_), channel_id=1, source_target_pairs={{0,1},{1,0},{2,3},{3,2},{4,5},{5,4},{6,7},{7,6},{8,9},{9,8},{10,11... | collective-permute-start | bytes 294920 | tf_op jit(solution)/shard_map/ppermute | solution.py:367
  (5 other events, 6.3 us)

commit v4 on v3

--- a/solution.py
+++ b/solution.py
@@ -141,13 +141,20 @@
     return matmul(flags, (at <= upto).astype(F32))
 
 
-def own_placement(users_ref, me, peers, capacity):
+def own_placement(users_ref, me, peers, capacity, paired):
     owner = lax.div(users_ref[pl.ds(me, 1), :], UPO)
     rows = owner.shape[1]
     match = (lax.broadcasted_iota(jnp.int32, (peers, rows), 0) == owner).astype(F32)
     rank = jnp.sum(running_count(match) * match, axis=0, keepdims=True) - 1.0
-    key = (owner ^ me) * capacity + rank.astype(jnp.int32)
+    block = owner ^ me
+    if not paired:
+        block = lax.div(block, 2) + lax.rem(block, 2) * (peers // 2)
+    key = block * capacity + rank.astype(jnp.int32)
     return (lax.broadcasted_iota(jnp.int32, (peers * capacity, rows), 0) == key).astype(BF16)
+
+
+def block_order(peers):
+    return [*range(0, peers, 2), *range(1, peers, 2)]
 
 
 def fetch(pairs, sems):
@@ -162,24 +169,34 @@
     users_copy, rows_copy = fetch([(users_hbm, users), (tokens_hbm, rows)], sems)
     me = lax.axis_index("dp")
     users_copy.wait()
-    place = own_placement(users, me, peers, capacity)
+    place = own_placement(users, me, peers, capacity, True)
     rows_copy.wait()
     packed = matmul(place, rows[...]).astype(BF16)
     for i, out_ref in enumerate(out_refs):
         out_ref[...] = packed[2 * i * capacity : 2 * (i + 1) * capacity]
 
 
+def sort_kernel(*refs):
+    *in_refs, mine_ref, other_ref = refs
+    capacity = in_refs[0].shape[0] // 2
+    for i, in_ref in enumerate(in_refs):
+        rows = slice(i * capacity, (i + 1) * capacity)
+        mine_ref[rows, :] = in_ref[:capacity, :]
+        other_ref[rows, :] = in_ref[capacity:, :]
+
+
 def slot_codes(users_ref, me, peers, capacity):
-    users = jnp.concatenate([users_ref[pl.ds(me ^ m, 1), :] for m in range(peers)], axis=0)
+    order = block_order(peers)
+    users = jnp.concatenate([users_ref[pl.ds(me ^ m, 1), :] for m in order], axis=0)
     rows = users.shape[1]
     match = (lax.div(users, UPO) == me).astype(F32)
     rank = running_count(match) * match - 1.0
     position = lax.broadcasted_iota(jnp.int32, (1, rows), 1)
     slot = lax.broadcasted_iota(jnp.int32, (capacity, rows), 0).astype(F32)
     codes = []
-    for m in range(peers):
-        code = (users[m : m + 1] + 1) * (peers * rows) + (me ^ m) * rows + position
-        picked = jnp.where(rank[m : m + 1] == slot, code.astype(F32), 0.0)
+    for i, m in enumerate(order):
+        code = (users[i : i + 1] + 1) * (peers * rows) + (me ^ m) * rows + position
+        picked = jnp.where(rank[i : i + 1] == slot, code.astype(F32), 0.0)
         codes.append(jnp.sum(picked, axis=1, keepdims=True))
     return jnp.concatenate(codes, axis=0)
 
@@ -192,33 +209,24 @@
     code_ref[...] = code
     key_ref[...] = code.T[0 : key_ref.shape[0]]
     grad_copy.wait()
-    for m in range(peers):
+    for i, m in enumerate(block_order(peers)):
         at = pl.multiple_of((me ^ m) * capacity, capacity)
-        grad_ref[m * capacity : (m + 1) * capacity, :] = grad[pl.ds(at, capacity), :].astype(F32) * gain_ref[...]
+        grad_ref[i * capacity : (i + 1) * capacity, :] = grad[pl.ds(at, capacity), :].astype(F32) * gain_ref[...]
     w_copy.wait()
 
 
-def attend_kernel(peers, capacity, batch_rows, gain_ref, w_ref, grad, code_ref, key_ref, *refs):
-    chips = peers // 2
-    near, far, refs = refs[:chips], refs[chips : 2 * chips], refs[2 * chips :]
-    attended_ref, *d_refs, x_own_ref, x_sib_ref, x, x_sib, act, slope = refs
+def attend_kernel(peers, capacity, batch_rows, gain_ref, w_ref, grad, code_ref, key_ref, near_ref, far_ref, *refs):
+    attended_ref, *d_refs, x_own_ref, x, act, slope = refs
     me = lax.axis_index("dp")
     slots = peers * capacity
     width, columns = w_ref.shape
     features = gain_ref.shape[1]
     block = width // peers
-    first, second = slice(0, capacity), slice(capacity, 2 * capacity)
-    for i in range(chips):
-        even = slice(2 * i * capacity, (2 * i + 1) * capacity)
-        odd = slice((2 * i + 1) * capacity, (2 * i + 2) * capacity)
-        x[even, :] = near[i][first, :]
-        x[odd, :] = far[i][second, :]
-        x_sib[even, :] = far[i][first, :]
-        x_sib[odd, :] = near[i][second, :]
-    for i in range(chips):
+    x[: slots // 2, :] = near_ref[...]
+    x[slots // 2 :, :] = far_ref[...]
+    for i in range(peers // 2):
         at = pl.multiple_of((me ^ (2 * i)) * block, block)
         x_own_ref[:, i * block : (i + 1) * block] = x[:, pl.ds(at, block)]
-        x_sib_ref[:, i * block : (i + 1) * block] = x_sib[:, pl.ds(at, block)]
     gain = gain_ref[...]
     step = 2 * HEAD_DIM
     for c in range(0, columns, step):
@@ -259,14 +267,14 @@
     grads = [part(grad, h) for h in range(HEADS)]
     for h in range(HEADS):
         normed = (unit[h] * part(gain, h)).astype(BF16)
-        for m in range(peers):
+        for i, m in enumerate(block_order(peers)):
             at = pl.multiple_of((me ^ m) * capacity, capacity)
-            attended_ref[pl.ds(at, capacity), h * HEAD_DIM : (h + 1) * HEAD_DIM] = normed[m * capacity : (m + 1) * capacity]
+            attended_ref[pl.ds(at, capacity), h * HEAD_DIM : (h + 1) * HEAD_DIM] = normed[i * capacity : (i + 1) * capacity]
     grad_mean = sum(jnp.sum(g, axis=1, keepdims=True) for g in grads) / features
     grad_unit = sum(jnp.sum(g * u, axis=1, keepdims=True) for g, u in zip(grads, unit)) / features
     per = HEADS // len(d_refs)
     for h in range(HEADS):
-        d_ref, at = d_refs[h // per], (h % per) * HEAD_DIM
+        d_ref, at = d_refs[h // per], h % per * HEAD_DIM
         d_mixed = ((grads[h] - grad_mean - unit[h] * grad_unit) * inverse).astype(BF16)
         d_scores = (matmul(d_mixed, head(2 * features, h), COLS_BY_COLS) * slopes[h]).astype(BF16)
         d_query = matmul(d_scores, head(features, h))
@@ -277,16 +285,27 @@
             d_ref[:, to : to + HEAD_DIM] = (d * part(slope, j * HEADS + h)).astype(BF16)
 
 
-def weight_block(i, x_own_ref, x_sib_ref, d_own_ref, d_sib_ref, block):
+def own_weight_kernel(peers, x_ref, near_sib_ref, far_sib_ref, d_first_ref, d_second_ref, first_ref, second_ref, x_sib_ref):
+    me = lax.axis_index("dp")
+    block = near_sib_ref.shape[1] // peers
+    half = near_sib_ref.shape[0]
+    for i in range(peers // 2):
+        at = pl.multiple_of((me ^ (2 * i)) * block, block)
+        x_sib_ref[:half, i * block : (i + 1) * block] = near_sib_ref[:, pl.ds(at, block)]
+        x_sib_ref[half:, i * block : (i + 1) * block] = far_sib_ref[:, pl.ds(at, block)]
+    first_ref[...] = matmul(x_ref[...], d_first_ref[...], ROWS_BY_ROWS)
+    second_ref[...] = matmul(x_ref[...], d_second_ref[...], ROWS_BY_ROWS)
+
+
+def weight_block(i, own_ref, x_sib_ref, d_sib_ref, block):
     at = slice(i * block, (i + 1) * block)
-    total = matmul(x_own_ref[:, at], d_own_ref[...], ROWS_BY_ROWS)
-    return total + matmul(x_sib_ref[:, at], d_sib_ref[...], ROWS_BY_ROWS)
-
-
-def weight_kernel(x_own_ref, x_sib_ref, d_own_ref, d_sib_ref, *out_refs):
-    block = x_own_ref.shape[1] // len(out_refs)
+    return own_ref[at, :] + matmul(x_sib_ref[:, at], d_sib_ref[...], ROWS_BY_ROWS)
+
+
+def weight_kernel(own_ref, x_sib_ref, d_sib_ref, *out_refs):
+    block = out_refs[0].shape[0]
     for i, out_ref in enumerate(out_refs):
-        out_ref[...] = weight_block(i, x_own_ref, x_sib_ref, d_own_ref, d_sib_ref, block).astype(out_ref.dtype)
+        out_ref[...] = weight_block(i, own_ref, x_sib_ref, d_sib_ref, block).astype(out_ref.dtype)
 
 
 def halves(half):
@@ -294,12 +313,12 @@
     return pl.multiple_of(side * half, half), pl.multiple_of((1 - side) * half, half)
 
 
-def weight_halves_kernel(blocks, x_own_ref, x_sib_ref, d_own_ref, d_sib_ref, keep_ref, send_ref, held):
+def weight_halves_kernel(blocks, own_ref, x_sib_ref, d_sib_ref, keep_ref, send_ref, held):
     block = held.shape[0]
     half = block // 2
     keep_at, send_at = halves(half)
     for i in range(blocks):
-        held[...] = weight_block(i, x_own_ref, x_sib_ref, d_own_ref, d_sib_ref, block)
+        held[...] = weight_block(i, own_ref, x_sib_ref, d_sib_ref, block)
         rows = slice(i * half, (i + 1) * half)
         keep_ref[rows, :] = held[pl.ds(keep_at, half), :]
         send_ref[rows, :] = held[pl.ds(send_at, half), :].astype(BF16)
@@ -326,10 +345,10 @@
 
 def join_kernel(features, *refs):
     *in_refs, out_ref = refs
-    half, size = in_refs[0].shape
+    half = out_ref.shape[0] // 2
     keep_at, send_at = halves(half)
-    per = size // 3
-    for p in range(len(in_refs) // 2):
+    per = in_refs[0].shape[1] // 3
+    for p in range(2):
         for in_ref, at in ((in_refs[2 * p], keep_at), (in_refs[2 * p + 1], send_at)):
             for j in range(3):
                 to = j * features + p * per
@@ -338,7 +357,8 @@
 
 def token_kernel(features, w_ref, *refs):
     d_refs, out_refs = refs[:2], refs[2:]
-    rows = out_refs[0].shape[0]
+    capacity = out_refs[0].shape[0] // 2
+    slots = d_refs[0].shape[0]
     per = d_refs[0].shape[1] // 3
     total = None
     for p, d_ref in enumerate(d_refs):
@@ -347,19 +367,19 @@
             term = matmul(d_ref[:, j * per : (j + 1) * per], w_ref[:, at : at + per], COLS_BY_COLS)
             total = term if total is None else total + term
     for i, out_ref in enumerate(out_refs):
-        out_ref[...] = total[i * rows : (i + 1) * rows].astype(BF16)
-
-
-def unpack_kernel(peers, capacity, users_hbm, *refs):
-    chips = peers // 2
-    near, far, (out_ref, held, users, sems) = refs[:chips], refs[chips : 2 * chips], refs[2 * chips :]
+        for j in range(2):
+            at = j * (slots // 2) + i * capacity
+            out_ref[j * capacity : (j + 1) * capacity, :] = total[at : at + capacity].astype(BF16)
+
+
+def unpack_kernel(peers, capacity, users_hbm, near_ref, far_ref, out_ref, held, users, sems):
     (users_copy,) = fetch([(users_hbm, users)], sems)
     me = lax.axis_index("dp")
-    for i in range(chips):
-        held[2 * i * capacity : (2 * i + 1) * capacity, :] = near[i][0:capacity, :]
-        held[(2 * i + 1) * capacity : (2 * i + 2) * capacity, :] = far[i][capacity : 2 * capacity, :]
+    half = near_ref.shape[0]
+    held[:half, :] = near_ref[...]
+    held[half:, :] = far_ref[...]
     users_copy.wait()
-    place = own_placement(users, me, peers, capacity)
+    place = own_placement(users, me, peers, capacity, False)
     out_ref[...] = matmul(place, held[...], ROWS_BY_ROWS).astype(BF16)
 
 
@@ -384,17 +404,11 @@
     exchange = functools.partial(swap, axis="dp", size=peers)
     swap_replicas = functools.partial(swap, axis="replica", size=replicas)
     pair = shaped((2 * capacity, width), BF16)
+    sorted_half = shaped((slots // 2, width), BF16)
     users_scratch = pltpu.VMEM((peers, rows), jnp.int32)
 
-    def farthest_first(arrays):
-        sent = [exchange(arrays[i], bits=2 * (i + 1)) for i in reversed(range(chips - 1))]
-        return sent[::-1]
-
-    def to_sources(pairs):
-        return [pairs[0]] + farthest_first(pairs[1:])
-
-    def to_siblings(pairs):
-        return [exchange(a, bits=1) for a in pairs]
+    def across_chips(arrays):
+        return [arrays[0]] + [exchange(arrays[i], bits=2 * i) for i in range(1, chips)]
 
     packed = call(
         functools.partial(pack_kernel, peers, capacity),
@@ -404,8 +418,8 @@
         [users_scratch, pltpu.VMEM((rows, width), BF16), pltpu.SemaphoreType.DMA((2,))],
         [HBM, HBM],
     )
-    near = to_sources(packed)
-    w_held, grad, code, key = call(
+    arrived = across_chips(packed)
+    prepared = call(
         functools.partial(prep_kernel, peers, capacity),
         [
             shaped((width, columns), BF16),
@@ -418,43 +432,57 @@
         [users_scratch, pltpu.VMEM((slots, features), BF16), pltpu.SemaphoreType.DMA((3,))],
         [HBM, VMEM, HBM, HBM],
     )
-    near, (w_held, grad, code, key) = lax.optimization_barrier((near, (w_held, grad, code, key)))
-    far = to_siblings(near)
-    attended, d_first, d_second, x_own, x_sib = call(
+    arrived, (w_held, grad, code, key) = lax.optimization_barrier((arrived, prepared))
+    near, far_sib = call(sort_kernel, [sorted_half] * 2, arrived, slots * width)
+    far = exchange(far_sib, bits=1)
+    far, near_sib = lax.optimization_barrier((far, exchange(near, bits=1)))
+    attended, d_first, d_second, x_own = call(
         functools.partial(attend_kernel, peers, capacity, peers * rows),
-        [shaped((slots, features), BF16)] + [shaped((slots, size), BF16)] * 2 + [shaped((slots, width // 2), BF16)] * 2,
-        [gain, w_held, grad, code, key, *near, *far],
+        [shaped((slots, features), BF16)] + [shaped((slots, size), BF16)] * 2 + [shaped((slots, width // 2), BF16)],
+        [gain, w_held, grad, code, key, near, far],
         2 * slots * width * columns + 14 * slots * slots * features,
         [
-            pltpu.VMEM((slots, width), BF16),
             pltpu.VMEM((slots, width), BF16),
             pltpu.VMEM((slots, columns), BF16),
             pltpu.VMEM((slots, columns), F32),
         ],
     )
-    flops = 4 * slots * (width // 2) * size
+    flops = slots * width * size
+    own_first, own_second, x_sib = call(
+        functools.partial(own_weight_kernel, peers),
+        [shaped((width // 2, size), F32)] * 2 + [shaped((slots, width // 2), BF16)],
+        [x_own, near_sib, far_sib, d_first, d_second],
+        2 * flops,
+    )
     own, *others = call(
         weight_kernel,
         [shaped((block, size), F32)] + [shaped((block, size), BF16)] * (chips - 1),
-        [x_own, x_sib, d_first, exchange(d_first, bits=1)],
+        [own_first, x_sib, exchange(d_first, bits=1)],
         flops,
     )
     keep_second, send_second = call(
         functools.partial(weight_halves_kernel, chips),
         [shaped((chips * half, size), F32), shaped((chips * half, size), BF16)],
-        [x_own, x_sib, d_second, exchange(d_second, bits=1)],
+        [own_second, x_sib, exchange(d_second, bits=1)],
         flops,
         [pltpu.VMEM((block, size), F32)],
     )
-    from_plane = farthest_first(others)
+    from_plane = across_chips([own, *others])[1:]
     from_neighbour = swap_replicas(send_second, bits=1)
+    d_slots = call(
+        functools.partial(token_kernel, features),
+        [pair] * chips,
+        [w_held, d_first, d_second],
+        2 * slots * width * columns,
+    )
+    from_neighbour, d_slots = lax.optimization_barrier((from_neighbour, d_slots))
     own_second, *others_second = call(
         sum_blocks_kernel,
         [shaped((half, size), F32)] + [shaped((half, size), BF16)] * (chips - 1),
         [keep_second, from_neighbour],
         chips * half * size,
     )
-    second_plane = farthest_first(others_second)
+    second_plane = across_chips([own_second, *others_second])[1:]
     from_plane, own_second = lax.optimization_barrier((from_plane, own_second))
     keep_first, send_first = call(
         sum_halves_kernel,
@@ -463,35 +491,30 @@
         chips * block * size,
         [pltpu.VMEM((block, size), F32)],
     )
-    first = keep_first + swap_replicas(send_first, bits=1).astype(F32)
+    first = (keep_first + swap_replicas(send_first, bits=1).astype(F32)).astype(BF16)
     second = own_second
     for other in second_plane:
         second = second + other.astype(F32)
-    d_slots = call(
-        functools.partial(token_kernel, features),
-        [pair] * chips,
-        [w_held, d_first, d_second],
-        2 * slots * width * columns,
-    )
-    d_slots, _, _ = lax.optimization_barrier((d_slots, first.astype(BF16), second.astype(BF16)))
-    near = to_sources(d_slots)
-    far = to_siblings(near)
+    second = second.astype(BF16)
+    d_slots, _, _ = lax.optimization_barrier((d_slots, first, second))
+    returned = across_chips(d_slots)
+    bits = 2
+    while 2 * bits < replicas:
+        first, second = [(v.astype(F32) + swap_replicas(v, bits=bits).astype(F32)).astype(BF16) for v in (first, second)]
+        bits *= 2
+    if bits < replicas:
+        first, second = [(v.astype(F32) + swap_replicas(v, bits=bits).astype(F32)).astype(BF16) for v in (first, second)]
+    joined = [first, swap_replicas(first, bits=1), second, swap_replicas(second, bits=1)]
+    near, far = call(sort_kernel, [sorted_half] * 2, returned, slots * width)
+    far = exchange(far, bits=1)
     (grad_tokens,) = call(
         functools.partial(unpack_kernel, peers, capacity),
         [shaped((rows, width), BF16)],
-        [users, *near, *far],
+        [users, near, far],
         2 * slots * rows * width,
         [pltpu.VMEM((slots, width), BF16), users_scratch, pltpu.SemaphoreType.DMA((1,))],
-        [HBM] + [VMEM] * (2 * chips),
-    )
-    joined = []
-    for total in (first, second):
-        held = total.astype(BF16)
-        bits = 2
-        while bits < replicas:
-            held = (held.astype(F32) + swap_replicas(held, bits=bits).astype(F32)).astype(BF16)
-            bits *= 2
-        joined += [held, swap_replicas(held, bits=1)]
+        [HBM, VMEM, VMEM],
+    )
     joined[-1], grad_tokens = lax.optimization_barrier((joined[-1], grad_tokens))
     (grad_weight,) = call(
         functools.partial(join_kernel, features),
@@ -499,7 +522,6 @@
         joined,
         block * columns,
     )
-
     return (attended[None], grad_tokens[None], grad_weight)
 
 

time: 59.6 us -> 57.3 us (0.961)
  starting transfers between devices: 26.3 us -> 24.7 us
  waiting for transfers between devices: 19.1 us -> 18.5 us
    ppermute x28 -> x23, starting transfers between devices: 26.3 us -> 24.7 us  [swap(): return lax.ppermute(array, axis, [(i, i ^ bits) for i in range(size)])]
    ppermute x28 -> x23, waiting for transfers between devices: 19.1 us -> 18.5 us  [swap(): return lax.ppermute(array, axis, [(i, i ^ bits) for i in range(size)])]
    pallas_call x10 -> x13, Pallas kernels: 12.4 us -> 12.3 us  [call(): pl.pallas_call(kernel, out_shape=outs, in_specs=specs, out_specs=[VMEM] *...]
  transfers between devices with their start and end apart: 28 -> 23, of which waited for: 14 -> 10; matrix products, arithmetic and copies ran while one was open for 0% -> 0% of each run, Pallas kernels for 11% -> 12%
where the time goes in v4:
time: 57.3 us; the launch traced here: 57.1 us
  starting transfers between devices  24.7 us (43%)
  waiting for transfers between devices  18.5 us (32%)
  Pallas kernels  12.3 us (21%)
  between operations  0.8 us (1%)
  local copies, waits for them, and re-layouts  0.68 us (1%)
    ppermute x23, starting transfers between devices, swap(): return lax.ppermute(array, axis, [(i, i ^ bits) for i in range(size)])  24.7 us
    ppermute x23, waiting for transfers between devices, swap(): return lax.ppermute(array, axis, [(i, i ^ bits) for i in range(size)])  18.5 us
    pallas_call x13, Pallas kernels, call(): pl.pallas_call(kernel, out_shape=outs, in_specs=specs, out_specs=[VMEM] *...  12.3 us
  transfers between devices with their start and end apart: 23, of which 10 were waited for; matrix products, arithmetic and copies ran while one was open for 0% of the time, Pallas kernels for 12%

profile of v4, /device:TPU:0, one launch (start us, length us, event | category | flops | bytes accessed | tf_op | source)
XLA Modules:
  0.0 57.1 jit_solution(7932926206335787545)
XLA Ops:
  0.6 1.3 %shard_map.76 = (bf16[64,1024]{1,0:T(8,128)(2,1)S(1)}, bf16[64,1024]{1,0:T(8,128)(2,1)S(1)}, bf16[64,1024]{1,0:T(8,128)(2,1)S(1)}, bf16[64,1024]{1,0:T(8,128)(2,1)S(1)}) custom-call(s32[8,128]{1,0:T(8,128)} %bitcast.11, bf16[128,1024]{1,0:T(8,128)(2,1)} %bitcast.10), custom_call_target="tpu_custom_call" | custom-call | flops 67108864 | bytes 790528 | tf_op jit(solution)/shard_map/pallas_call | solution.py:122
  1.9 3.0 %collective-permute-start = (bf16[64,1024]{1,0:T(8,128)(2,1)S(1)}, bf16[64,1024]{1,0:T(8,128)(2,1)S(1)}, u32[]{:S(2)}, u32[]{:S(2)}) collective-permute-start(bf16[64,1024]{1,0:T(8,128)(2,1)S(1)} %get-tuple-element.64), channel_id=1, source_target_pairs={{0,8},{4,12},{8,0},{12,4},{16,24},{20,28},{24,16},{28,20},{1,9},{5... | collective-permute-start | bytes 393224 | tf_op jit(solution)/shard_map/ppermute | solution.py:387
  4.9 1.5 %collective-permute-start.1 = (bf16[64,1024]{1,0:T(8,128)(2,1)S(1)}, bf16[64,1024]{1,0:T(8,128)(2,1)S(1)}, u32[]{:S(2)}, u32[]{:S(2)}) collective-permute-start(bf16[64,1024]{1,0:T(8,128)(2,1)S(1)} %get-tuple-element.65), channel_id=1, source_target_pairs={{0,16},{4,20},{8,24},{12,28},{16,0},{20,4},{24,8},{28,12},{1,17},{... | collective-permute-start | bytes 393224 | tf_op jit(solution)/shard_map/ppermute | solution.py:387
  7.1 2.0 %shard_map.77 = (bf16[1024,1536]{1,0:T(8,128)(2,1)S(1)}, f32[256,512]{1,0:T(8,128)S(1)}, f32[256,128]{1,0:T(8,128)S(1)}, f32[8,256]{1,0:T(8,128)S(1)}) custom-call(s32[8,128]{1,0:T(8,128)} %bitcast.12, f32[1,512]{1,0:T(1,128)S(1)} %bitcast.6, bf16[1024,1536]{1,0:T(8,128)(2,1)} %w_hbm.1, bf16[256,512]{1,0:T(8,128)(2,1)} %bitcast.8), custom_call_target="tpu_custom_call" | custom-call | flops 16777216 | bytes 7223296 | tf_op jit(solution)/shard_map/pallas_call | solution.py:122
  9.2 3.5 %collective-permute-done.1.refs_2_ = bf16[64,1024]{1,0:T(8,128)(2,1)S(1)} collective-permute-done((bf16[64,1024]{1,0:T(8,128)(2,1)S(1)}, bf16[64,1024]{1,0:T(8,128)(2,1)S(1)}, u32[]{:S(2)}, u32[]{:S(2)}) %collective-permute-start.1) | collective-permute-done | bytes 131104 | tf_op jit(solution)/shard_map/ppermute | solution.py:387
  13.3 1.0 %collective-permute-done.4.near_sib_ref = bf16[128,1024]{1,0:T(8,128)(2,1)S(1)} collective-permute-done((bf16[128,1024]{1,0:T(8,128)(2,1)S(1)}, bf16[128,1024]{1,0:T(8,128)(2,1)S(1)}, u32[]{:S(2)}, u32[]{:S(2)}) %collective-permute-start.4) | collective-permute-done | bytes 262176 | tf_op jit(solution)/shard_map/ppermute | solution.py:387
  14.7 3.3 %shard_map.79 = (bf16[256,512]{1,0:T(8,128)(2,1)}, bf16[256,768]{1,0:T(8,128)(2,1)S(1)}, bf16[256,768]{1,0:T(8,128)(2,1)S(1)}, bf16[256,512]{1,0:T(8,128)(2,1)S(1)}) custom-call(f32[1,512]{1,0:T(1,128)S(1)} %bitcast.7, bf16[1024,1536]{1,0:T(8,128)(2,1)S(1)} %get-tuple-element.71.w_ref, f32[256,512]{1,0:T(8,128)S(1)} %get-tuple-element.72.grad, ...), custom_call_target="tpu_custom_call" | custom-call | flops 1275068416 | bytes 5646336 | tf_op jit(solution)/shard_map/pallas_call | solution.py:122
  20.4 1.6 %collective-permute-start.10 = (bf16[256,768]{1,0:T(8,128)(2,1)S(1)}, bf16[256,768]{1,0:T(8,128)(2,1)S(1)}, u32[]{:S(2)}, u32[]{:S(2)}) collective-permute-start(bf16[256,768]{1,0:T(8,128)(2,1)S(1)} %get-tuple-element.94), channel_id=1, source_target_pairs={{0,1},{1,0},{2,3},{3,2},{4,5},{5,4},{6,7},{7,6},{8,9},{9,8},{10,11... | collective-permute-start | bytes 1179656 | tf_op jit(solution)/shard_map/ppermute | solution.py:387
  22.5 1.3 %collective-permute-start.6 = (bf16[128,768]{1,0:T(8,128)(2,1)S(1)}, bf16[128,768]{1,0:T(8,128)(2,1)S(1)}, u32[]{:S(2)}, u32[]{:S(2)}) collective-permute-start(bf16[128,768]{1,0:T(8,128)(2,1)S(1)} %get-tuple-element.89), channel_id=1, source_target_pairs={{0,8},{4,12},{8,0},{12,4},{16,24},{20,28},{24,16},{28,20},{1,9},{5... | collective-permute-start | bytes 589832 | tf_op jit(solution)/shard_map/ppermute | solution.py:387
  24.6 1.4 %collective-permute-start.8 = (bf16[128,768]{1,0:T(8,128)(2,1)S(1)}, bf16[128,768]{1,0:T(8,128)(2,1)S(1)}, u32[]{:S(2)}, u32[]{:S(2)}) collective-permute-start(bf16[128,768]{1,0:T(8,128)(2,1)S(1)} %get-tuple-element.91), channel_id=1, source_target_pairs={{0,24},{4,28},{8,16},{12,20},{16,8},{20,12},{24,0},{28,4},{1,25},{... | collective-permute-start | bytes 589832 | tf_op jit(solution)/shard_map/ppermute | solution.py:387
  27.1 4.6 %collective-permute-done.10.in_ref = bf16[256,768]{1,0:T(8,128)(2,1)S(1)} collective-permute-done((bf16[256,768]{1,0:T(8,128)(2,1)S(1)}, bf16[256,768]{1,0:T(8,128)(2,1)S(1)}, u32[]{:S(2)}, u32[]{:S(2)}) %collective-permute-start.10) | collective-permute-done | bytes 393248 | tf_op jit(solution)/shard_map/ppermute | solution.py:387
  31.7 1.3 %collective-permute-start.11 = (bf16[64,768]{1,0:T(8,128)(2,1)S(1)}, bf16[64,768]{1,0:T(8,128)(2,1)S(1)}, u32[]{:S(2)}, u32[]{:S(2)}) collective-permute-start(bf16[64,768]{1,0:T(8,128)(2,1)S(1)} %get-tuple-element.102), channel_id=1, source_target_pairs={{0,8},{4,12},{8,0},{12,4},{16,24},{20,28},{24,16},{28,20},{1,9},{5... | collective-permute-start | bytes 294920 | tf_op jit(solution)/shard_map/ppermute | solution.py:387
  33.8 1.5 %collective-permute-start.13 = (bf16[64,768]{1,0:T(8,128)(2,1)S(1)}, bf16[64,768]{1,0:T(8,128)(2,1)S(1)}, u32[]{:S(2)}, u32[]{:S(2)}) collective-permute-start(bf16[64,768]{1,0:T(8,128)(2,1)S(1)} %get-tuple-element.104), channel_id=1, source_target_pairs={{0,24},{4,28},{8,16},{12,20},{16,8},{20,12},{24,0},{28,4},{1,25},{... | collective-permute-start | bytes 294920 | tf_op jit(solution)/shard_map/ppermute | solution.py:387
  35.5 1.6 %collective-permute-start.16 = (bf16[64,768]{1,0:T(8,128)(2,1)S(1)}, bf16[64,768]{1,0:T(8,128)(2,1)S(1)}, u32[]{:S(2)}, u32[]{:S(2)}) collective-permute-start(bf16[64,768]{1,0:T(8,128)(2,1)S(1)} %get-tuple-element.114), channel_id=1, source_target_pairs={{0,1},{1,0},{2,3},{3,2},{4,5},{5,4},{6,7},{7,6},{8,9},{9,8},{10,11... | collective-permute-start | bytes 294920 | tf_op jit(solution)/shard_map/ppermute | solution.py:387
  37.1 1.2 %collective-permute-done.12 = bf16[64,768]{1,0:T(8,128)(2,1)S(1)} collective-permute-done((bf16[64,768]{1,0:T(8,128)(2,1)S(1)}, bf16[64,768]{1,0:T(8,128)(2,1)S(1)}, u32[]{:S(2)}, u32[]{:S(2)}) %collective-permute-start.12) | collective-permute-done | bytes 98336 | tf_op jit(solution)/shard_map/ppermute | solution.py:387
  38.3 1.0 %collective-permute-done.13 = bf16[64,768]{1,0:T(8,128)(2,1)S(1)} collective-permute-done((bf16[64,768]{1,0:T(8,128)(2,1)S(1)}, bf16[64,768]{1,0:T(8,128)(2,1)S(1)}, u32[]{:S(2)}, u32[]{:S(2)}) %collective-permute-start.13) | collective-permute-done | bytes 98336 | tf_op jit(solution)/shard_map/ppermute | solution.py:387
  39.4 2.7 %collective-permute-start.14 = (bf16[64,768]{1,0:T(8,128)(2,1)S(1)}, bf16[64,768]{1,0:T(8,128)(2,1)S(1)}, u32[]{:S(2)}, u32[]{:S(2)}) collective-permute-start(bf16[64,768]{1,0:T(8,128)(2,1)S(1)} %add_convert_fusion.3), channel_id=1, source_target_pairs={{0,2},{1,3},{2,0},{3,1},{4,6},{5,7},{6,4},{7,5},{8,10},{9,11},{10,... | collective-permute-start | bytes 294920 | tf_op jit(solution)/shard_map/ppermute | solution.py:387
  42.8 1.2 %collective-permute-start.17 = (bf16[64,1024]{1,0:T(8,128)(2,1)S(1)}, bf16[64,1024]{1,0:T(8,128)(2,1)S(1)}, u32[]{:S(2)}, u32[]{:S(2)}) collective-permute-start(bf16[64,1024]{1,0:T(8,128)(2,1)S(1)} %get-tuple-element.116), channel_id=1, source_target_pairs={{0,8},{4,12},{8,0},{12,4},{16,24},{20,28},{24,16},{28,20},{1,9},{5... | collective-permute-start | bytes 393224 | tf_op jit(solution)/shard_map/ppermute | solution.py:387
  44.9 1.4 %collective-permute-start.19 = (bf16[64,1024]{1,0:T(8,128)(2,1)S(1)}, bf16[64,1024]{1,0:T(8,128)(2,1)S(1)}, u32[]{:S(2)}, u32[]{:S(2)}) collective-permute-start(bf16[64,1024]{1,0:T(8,128)(2,1)S(1)} %get-tuple-element.118), channel_id=1, source_target_pairs={{0,24},{4,28},{8,16},{12,20},{16,8},{20,12},{24,0},{28,4},{1,25},{... | collective-permute-start | bytes 393224 | tf_op jit(solution)/shard_map/ppermute | solution.py:387
  46.3 2.8 %collective-permute-done.14 = bf16[64,768]{1,0:T(8,128)(2,1)S(1)} collective-permute-done((bf16[64,768]{1,0:T(8,128)(2,1)S(1)}, bf16[64,768]{1,0:T(8,128)(2,1)S(1)}, u32[]{:S(2)}, u32[]{:S(2)}) %collective-permute-start.14) | collective-permute-done | bytes 98336 | tf_op jit(solution)/shard_map/ppermute | solution.py:387
  49.2 1.5 %collective-permute-done.19.refs_3_ = bf16[64,1024]{1,0:T(8,128)(2,1)S(1)} collective-permute-done((bf16[64,1024]{1,0:T(8,128)(2,1)S(1)}, bf16[64,1024]{1,0:T(8,128)(2,1)S(1)}, u32[]{:S(2)}, u32[]{:S(2)}) %collective-permute-start.19) | collective-permute-done | bytes 131104 | tf_op jit(solution)/shard_map/ppermute | solution.py:387
  50.9 1.6 %collective-permute-start.22 = (bf16[64,768]{1,0:T(8,128)(2,1)S(1)}, bf16[64,768]{1,0:T(8,128)(2,1)S(1)}, u32[]{:S(2)}, u32[]{:S(2)}) collective-permute-start(bf16[64,768]{1,0:T(8,128)(2,1)S(1)} %add_convert_fusion.refs_0_), channel_id=1, source_target_pairs={{0,1},{1,0},{2,3},{3,2},{4,5},{5,4},{6,7},{7,6},{8,9},{9,8},{10,11... | collective-permute-start | bytes 294920 | tf_op jit(solution)/shard_map/ppermute | solution.py:387
  52.5 1.8 %shard_map.87 = bf16[128,1024]{1,0:T(8,128)(2,1)} custom-call(s32[8,128]{1,0:T(8,128)} %bitcast.13, bf16[128,1024]{1,0:T(8,128)(2,1)S(1)} %get-tuple-element.119.near_ref, bf16[128,1024]{1,0:T(8,128)(2,1)S(1)} %collective-permute-done.20.far_ref), custom_call_target="tpu_custom_call" | custom-call | flops 67108864 | bytes 790528 | tf_op jit(solution)/shard_map/pallas_call | solution.py:122
  54.4 1.8 %collective-permute-done.22.refs_1_ = bf16[64,768]{1,0:T(8,128)(2,1)S(1)} collective-permute-done((bf16[64,768]{1,0:T(8,128)(2,1)S(1)}, bf16[64,768]{1,0:T(8,128)(2,1)S(1)}, u32[]{:S(2)}, u32[]{:S(2)}) %collective-permute-start.22) | collective-permute-done | bytes 98336 | tf_op jit(solution)/shard_map/ppermute | solution.py:387
  (41 shorter events, 10.1 us)
Async XLA Ops:
  1.9 7.3 %collective-permute-start = (bf16[64,1024]{1,0:T(8,128)(2,1)S(1)}, bf16[64,1024]{1,0:T(8,128)(2,1)S(1)}, u32[]{:S(2)}, u32[]{:S(2)}) collective-permute-start(bf16[64,1024]{1,0:T(8,128)(2,1)S(1)} %get-tuple-element.64), channel_id=1, source_target_pairs={{0,8},{4,12},{8,0},{12,4},{16,24},{20,28},{24,16},{28,20},{1,9},{5... | collective-permute-start | bytes 393224 | tf_op jit(solution)/shard_map/ppermute | solution.py:387
  4.9 7.8 %collective-permute-start.1 = (bf16[64,1024]{1,0:T(8,128)(2,1)S(1)}, bf16[64,1024]{1,0:T(8,128)(2,1)S(1)}, u32[]{:S(2)}, u32[]{:S(2)}) collective-permute-start(bf16[64,1024]{1,0:T(8,128)(2,1)S(1)} %get-tuple-element.65), channel_id=1, source_target_pairs={{0,16},{4,20},{8,24},{12,28},{16,0},{20,4},{24,8},{28,12},{1,17},{... | collective-permute-start | bytes 393224 | tf_op jit(solution)/shard_map/ppermute | solution.py:387
  6.4 6.3 %collective-permute-start.2 = (bf16[64,1024]{1,0:T(8,128)(2,1)S(1)}, bf16[64,1024]{1,0:T(8,128)(2,1)S(1)}, u32[]{:S(2)}, u32[]{:S(2)}) collective-permute-start(bf16[64,1024]{1,0:T(8,128)(2,1)S(1)} %get-tuple-element.66), channel_id=1, source_target_pairs={{0,24},{4,28},{8,16},{12,20},{16,8},{20,12},{24,0},{28,4},{1,25},{... | collective-permute-start | bytes 393224 | tf_op jit(solution)/shard_map/ppermute | solution.py:387
  6.5 0.7 %copy-start = (f32[512]{0:T(512)S(1)}, f32[512]{0:T(512)}, u32[]{:S(2)}) copy-start(f32[512]{0:T(512)} %param.8) | copy-start | bytes 6148
  12.7 1.6 %collective-permute-start.4 = (bf16[128,1024]{1,0:T(8,128)(2,1)S(1)}, bf16[128,1024]{1,0:T(8,128)(2,1)S(1)}, u32[]{:S(2)}, u32[]{:S(2)}) collective-permute-start(bf16[128,1024]{1,0:T(8,128)(2,1)S(1)} %get-tuple-element.79.near_ref), channel_id=1, source_target_pairs={{0,4},{4,0},{8,12},{12,8},{16,20},{20,16},{24,28},{28,24},{1,5},{5... | collective-permute-start | bytes 786440 | tf_op jit(solution)/shard_map/ppermute | solution.py:387
  12.8 1.9 %collective-permute-start.3 = (bf16[128,1024]{1,0:T(8,128)(2,1)S(1)}, bf16[128,1024]{1,0:T(8,128)(2,1)S(1)}, u32[]{:S(2)}, u32[]{:S(2)}) collective-permute-start(bf16[128,1024]{1,0:T(8,128)(2,1)S(1)} %get-tuple-element.80.far_sib_ref), channel_id=1, source_target_pairs={{0,4},{4,0},{8,12},{12,8},{16,20},{20,16},{24,28},{28,24},{1,5},{5... | collective-permute-start | bytes 786440 | tf_op jit(solution)/shard_map/ppermute | solution.py:387
  18.0 1.8 %collective-permute-start.9 = (bf16[256,768]{1,0:T(8,128)(2,1)S(1)}, bf16[256,768]{1,0:T(8,128)(2,1)S(1)}, u32[]{:S(2)}, u32[]{:S(2)}) collective-permute-start(bf16[256,768]{1,0:T(8,128)(2,1)S(1)} %get-tuple-element.86.d_second_ref.refs_1_), channel_id=1, source_target_pairs={{0,4},{4,0},{8,12},{12,8},{16,20},{20,16},{24,28},{28,24},{1,5},{5... | collective-permute-start | bytes 1179656 | tf_op jit(solution)/shard_map/ppermute | solution.py:387
  18.3 3.8 %collective-permute-start.5 = (bf16[256,768]{1,0:T(8,128)(2,1)S(1)}, bf16[256,768]{1,0:T(8,128)(2,1)S(1)}, u32[]{:S(2)}, u32[]{:S(2)}) collective-permute-start(bf16[256,768]{1,0:T(8,128)(2,1)S(1)} %get-tuple-element.85.d_first_ref.refs_0_), channel_id=1, source_target_pairs={{0,4},{4,0},{8,12},{12,8},{16,20},{20,16},{24,28},{28,24},{1,5},{5... | collective-permute-start | bytes 1179656 | tf_op jit(solution)/shard_map/ppermute | solution.py:387
  20.4 11.2 %collective-permute-start.10 = (bf16[256,768]{1,0:T(8,128)(2,1)S(1)}, bf16[256,768]{1,0:T(8,128)(2,1)S(1)}, u32[]{:S(2)}, u32[]{:S(2)}) collective-permute-start(bf16[256,768]{1,0:T(8,128)(2,1)S(1)} %get-tuple-element.94), channel_id=1, source_target_pairs={{0,1},{1,0},{2,3},{3,2},{4,5},{5,4},{6,7},{7,6},{8,9},{9,8},{10,11... | collective-permute-start | bytes 1179656 | tf_op jit(solution)/shard_map/ppermute | solution.py:387
  22.5 11.4 %collective-permute-start.6 = (bf16[128,768]{1,0:T(8,128)(2,1)S(1)}, bf16[128,768]{1,0:T(8,128)(2,1)S(1)}, u32[]{:S(2)}, u32[]{:S(2)}) collective-permute-start(bf16[128,768]{1,0:T(8,128)(2,1)S(1)} %get-tuple-element.89), channel_id=1, source_target_pairs={{0,8},{4,12},{8,0},{12,4},{16,24},{20,28},{24,16},{28,20},{1,9},{5... | collective-permute-start | bytes 589832 | tf_op jit(solution)/shard_map/ppermute | solution.py:387
  23.8 11.5 %collective-permute-start.7 = (bf16[128,768]{1,0:T(8,128)(2,1)S(1)}, bf16[128,768]{1,0:T(8,128)(2,1)S(1)}, u32[]{:S(2)}, u32[]{:S(2)}) collective-permute-start(bf16[128,768]{1,0:T(8,128)(2,1)S(1)} %get-tuple-element.90), channel_id=1, source_target_pairs={{0,16},{4,20},{8,24},{12,28},{16,0},{20,4},{24,8},{28,12},{1,17},{... | collective-permute-start | bytes 589832 | tf_op jit(solution)/shard_map/ppermute | solution.py:387
  24.6 10.7 %collective-permute-start.8 = (bf16[128,768]{1,0:T(8,128)(2,1)S(1)}, bf16[128,768]{1,0:T(8,128)(2,1)S(1)}, u32[]{:S(2)}, u32[]{:S(2)}) collective-permute-start(bf16[128,768]{1,0:T(8,128)(2,1)S(1)} %get-tuple-element.91), channel_id=1, source_target_pairs={{0,24},{4,28},{8,16},{12,20},{16,8},{20,12},{24,0},{28,4},{1,25},{... | collective-permute-start | bytes 589832 | tf_op jit(solution)/shard_map/ppermute | solution.py:387
  31.7 5.4 %collective-permute-start.11 = (bf16[64,768]{1,0:T(8,128)(2,1)S(1)}, bf16[64,768]{1,0:T(8,128)(2,1)S(1)}, u32[]{:S(2)}, u32[]{:S(2)}) collective-permute-start(bf16[64,768]{1,0:T(8,128)(2,1)S(1)} %get-tuple-element.102), channel_id=1, source_target_pairs={{0,8},{4,12},{8,0},{12,4},{16,24},{20,28},{24,16},{28,20},{1,9},{5... | collective-permute-start | bytes 294920 | tf_op jit(solution)/shard_map/ppermute | solution.py:387
  33.0 5.3 %collective-permute-start.12 = (bf16[64,768]{1,0:T(8,128)(2,1)S(1)}, bf16[64,768]{1,0:T(8,128)(2,1)S(1)}, u32[]{:S(2)}, u32[]{:S(2)}) collective-permute-start(bf16[64,768]{1,0:T(8,128)(2,1)S(1)} %get-tuple-element.103), channel_id=1, source_target_pairs={{0,16},{4,20},{8,24},{12,28},{16,0},{20,4},{24,8},{28,12},{1,17},{... | collective-permute-start | bytes 294920 | tf_op jit(solution)/shard_map/ppermute | solution.py:387
  33.8 5.5 %collective-permute-start.13 = (bf16[64,768]{1,0:T(8,128)(2,1)S(1)}, bf16[64,768]{1,0:T(8,128)(2,1)S(1)}, u32[]{:S(2)}, u32[]{:S(2)}) collective-permute-start(bf16[64,768]{1,0:T(8,128)(2,1)S(1)} %get-tuple-element.104), channel_id=1, source_target_pairs={{0,24},{4,28},{8,16},{12,20},{16,8},{20,12},{24,0},{28,4},{1,25},{... | collective-permute-start | bytes 294920 | tf_op jit(solution)/shard_map/ppermute | solution.py:387
  35.5 6.6 %collective-permute-start.16 = (bf16[64,768]{1,0:T(8,128)(2,1)S(1)}, bf16[64,768]{1,0:T(8,128)(2,1)S(1)}, u32[]{:S(2)}, u32[]{:S(2)}) collective-permute-start(bf16[64,768]{1,0:T(8,128)(2,1)S(1)} %get-tuple-element.114), channel_id=1, source_target_pairs={{0,1},{1,0},{2,3},{3,2},{4,5},{5,4},{6,7},{7,6},{8,9},{9,8},{10,11... | collective-permute-start | bytes 294920 | tf_op jit(solution)/shard_map/ppermute | solution.py:387
  39.4 9.6 %collective-permute-start.14 = (bf16[64,768]{1,0:T(8,128)(2,1)S(1)}, bf16[64,768]{1,0:T(8,128)(2,1)S(1)}, u32[]{:S(2)}, u32[]{:S(2)}) collective-permute-start(bf16[64,768]{1,0:T(8,128)(2,1)S(1)} %add_convert_fusion.3), channel_id=1, source_target_pairs={{0,2},{1,3},{2,0},{3,1},{4,6},{5,7},{6,4},{7,5},{8,10},{9,11},{10,... | collective-permute-start | bytes 294920 | tf_op jit(solution)/shard_map/ppermute | solution.py:387
  42.1 8.7 %collective-permute-start.21 = (bf16[64,768]{1,0:T(8,128)(2,1)S(1)}, bf16[64,768]{1,0:T(8,128)(2,1)S(1)}, u32[]{:S(2)}, u32[]{:S(2)}) collective-permute-start(bf16[64,768]{1,0:T(8,128)(2,1)S(1)} %add_convert_fusion.1), channel_id=1, source_target_pairs={{0,2},{1,3},{2,0},{3,1},{4,6},{5,7},{6,4},{7,5},{8,10},{9,11},{10,... | collective-permute-start | bytes 294920 | tf_op jit(solution)/shard_map/ppermute | solution.py:387
  42.8 6.4 %collective-permute-start.17 = (bf16[64,1024]{1,0:T(8,128)(2,1)S(1)}, bf16[64,1024]{1,0:T(8,128)(2,1)S(1)}, u32[]{:S(2)}, u32[]{:S(2)}) collective-permute-start(bf16[64,1024]{1,0:T(8,128)(2,1)S(1)} %get-tuple-element.116), channel_id=1, source_target_pairs={{0,8},{4,12},{8,0},{12,4},{16,24},{20,28},{24,16},{28,20},{1,9},{5... | collective-permute-start | bytes 393224 | tf_op jit(solution)/shard_map/ppermute | solution.py:387
  44.0 5.2 %collective-permute-start.18 = (bf16[64,1024]{1,0:T(8,128)(2,1)S(1)}, bf16[64,1024]{1,0:T(8,128)(2,1)S(1)}, u32[]{:S(2)}, u32[]{:S(2)}) collective-permute-start(bf16[64,1024]{1,0:T(8,128)(2,1)S(1)} %get-tuple-element.117), channel_id=1, source_target_pairs={{0,16},{4,20},{8,24},{12,28},{16,0},{20,4},{24,8},{28,12},{1,17},{... | collective-permute-start | bytes 393224 | tf_op jit(solution)/shard_map/ppermute | solution.py:387
  44.9 5.9 %collective-permute-start.19 = (bf16[64,1024]{1,0:T(8,128)(2,1)S(1)}, bf16[64,1024]{1,0:T(8,128)(2,1)S(1)}, u32[]{:S(2)}, u32[]{:S(2)}) collective-permute-start(bf16[64,1024]{1,0:T(8,128)(2,1)S(1)} %get-tuple-element.118), channel_id=1, source_target_pairs={{0,24},{4,28},{8,16},{12,20},{16,8},{20,12},{24,0},{28,4},{1,25},{... | collective-permute-start | bytes 393224 | tf_op jit(solution)/shard_map/ppermute | solution.py:387
  49.1 5.2 %collective-permute-start.15 = (bf16[64,768]{1,0:T(8,128)(2,1)S(1)}, bf16[64,768]{1,0:T(8,128)(2,1)S(1)}, u32[]{:S(2)}, u32[]{:S(2)}) collective-permute-start(bf16[64,768]{1,0:T(8,128)(2,1)S(1)} %add_convert_fusion.2.refs_2_), channel_id=1, source_target_pairs={{0,1},{1,0},{2,3},{3,2},{4,5},{5,4},{6,7},{7,6},{8,9},{9,8},{10,11... | collective-permute-start | bytes 294920 | tf_op jit(solution)/shard_map/ppermute | solution.py:387
  50.8 1.8 %collective-permute-start.20 = (bf16[128,1024]{1,0:T(8,128)(2,1)S(1)}, bf16[128,1024]{1,0:T(8,128)(2,1)S(1)}, u32[]{:S(2)}, u32[]{:S(2)}) collective-permute-start(bf16[128,1024]{1,0:T(8,128)(2,1)S(1)} %get-tuple-element.120), channel_id=1, source_target_pairs={{0,4},{4,0},{8,12},{12,8},{16,20},{20,16},{24,28},{28,24},{1,5},{5... | collective-permute-start | bytes 786440 | tf_op jit(solution)/shard_map/ppermute | solution.py:387
  50.9 5.2 %collective-permute-start.22 = (bf16[64,768]{1,0:T(8,128)(2,1)S(1)}, bf16[64,768]{1,0:T(8,128)(2,1)S(1)}, u32[]{:S(2)}, u32[]{:S(2)}) collective-permute-start(bf16[64,768]{1,0:T(8,128)(2,1)S(1)} %add_convert_fusion.refs_0_), channel_id=1, source_target_pairs={{0,1},{1,0},{2,3},{3,2},{4,5},{5,4},{6,7},{7,6},{8,9},{9,8},{10,11... | collective-permute-start | bytes 294920 | tf_op jit(solution)/shard_map/ppermute | solution.py:387

commit v5 on v4

--- a/solution.py
+++ b/solution.py
@@ -176,13 +176,29 @@
         out_ref[...] = packed[2 * i * capacity : 2 * (i + 1) * capacity]
 
 
-def sort_kernel(*refs):
-    *in_refs, mine_ref, other_ref = refs
+def sort_kernel(chips, *refs):
+    in_refs, mine_ref, other_refs = refs[:chips], refs[chips], refs[chips + 1 :]
     capacity = in_refs[0].shape[0] // 2
+    for i, in_ref in enumerate(in_refs):
+        mine_ref[i * capacity : (i + 1) * capacity, :] = in_ref[:capacity, :]
+        other_refs[i][...] = in_ref[capacity:, :]
+
+
+def sort_arrived_kernel(chips, *refs):
+    in_refs, (mine_ref, other_ref, mine_part_ref, other_part_ref) = refs[:chips], refs[chips:]
+    me = lax.axis_index("dp")
+    capacity = in_refs[0].shape[0] // 2
+    block = in_refs[0].shape[1] // (2 * chips)
     for i, in_ref in enumerate(in_refs):
         rows = slice(i * capacity, (i + 1) * capacity)
         mine_ref[rows, :] = in_ref[:capacity, :]
         other_ref[rows, :] = in_ref[capacity:, :]
+    for i in range(chips):
+        columns = slice(i * block, (i + 1) * block)
+        theirs = pl.multiple_of((me ^ (2 * i + 1)) * block, block)
+        ours = pl.multiple_of((me ^ (2 * i)) * block, block)
+        mine_part_ref[:, columns] = mine_ref[:, pl.ds(theirs, block)]
+        other_part_ref[:, columns] = other_ref[:, pl.ds(ours, block)]
 
 
 def slot_codes(users_ref, me, peers, capacity):
@@ -201,13 +217,14 @@
     return jnp.concatenate(codes, axis=0)
 
 
-def prep_kernel(peers, capacity, users_hbm, gain_ref, w_hbm, grad_hbm, w_ref, grad_ref, code_ref, key_ref, users, grad, sems):
+def prep_kernel(peers, capacity, users_hbm, gain_ref, w_hbm, grad_hbm, w_ref, grad_ref, code_ref, key_ref, place_ref, users, grad, sems):
     users_copy, grad_copy, w_copy = fetch([(users_hbm, users), (grad_hbm, grad), (w_hbm, w_ref)], sems)
     me = lax.axis_index("dp")
     users_copy.wait()
     code = jnp.broadcast_to(slot_codes(users, me, peers, capacity), code_ref.shape)
     code_ref[...] = code
     key_ref[...] = code.T[0 : key_ref.shape[0]]
+    place_ref[...] = own_placement(users, me, peers, capacity, False)
     grad_copy.wait()
     for i, m in enumerate(block_order(peers)):
         at = pl.multiple_of((me ^ m) * capacity, capacity)
@@ -285,14 +302,10 @@
             d_ref[:, to : to + HEAD_DIM] = (d * part(slope, j * HEADS + h)).astype(BF16)
 
 
-def own_weight_kernel(peers, x_ref, near_sib_ref, far_sib_ref, d_first_ref, d_second_ref, first_ref, second_ref, x_sib_ref):
-    me = lax.axis_index("dp")
-    block = near_sib_ref.shape[1] // peers
-    half = near_sib_ref.shape[0]
-    for i in range(peers // 2):
-        at = pl.multiple_of((me ^ (2 * i)) * block, block)
-        x_sib_ref[:half, i * block : (i + 1) * block] = near_sib_ref[:, pl.ds(at, block)]
-        x_sib_ref[half:, i * block : (i + 1) * block] = far_sib_ref[:, pl.ds(at, block)]
+def own_weight_kernel(x_ref, near_part_ref, far_part_ref, d_first_ref, d_second_ref, first_ref, second_ref, x_sib_ref):
+    half = near_part_ref.shape[0]
+    x_sib_ref[:half, :] = near_part_ref[...]
+    x_sib_ref[half:, :] = far_part_ref[...]
     first_ref[...] = matmul(x_ref[...], d_first_ref[...], ROWS_BY_ROWS)
     second_ref[...] = matmul(x_ref[...], d_second_ref[...], ROWS_BY_ROWS)
 
@@ -372,15 +385,14 @@
             out_ref[j * capacity : (j + 1) * capacity, :] = total[at : at + capacity].astype(BF16)
 
 
-def unpack_kernel(peers, capacity, users_hbm, near_ref, far_ref, out_ref, held, users, sems):
-    (users_copy,) = fetch([(users_hbm, users)], sems)
-    me = lax.axis_index("dp")
-    half = near_ref.shape[0]
-    held[:half, :] = near_ref[...]
-    held[half:, :] = far_ref[...]
-    users_copy.wait()
-    place = own_placement(users, me, peers, capacity, False)
-    out_ref[...] = matmul(place, held[...], ROWS_BY_ROWS).astype(BF16)
+def unpack_kernel(place_ref, near_ref, *refs):
+    *far_refs, out_ref, held = refs
+    at = near_ref.shape[0]
+    held[:at, :] = near_ref[...]
+    for far_ref in far_refs:
+        held[at : at + far_ref.shape[0], :] = far_ref[...]
+        at += far_ref.shape[0]
+    out_ref[...] = matmul(place_ref[...], held[...], ROWS_BY_ROWS).astype(BF16)
 
 
 def swap(array, axis, size, bits):
@@ -426,16 +438,21 @@
             shaped((slots, features), F32),
             shaped((slots, HEAD_DIM), F32),
             shaped((8, slots), F32),
+            shaped((slots, rows), BF16),
         ],
         [users, gain, proj_weight, grad_out[0]],
         2 * slots * slots * rows,
         [users_scratch, pltpu.VMEM((slots, features), BF16), pltpu.SemaphoreType.DMA((3,))],
         [HBM, VMEM, HBM, HBM],
     )
-    arrived, (w_held, grad, code, key) = lax.optimization_barrier((arrived, prepared))
-    near, far_sib = call(sort_kernel, [sorted_half] * 2, arrived, slots * width)
-    far = exchange(far_sib, bits=1)
-    far, near_sib = lax.optimization_barrier((far, exchange(near, bits=1)))
+    arrived, (w_held, grad, code, key, place) = lax.optimization_barrier((arrived, prepared))
+    near, far_sib, near_part, far_part = call(
+        functools.partial(sort_arrived_kernel, chips),
+        [sorted_half] * 2 + [shaped((slots // 2, width // 2), BF16)] * 2,
+        arrived,
+        slots * width,
+    )
+    far, near_part = lax.optimization_barrier((exchange(far_sib, bits=1), exchange(near_part, bits=1)))
     attended, d_first, d_second, x_own = call(
         functools.partial(attend_kernel, peers, capacity, peers * rows),
         [shaped((slots, features), BF16)] + [shaped((slots, size), BF16)] * 2 + [shaped((slots, width // 2), BF16)],
@@ -449,9 +466,9 @@
     )
     flops = slots * width * size
     own_first, own_second, x_sib = call(
-        functools.partial(own_weight_kernel, peers),
+        own_weight_kernel,
         [shaped((width // 2, size), F32)] * 2 + [shaped((slots, width // 2), BF16)],
-        [x_own, near_sib, far_sib, d_first, d_second],
+        [x_own, near_part, far_part, d_first, d_second],
         2 * flops,
     )
     own, *others = call(
@@ -496,7 +513,7 @@
     for other in second_plane:
         second = second + other.astype(F32)
     second = second.astype(BF16)
-    d_slots, _, _ = lax.optimization_barrier((d_slots, first, second))
+    d_slots, _ = lax.optimization_barrier((d_slots, keep_first))
     returned = across_chips(d_slots)
     bits = 2
     while 2 * bits < replicas:
@@ -505,15 +522,19 @@
     if bits < replicas:
         first, second = [(v.astype(F32) + swap_replicas(v, bits=bits).astype(F32)).astype(BF16) for v in (first, second)]
     joined = [first, swap_replicas(first, bits=1), second, swap_replicas(second, bits=1)]
-    near, far = call(sort_kernel, [sorted_half] * 2, returned, slots * width)
-    far = exchange(far, bits=1)
+    near, *far = call(
+        functools.partial(sort_kernel, chips),
+        [sorted_half] + [shaped((capacity, width), BF16)] * chips,
+        returned,
+        slots * width,
+    )
+    far = [exchange(a, bits=1) for a in far]
     (grad_tokens,) = call(
-        functools.partial(unpack_kernel, peers, capacity),
+        unpack_kernel,
         [shaped((rows, width), BF16)],
-        [users, near, far],
+        [place, near, *far],
         2 * slots * rows * width,
-        [pltpu.VMEM((slots, width), BF16), users_scratch, pltpu.SemaphoreType.DMA((1,))],
-        [HBM, VMEM, VMEM],
+        [pltpu.VMEM((slots, width), BF16)],
     )
     joined[-1], grad_tokens = lax.optimization_barrier((joined[-1], grad_tokens))
     (grad_weight,) = call(

time: 57.3 us -> 55.5 us (0.969)
  waiting for transfers between devices: 18.5 us -> 15.8 us
  starting transfers between devices: 24.7 us -> 26.4 us
  Pallas kernels: 12.3 us -> 11.5 us
    ppermute x23 -> x26, waiting for transfers between devices: 18.5 us -> 15.8 us  [swap(): return lax.ppermute(array, axis, [(i, i ^ bits) for i in range(size)])]
    ppermute x23 -> x26, starting transfers between devices: 24.7 us -> 26.4 us  [swap(): return lax.ppermute(array, axis, [(i, i ^ bits) for i in range(size)])]
    pallas_call x13, Pallas kernels: 12.3 us -> 11.5 us  [call(): pl.pallas_call(kernel, out_shape=outs, in_specs=specs, out_specs=[VMEM] *...]
  transfers between devices with their start and end apart: 23 -> 26, of which waited for: 10 -> 10; matrix products, arithmetic and copies ran while one was open for 0% -> 0% of each run, Pallas kernels for 12% -> 11%
where the time goes in v5:
time: 55.5 us; the launch traced here: 55.2 us
  starting transfers between devices  26.4 us (48%)
  waiting for transfers between devices  15.8 us (28%)
  Pallas kernels  11.5 us (21%)
  between operations  0.75 us (1%)
  local copies, waits for them, and re-layouts  0.68 us (1%)
    ppermute x26, starting transfers between devices, swap(): return lax.ppermute(array, axis, [(i, i ^ bits) for i in range(size)])  26.4 us
    ppermute x26, waiting for transfers between devices, swap(): return lax.ppermute(array, axis, [(i, i ^ bits) for i in range(size)])  15.8 us
    pallas_call x13, Pallas kernels, call(): pl.pallas_call(kernel, out_shape=outs, in_specs=specs, out_specs=[VMEM] *...  11.5 us
  transfers between devices with their start and end apart: 26, of which 10 were waited for; matrix products, arithmetic and copies ran while one was open for 0% of the time, Pallas kernels for 11%

profile of v5, /device:TPU:0, one launch (start us, length us, event | category | flops | bytes accessed | tf_op | source)
XLA Modules:
  0.0 55.2 jit_solution(4731789371363617831)
XLA Ops:
  0.6 1.3 %shard_map.76 = (bf16[64,1024]{1,0:T(8,128)(2,1)S(1)}, bf16[64,1024]{1,0:T(8,128)(2,1)S(1)}, bf16[64,1024]{1,0:T(8,128)(2,1)S(1)}, bf16[64,1024]{1,0:T(8,128)(2,1)S(1)}) custom-call(s32[8,128]{1,0:T(8,128)} %bitcast.11, bf16[128,1024]{1,0:T(8,128)(2,1)} %bitcast.9), custom_call_target="tpu_custom_call" | custom-call | flops 67108864 | bytes 790528 | tf_op jit(solution)/shard_map/pallas_call | solution.py:122
  1.9 3.0 %collective-permute-start = (bf16[64,1024]{1,0:T(8,128)(2,1)S(1)}, bf16[64,1024]{1,0:T(8,128)(2,1)S(1)}, u32[]{:S(2)}, u32[]{:S(2)}) collective-permute-start(bf16[64,1024]{1,0:T(8,128)(2,1)S(1)} %get-tuple-element.71), channel_id=1, source_target_pairs={{0,8},{4,12},{8,0},{12,4},{16,24},{20,28},{24,16},{28,20},{1,9},{5... | collective-permute-start | bytes 393224 | tf_op jit(solution)/shard_map/ppermute | solution.py:399
  4.9 1.5 %collective-permute-start.1 = (bf16[64,1024]{1,0:T(8,128)(2,1)S(1)}, bf16[64,1024]{1,0:T(8,128)(2,1)S(1)}, u32[]{:S(2)}, u32[]{:S(2)}) collective-permute-start(bf16[64,1024]{1,0:T(8,128)(2,1)S(1)} %get-tuple-element.72), channel_id=1, source_target_pairs={{0,16},{4,20},{8,24},{12,28},{16,0},{20,4},{24,8},{28,12},{1,17},{... | collective-permute-start | bytes 393224 | tf_op jit(solution)/shard_map/ppermute | solution.py:399
  7.1 2.0 %shard_map.77 = (bf16[1024,1536]{1,0:T(8,128)(2,1)S(1)}, f32[256,512]{1,0:T(8,128)S(1)}, f32[256,128]{1,0:T(8,128)S(1)}, f32[8,256]{1,0:T(8,128)S(1)}, bf16[256,128]{1,0:T(8,128)(2,1)S(1)}) custom-call(s32[8,128]{1,0:T(8,128)} %bitcast.12, f32[1,512]{1,0:T(1,128)S(1)} %bitcast.6, bf16[1024,1536]{1,0:T(8,128)(2,1)} %w_hbm.1, bf16[256,512]{1,0:T(8,128)(2,1)} %bitcast.8), custom_call_target="tpu_custom_call" | custom-call | flops 16777216 | bytes 7288832 | tf_op jit(solution)/shard_map/pallas_call | solution.py:122
  9.2 3.5 %collective-permute-done.1.refs_2_ = bf16[64,1024]{1,0:T(8,128)(2,1)S(1)} collective-permute-done((bf16[64,1024]{1,0:T(8,128)(2,1)S(1)}, bf16[64,1024]{1,0:T(8,128)(2,1)S(1)}, u32[]{:S(2)}, u32[]{:S(2)}) %collective-permute-start.1) | collective-permute-done | bytes 131104 | tf_op jit(solution)/shard_map/ppermute | solution.py:399
  13.4 1.2 %collective-permute-done.4.near_part_ref = bf16[128,512]{1,0:T(8,128)(2,1)S(1)} collective-permute-done((bf16[128,512]{1,0:T(8,128)(2,1)S(1)}, bf16[128,512]{1,0:T(8,128)(2,1)S(1)}, u32[]{:S(2)}, u32[]{:S(2)}) %collective-permute-start.4) | collective-permute-done | bytes 131104 | tf_op jit(solution)/shard_map/ppermute | solution.py:399
  14.6 3.3 %shard_map.79 = (bf16[256,512]{1,0:T(8,128)(2,1)}, bf16[256,768]{1,0:T(8,128)(2,1)S(1)}, bf16[256,768]{1,0:T(8,128)(2,1)S(1)}, bf16[256,512]{1,0:T(8,128)(2,1)S(1)}) custom-call(f32[1,512]{1,0:T(1,128)S(1)} %bitcast.7, bf16[1024,1536]{1,0:T(8,128)(2,1)S(1)} %get-tuple-element.79.w_ref, f32[256,512]{1,0:T(8,128)S(1)} %get-tuple-element.80.grad, ...), custom_call_target="tpu_custom_call" | custom-call | flops 1275068416 | bytes 5646336 | tf_op jit(solution)/shard_map/pallas_call | solution.py:122
  20.4 1.6 %collective-permute-start.10 = (bf16[256,768]{1,0:T(8,128)(2,1)S(1)}, bf16[256,768]{1,0:T(8,128)(2,1)S(1)}, u32[]{:S(2)}, u32[]{:S(2)}) collective-permute-start(bf16[256,768]{1,0:T(8,128)(2,1)S(1)} %get-tuple-element.104), channel_id=1, source_target_pairs={{0,1},{1,0},{2,3},{3,2},{4,5},{5,4},{6,7},{7,6},{8,9},{9,8},{10,11... | collective-permute-start | bytes 1179656 | tf_op jit(solution)/shard_map/ppermute | solution.py:399
  22.4 1.3 %collective-permute-start.6 = (bf16[128,768]{1,0:T(8,128)(2,1)S(1)}, bf16[128,768]{1,0:T(8,128)(2,1)S(1)}, u32[]{:S(2)}, u32[]{:S(2)}) collective-permute-start(bf16[128,768]{1,0:T(8,128)(2,1)S(1)} %get-tuple-element.99), channel_id=1, source_target_pairs={{0,8},{4,12},{8,0},{12,4},{16,24},{20,28},{24,16},{28,20},{1,9},{5... | collective-permute-start | bytes 589832 | tf_op jit(solution)/shard_map/ppermute | solution.py:399
  24.5 1.4 %collective-permute-start.8 = (bf16[128,768]{1,0:T(8,128)(2,1)S(1)}, bf16[128,768]{1,0:T(8,128)(2,1)S(1)}, u32[]{:S(2)}, u32[]{:S(2)}) collective-permute-start(bf16[128,768]{1,0:T(8,128)(2,1)S(1)} %get-tuple-element.101), channel_id=1, source_target_pairs={{0,24},{4,28},{8,16},{12,20},{16,8},{20,12},{24,0},{28,4},{1,25},{... | collective-permute-start | bytes 589832 | tf_op jit(solution)/shard_map/ppermute | solution.py:399
  26.0 1.0 %shard_map.83 = (bf16[64,1024]{1,0:T(8,128)(2,1)S(1)}, bf16[64,1024]{1,0:T(8,128)(2,1)S(1)}, bf16[64,1024]{1,0:T(8,128)(2,1)S(1)}, bf16[64,1024]{1,0:T(8,128)(2,1)S(1)}) custom-call(bf16[1024,1536]{1,0:T(8,128)(2,1)S(1)} %get-tuple-element.79.w_ref, bf16[256,768]{1,0:T(8,128)(2,1)S(1)} %get-tuple-element.95.d_first_ref.refs_0_, ...), custom_call_target="tpu_custom_call" | custom-call | flops 805306368 | bytes 4456448 | tf_op jit(solution)/shard_map/pallas_call | solution.py:122
  27.0 4.6 %collective-permute-done.10.in_ref = bf16[256,768]{1,0:T(8,128)(2,1)S(1)} collective-permute-done((bf16[256,768]{1,0:T(8,128)(2,1)S(1)}, bf16[256,768]{1,0:T(8,128)(2,1)S(1)}, u32[]{:S(2)}, u32[]{:S(2)}) %collective-permute-start.10) | collective-permute-done | bytes 393248 | tf_op jit(solution)/shard_map/ppermute | solution.py:399
  31.7 1.3 %collective-permute-start.11 = (bf16[64,768]{1,0:T(8,128)(2,1)S(1)}, bf16[64,768]{1,0:T(8,128)(2,1)S(1)}, u32[]{:S(2)}, u32[]{:S(2)}) collective-permute-start(bf16[64,768]{1,0:T(8,128)(2,1)S(1)} %get-tuple-element.112), channel_id=1, source_target_pairs={{0,8},{4,12},{8,0},{12,4},{16,24},{20,28},{24,16},{28,20},{1,9},{5... | collective-permute-start | bytes 294920 | tf_op jit(solution)/shard_map/ppermute | solution.py:399
  33.8 1.5 %collective-permute-start.13 = (bf16[64,768]{1,0:T(8,128)(2,1)S(1)}, bf16[64,768]{1,0:T(8,128)(2,1)S(1)}, u32[]{:S(2)}, u32[]{:S(2)}) collective-permute-start(bf16[64,768]{1,0:T(8,128)(2,1)S(1)} %get-tuple-element.114), channel_id=1, source_target_pairs={{0,24},{4,28},{8,16},{12,20},{16,8},{20,12},{24,0},{28,4},{1,25},{... | collective-permute-start | bytes 294920 | tf_op jit(solution)/shard_map/ppermute | solution.py:399
  35.4 1.6 %collective-permute-start.23 = (bf16[64,768]{1,0:T(8,128)(2,1)S(1)}, bf16[64,768]{1,0:T(8,128)(2,1)S(1)}, u32[]{:S(2)}, u32[]{:S(2)}) collective-permute-start(bf16[64,768]{1,0:T(8,128)(2,1)S(1)} %get-tuple-element.135), channel_id=1, source_target_pairs={{0,1},{1,0},{2,3},{3,2},{4,5},{5,4},{6,7},{7,6},{8,9},{9,8},{10,11... | collective-permute-start | bytes 294920 | tf_op jit(solution)/shard_map/ppermute | solution.py:399
  37.0 1.2 %collective-permute-start.16 = (bf16[64,1024]{1,0:T(8,128)(2,1)S(1)}, bf16[64,1024]{1,0:T(8,128)(2,1)S(1)}, u32[]{:S(2)}, u32[]{:S(2)}) collective-permute-start(bf16[64,1024]{1,0:T(8,128)(2,1)S(1)} %get-tuple-element.126), channel_id=1, source_target_pairs={{0,8},{4,12},{8,0},{12,4},{16,24},{20,28},{24,16},{28,20},{1,9},{5... | collective-permute-start | bytes 393224 | tf_op jit(solution)/shard_map/ppermute | solution.py:399
  39.1 1.4 %collective-permute-start.18 = (bf16[64,1024]{1,0:T(8,128)(2,1)S(1)}, bf16[64,1024]{1,0:T(8,128)(2,1)S(1)}, u32[]{:S(2)}, u32[]{:S(2)}) collective-permute-start(bf16[64,1024]{1,0:T(8,128)(2,1)S(1)} %get-tuple-element.128), channel_id=1, source_target_pairs={{0,24},{4,28},{8,16},{12,20},{16,8},{20,12},{24,0},{28,4},{1,25},{... | collective-permute-start | bytes 393224 | tf_op jit(solution)/shard_map/ppermute | solution.py:399
  40.6 2.7 %collective-permute-start.14 = (bf16[64,768]{1,0:T(8,128)(2,1)S(1)}, bf16[64,768]{1,0:T(8,128)(2,1)S(1)}, u32[]{:S(2)}, u32[]{:S(2)}) collective-permute-start(bf16[64,768]{1,0:T(8,128)(2,1)S(1)} %add_convert_fusion.3), channel_id=1, source_target_pairs={{0,2},{1,3},{2,0},{3,1},{4,6},{5,7},{6,4},{7,5},{8,10},{9,11},{10,... | collective-permute-start | bytes 294920 | tf_op jit(solution)/shard_map/ppermute | solution.py:399
  43.7 1.3 %collective-permute-done.18.refs_3_ = bf16[64,1024]{1,0:T(8,128)(2,1)S(1)} collective-permute-done((bf16[64,1024]{1,0:T(8,128)(2,1)S(1)}, bf16[64,1024]{1,0:T(8,128)(2,1)S(1)}, u32[]{:S(2)}, u32[]{:S(2)}) %collective-permute-start.18) | collective-permute-done | bytes 131104 | tf_op jit(solution)/shard_map/ppermute | solution.py:399
  45.1 3.0 %collective-permute-done.14 = bf16[64,768]{1,0:T(8,128)(2,1)S(1)} collective-permute-done((bf16[64,768]{1,0:T(8,128)(2,1)S(1)}, bf16[64,768]{1,0:T(8,128)(2,1)S(1)}, u32[]{:S(2)}, u32[]{:S(2)}) %collective-permute-start.14) | collective-permute-done | bytes 98336 | tf_op jit(solution)/shard_map/ppermute | solution.py:399
  48.1 1.5 %collective-permute-start.15 = (bf16[64,768]{1,0:T(8,128)(2,1)S(1)}, bf16[64,768]{1,0:T(8,128)(2,1)S(1)}, u32[]{:S(2)}, u32[]{:S(2)}) collective-permute-start(bf16[64,768]{1,0:T(8,128)(2,1)S(1)} %add_convert_fusion.2.refs_2_), channel_id=1, source_target_pairs={{0,1},{1,0},{2,3},{3,2},{4,5},{5,4},{6,7},{7,6},{8,9},{9,8},{10,11... | collective-permute-start | bytes 294920 | tf_op jit(solution)/shard_map/ppermute | solution.py:399
  49.6 1.7 %collective-permute-start.25 = (bf16[64,768]{1,0:T(8,128)(2,1)S(1)}, bf16[64,768]{1,0:T(8,128)(2,1)S(1)}, u32[]{:S(2)}, u32[]{:S(2)}) collective-permute-start(bf16[64,768]{1,0:T(8,128)(2,1)S(1)} %add_convert_fusion.refs_0_), channel_id=1, source_target_pairs={{0,1},{1,0},{2,3},{3,2},{4,5},{5,4},{6,7},{7,6},{8,9},{9,8},{10,11... | collective-permute-start | bytes 294920 | tf_op jit(solution)/shard_map/ppermute | solution.py:399
  53.1 1.0 %shard_map.87 = bf16[128,1024]{1,0:T(8,128)(2,1)} custom-call(bf16[256,128]{1,0:T(8,128)(2,1)S(1)} %get-tuple-element.115.place_ref, bf16[128,1024]{1,0:T(8,128)(2,1)S(1)} %get-tuple-element.129.near_ref, bf16[32,1024]{1,0:T(8,128)(2,1)S(1)} %collective-permute-done.19.refs_0_, bf16[32,1024]{1,0:T(8,128)(2,1)S(1)} %collective-permute-done.20.refs_1_, ...), custom_call_target="tpu_custom_call" | custom-call | flops 67108864 | bytes 851968 | tf_op jit(solution)/shard_map/pallas_call | solution.py:122
  54.3 0.9 %shard_map.88 = f32[128,1536]{1,0:T(8,128)} custom-call(bf16[64,768]{1,0:T(8,128)(2,1)S(1)} %add_convert_fusion.refs_0_, bf16[64,768]{1,0:T(8,128)(2,1)S(1)} %collective-permute-done.25.refs_1_, bf16[64,768]{1,0:T(8,128)(2,1)S(1)} %add_convert_fusion.2.refs_2_, bf16[64,768]{1,0:T(8,128)(2,1)S(1)} %collective-permute-done.15.refs_3_), custom_call_target="tpu_custom_call" | custom-call | flops 196608 | bytes 1179648 | tf_op jit(solution)/shard_map/pallas_call | solution.py:122
  (47 shorter events, 9.5 us)
Async XLA Ops:
  1.9 7.3 %collective-permute-start = (bf16[64,1024]{1,0:T(8,128)(2,1)S(1)}, bf16[64,1024]{1,0:T(8,128)(2,1)S(1)}, u32[]{:S(2)}, u32[]{:S(2)}) collective-permute-start(bf16[64,1024]{1,0:T(8,128)(2,1)S(1)} %get-tuple-element.71), channel_id=1, source_target_pairs={{0,8},{4,12},{8,0},{12,4},{16,24},{20,28},{24,16},{28,20},{1,9},{5... | collective-permute-start | bytes 393224 | tf_op jit(solution)/shard_map/ppermute | solution.py:399
  4.9 7.8 %collective-permute-start.1 = (bf16[64,1024]{1,0:T(8,128)(2,1)S(1)}, bf16[64,1024]{1,0:T(8,128)(2,1)S(1)}, u32[]{:S(2)}, u32[]{:S(2)}) collective-permute-start(bf16[64,1024]{1,0:T(8,128)(2,1)S(1)} %get-tuple-element.72), channel_id=1, source_target_pairs={{0,16},{4,20},{8,24},{12,28},{16,0},{20,4},{24,8},{28,12},{1,17},{... | collective-permute-start | bytes 393224 | tf_op jit(solution)/shard_map/ppermute | solution.py:399
  6.4 6.3 %collective-permute-start.2 = (bf16[64,1024]{1,0:T(8,128)(2,1)S(1)}, bf16[64,1024]{1,0:T(8,128)(2,1)S(1)}, u32[]{:S(2)}, u32[]{:S(2)}) collective-permute-start(bf16[64,1024]{1,0:T(8,128)(2,1)S(1)} %get-tuple-element.73), channel_id=1, source_target_pairs={{0,24},{4,28},{8,16},{12,20},{16,8},{20,12},{24,0},{28,4},{1,25},{... | collective-permute-start | bytes 393224 | tf_op jit(solution)/shard_map/ppermute | solution.py:399
  12.8 1.8 %collective-permute-start.3 = (bf16[128,1024]{1,0:T(8,128)(2,1)S(1)}, bf16[128,1024]{1,0:T(8,128)(2,1)S(1)}, u32[]{:S(2)}, u32[]{:S(2)}) collective-permute-start(bf16[128,1024]{1,0:T(8,128)(2,1)S(1)} %get-tuple-element.88), channel_id=1, source_target_pairs={{0,4},{4,0},{8,12},{12,8},{16,20},{20,16},{24,28},{28,24},{1,5},{5... | collective-permute-start | bytes 786440 | tf_op jit(solution)/shard_map/ppermute | solution.py:399
  12.9 1.7 %collective-permute-start.4 = (bf16[128,512]{1,0:T(8,128)(2,1)S(1)}, bf16[128,512]{1,0:T(8,128)(2,1)S(1)}, u32[]{:S(2)}, u32[]{:S(2)}) collective-permute-start(bf16[128,512]{1,0:T(8,128)(2,1)S(1)} %get-tuple-element.89), channel_id=1, source_target_pairs={{0,4},{4,0},{8,12},{12,8},{16,20},{20,16},{24,28},{28,24},{1,5},{5... | collective-permute-start | bytes 393224 | tf_op jit(solution)/shard_map/ppermute | solution.py:399
  18.0 1.8 %collective-permute-start.9 = (bf16[256,768]{1,0:T(8,128)(2,1)S(1)}, bf16[256,768]{1,0:T(8,128)(2,1)S(1)}, u32[]{:S(2)}, u32[]{:S(2)}) collective-permute-start(bf16[256,768]{1,0:T(8,128)(2,1)S(1)} %get-tuple-element.96.d_second_ref.refs_1_), channel_id=1, source_target_pairs={{0,4},{4,0},{8,12},{12,8},{16,20},{20,16},{24,28},{28,24},{1,5},{5... | collective-permute-start | bytes 1179656 | tf_op jit(solution)/shard_map/ppermute | solution.py:399
  18.2 3.8 %collective-permute-start.5 = (bf16[256,768]{1,0:T(8,128)(2,1)S(1)}, bf16[256,768]{1,0:T(8,128)(2,1)S(1)}, u32[]{:S(2)}, u32[]{:S(2)}) collective-permute-start(bf16[256,768]{1,0:T(8,128)(2,1)S(1)} %get-tuple-element.95.d_first_ref.refs_0_), channel_id=1, source_target_pairs={{0,4},{4,0},{8,12},{12,8},{16,20},{20,16},{24,28},{28,24},{1,5},{5... | collective-permute-start | bytes 1179656 | tf_op jit(solution)/shard_map/ppermute | solution.py:399
  20.4 11.2 %collective-permute-start.10 = (bf16[256,768]{1,0:T(8,128)(2,1)S(1)}, bf16[256,768]{1,0:T(8,128)(2,1)S(1)}, u32[]{:S(2)}, u32[]{:S(2)}) collective-permute-start(bf16[256,768]{1,0:T(8,128)(2,1)S(1)} %get-tuple-element.104), channel_id=1, source_target_pairs={{0,1},{1,0},{2,3},{3,2},{4,5},{5,4},{6,7},{7,6},{8,9},{9,8},{10,11... | collective-permute-start | bytes 1179656 | tf_op jit(solution)/shard_map/ppermute | solution.py:399
  22.4 11.4 %collective-permute-start.6 = (bf16[128,768]{1,0:T(8,128)(2,1)S(1)}, bf16[128,768]{1,0:T(8,128)(2,1)S(1)}, u32[]{:S(2)}, u32[]{:S(2)}) collective-permute-start(bf16[128,768]{1,0:T(8,128)(2,1)S(1)} %get-tuple-element.99), channel_id=1, source_target_pairs={{0,8},{4,12},{8,0},{12,4},{16,24},{20,28},{24,16},{28,20},{1,9},{5... | collective-permute-start | bytes 589832 | tf_op jit(solution)/shard_map/ppermute | solution.py:399
  23.7 11.5 %collective-permute-start.7 = (bf16[128,768]{1,0:T(8,128)(2,1)S(1)}, bf16[128,768]{1,0:T(8,128)(2,1)S(1)}, u32[]{:S(2)}, u32[]{:S(2)}) collective-permute-start(bf16[128,768]{1,0:T(8,128)(2,1)S(1)} %get-tuple-element.100), channel_id=1, source_target_pairs={{0,16},{4,20},{8,24},{12,28},{16,0},{20,4},{24,8},{28,12},{1,17},{... | collective-permute-start | bytes 589832 | tf_op jit(solution)/shard_map/ppermute | solution.py:399
  24.5 10.7 %collective-permute-start.8 = (bf16[128,768]{1,0:T(8,128)(2,1)S(1)}, bf16[128,768]{1,0:T(8,128)(2,1)S(1)}, u32[]{:S(2)}, u32[]{:S(2)}) collective-permute-start(bf16[128,768]{1,0:T(8,128)(2,1)S(1)} %get-tuple-element.101), channel_id=1, source_target_pairs={{0,24},{4,28},{8,16},{12,20},{16,8},{20,12},{24,0},{28,4},{1,25},{... | collective-permute-start | bytes 589832 | tf_op jit(solution)/shard_map/ppermute | solution.py:399
  31.7 6.6 %collective-permute-start.11 = (bf16[64,768]{1,0:T(8,128)(2,1)S(1)}, bf16[64,768]{1,0:T(8,128)(2,1)S(1)}, u32[]{:S(2)}, u32[]{:S(2)}) collective-permute-start(bf16[64,768]{1,0:T(8,128)(2,1)S(1)} %get-tuple-element.112), channel_id=1, source_target_pairs={{0,8},{4,12},{8,0},{12,4},{16,24},{20,28},{24,16},{28,20},{1,9},{5... | collective-permute-start | bytes 294920 | tf_op jit(solution)/shard_map/ppermute | solution.py:399
  32.9 6.1 %collective-permute-start.12 = (bf16[64,768]{1,0:T(8,128)(2,1)S(1)}, bf16[64,768]{1,0:T(8,128)(2,1)S(1)}, u32[]{:S(2)}, u32[]{:S(2)}) collective-permute-start(bf16[64,768]{1,0:T(8,128)(2,1)S(1)} %get-tuple-element.113), channel_id=1, source_target_pairs={{0,16},{4,20},{8,24},{12,28},{16,0},{20,4},{24,8},{28,12},{1,17},{... | collective-permute-start | bytes 294920 | tf_op jit(solution)/shard_map/ppermute | solution.py:399
  33.8 6.8 %collective-permute-start.13 = (bf16[64,768]{1,0:T(8,128)(2,1)S(1)}, bf16[64,768]{1,0:T(8,128)(2,1)S(1)}, u32[]{:S(2)}, u32[]{:S(2)}) collective-permute-start(bf16[64,768]{1,0:T(8,128)(2,1)S(1)} %get-tuple-element.114), channel_id=1, source_target_pairs={{0,24},{4,28},{8,16},{12,20},{16,8},{20,12},{24,0},{28,4},{1,25},{... | collective-permute-start | bytes 294920 | tf_op jit(solution)/shard_map/ppermute | solution.py:399
  35.4 7.9 %collective-permute-start.23 = (bf16[64,768]{1,0:T(8,128)(2,1)S(1)}, bf16[64,768]{1,0:T(8,128)(2,1)S(1)}, u32[]{:S(2)}, u32[]{:S(2)}) collective-permute-start(bf16[64,768]{1,0:T(8,128)(2,1)S(1)} %get-tuple-element.135), channel_id=1, source_target_pairs={{0,1},{1,0},{2,3},{3,2},{4,5},{5,4},{6,7},{7,6},{8,9},{9,8},{10,11... | collective-permute-start | bytes 294920 | tf_op jit(solution)/shard_map/ppermute | solution.py:399
  37.0 6.6 %collective-permute-start.16 = (bf16[64,1024]{1,0:T(8,128)(2,1)S(1)}, bf16[64,1024]{1,0:T(8,128)(2,1)S(1)}, u32[]{:S(2)}, u32[]{:S(2)}) collective-permute-start(bf16[64,1024]{1,0:T(8,128)(2,1)S(1)} %get-tuple-element.126), channel_id=1, source_target_pairs={{0,8},{4,12},{8,0},{12,4},{16,24},{20,28},{24,16},{28,20},{1,9},{5... | collective-permute-start | bytes 393224 | tf_op jit(solution)/shard_map/ppermute | solution.py:399
  38.2 5.4 %collective-permute-start.17 = (bf16[64,1024]{1,0:T(8,128)(2,1)S(1)}, bf16[64,1024]{1,0:T(8,128)(2,1)S(1)}, u32[]{:S(2)}, u32[]{:S(2)}) collective-permute-start(bf16[64,1024]{1,0:T(8,128)(2,1)S(1)} %get-tuple-element.127), channel_id=1, source_target_pairs={{0,16},{4,20},{8,24},{12,28},{16,0},{20,4},{24,8},{28,12},{1,17},{... | collective-permute-start | bytes 393224 | tf_op jit(solution)/shard_map/ppermute | solution.py:399
  39.1 5.9 %collective-permute-start.18 = (bf16[64,1024]{1,0:T(8,128)(2,1)S(1)}, bf16[64,1024]{1,0:T(8,128)(2,1)S(1)}, u32[]{:S(2)}, u32[]{:S(2)}) collective-permute-start(bf16[64,1024]{1,0:T(8,128)(2,1)S(1)} %get-tuple-element.128), channel_id=1, source_target_pairs={{0,24},{4,28},{8,16},{12,20},{16,8},{20,12},{24,0},{28,4},{1,25},{... | collective-permute-start | bytes 393224 | tf_op jit(solution)/shard_map/ppermute | solution.py:399
  40.6 7.5 %collective-permute-start.14 = (bf16[64,768]{1,0:T(8,128)(2,1)S(1)}, bf16[64,768]{1,0:T(8,128)(2,1)S(1)}, u32[]{:S(2)}, u32[]{:S(2)}) collective-permute-start(bf16[64,768]{1,0:T(8,128)(2,1)S(1)} %add_convert_fusion.3), channel_id=1, source_target_pairs={{0,2},{1,3},{2,0},{3,1},{4,6},{5,7},{6,4},{7,5},{8,10},{9,11},{10,... | collective-permute-start | bytes 294920 | tf_op jit(solution)/shard_map/ppermute | solution.py:399
  43.3 6.3 %collective-permute-start.24 = (bf16[64,768]{1,0:T(8,128)(2,1)S(1)}, bf16[64,768]{1,0:T(8,128)(2,1)S(1)}, u32[]{:S(2)}, u32[]{:S(2)}) collective-permute-start(bf16[64,768]{1,0:T(8,128)(2,1)S(1)} %add_convert_fusion.1), channel_id=1, source_target_pairs={{0,2},{1,3},{2,0},{3,1},{4,6},{5,7},{6,4},{7,5},{8,10},{9,11},{10,... | collective-permute-start | bytes 294920 | tf_op jit(solution)/shard_map/ppermute | solution.py:399
  45.0 6.8 %collective-permute-start.19 = (bf16[32,1024]{1,0:T(8,128)(2,1)S(1)}, bf16[32,1024]{1,0:T(8,128)(2,1)S(1)}, u32[]{:S(2)}, u32[]{:S(2)}) collective-permute-start(bf16[32,1024]{1,0:T(8,128)(2,1)S(1)} %get-tuple-element.130), channel_id=1, source_target_pairs={{0,4},{4,0},{8,12},{12,8},{16,20},{20,16},{24,28},{28,24},{1,5},{5... | collective-permute-start | bytes 196616 | tf_op jit(solution)/shard_map/ppermute | solution.py:399
  48.1 5.9 %collective-permute-start.15 = (bf16[64,768]{1,0:T(8,128)(2,1)S(1)}, bf16[64,768]{1,0:T(8,128)(2,1)S(1)}, u32[]{:S(2)}, u32[]{:S(2)}) collective-permute-start(bf16[64,768]{1,0:T(8,128)(2,1)S(1)} %add_convert_fusion.2.refs_2_), channel_id=1, source_target_pairs={{0,1},{1,0},{2,3},{3,2},{4,5},{5,4},{6,7},{7,6},{8,9},{9,8},{10,11... | collective-permute-start | bytes 294920 | tf_op jit(solution)/shard_map/ppermute | solution.py:399
  49.6 4.7 %collective-permute-start.25 = (bf16[64,768]{1,0:T(8,128)(2,1)S(1)}, bf16[64,768]{1,0:T(8,128)(2,1)S(1)}, u32[]{:S(2)}, u32[]{:S(2)}) collective-permute-start(bf16[64,768]{1,0:T(8,128)(2,1)S(1)} %add_convert_fusion.refs_0_), channel_id=1, source_target_pairs={{0,1},{1,0},{2,3},{3,2},{4,5},{5,4},{6,7},{7,6},{8,9},{9,8},{10,11... | collective-permute-start | bytes 294920 | tf_op jit(solution)/shard_map/ppermute | solution.py:399
  51.3 1.4 %collective-permute-start.21 = (bf16[32,1024]{1,0:T(8,128)(2,1)S(1)}, bf16[32,1024]{1,0:T(8,128)(2,1)S(1)}, u32[]{:S(2)}, u32[]{:S(2)}) collective-permute-start(bf16[32,1024]{1,0:T(8,128)(2,1)S(1)} %get-tuple-element.132), channel_id=1, source_target_pairs={{0,4},{4,0},{8,12},{12,8},{16,20},{20,16},{24,28},{28,24},{1,5},{5... | collective-permute-start | bytes 196616 | tf_op jit(solution)/shard_map/ppermute | solution.py:399
  (3 other events, 3.2 us)

commit v6 on v5

--- a/solution.py
+++ b/solution.py
@@ -522,13 +522,13 @@
     if bits < replicas:
         first, second = [(v.astype(F32) + swap_replicas(v, bits=bits).astype(F32)).astype(BF16) for v in (first, second)]
     joined = [first, swap_replicas(first, bits=1), second, swap_replicas(second, bits=1)]
-    near, *far = call(
-        functools.partial(sort_kernel, chips),
-        [sorted_half] + [shaped((capacity, width), BF16)] * chips,
+    near, far, _, _ = call(
+        functools.partial(sort_arrived_kernel, chips),
+        [sorted_half] * 2 + [shaped((slots // 2, width // 2), BF16)] * 2,
         returned,
         slots * width,
     )
-    far = [exchange(a, bits=1) for a in far]
+    far = [exchange(far, bits=1)]
     (grad_tokens,) = call(
         unpack_kernel,
         [shaped((rows, width), BF16)],

time: 55.5 us -> 55.5 us (level)
  Pallas kernels: 11.5 us -> 12.3 us
  starting transfers between devices: 26.4 us -> 25.6 us
    pallas_call x13, Pallas kernels: 11.5 us -> 12.3 us  [call(): pl.pallas_call(kernel, out_shape=outs, in_specs=specs, out_specs=[VMEM] *...]
    ppermute x26 -> x23, starting transfers between devices: 26.4 us -> 25.6 us  [swap(): return lax.ppermute(array, axis, [(i, i ^ bits) for i in range(size)])]
    ppermute x26 -> x23, waiting for transfers between devices: 15.8 us -> 15.8 us  [swap(): return lax.ppermute(array, axis, [(i, i ^ bits) for i in range(size)])]
  transfers between devices with their start and end apart: 26 -> 23, of which waited for: 10 -> 8; matrix products, arithmetic and copies ran while one was open for 0% -> 0% of each run, Pallas kernels for 11% -> 12%
where the time goes in v6:
time: 55.5 us; the launch traced here: 55.2 us
  starting transfers between devices  25.6 us (46%)
  waiting for transfers between devices  15.8 us (28%)
  Pallas kernels  12.3 us (22%)
  between operations  0.74 us (1%)
  local copies, waits for them, and re-layouts  0.68 us (1%)
    ppermute x23, starting transfers between devices, swap(): return lax.ppermute(array, axis, [(i, i ^ bits) for i in range(size)])  25.6 us
    ppermute x23, waiting for transfers between devices, swap(): return lax.ppermute(array, axis, [(i, i ^ bits) for i in range(size)])  15.8 us
    pallas_call x13, Pallas kernels, call(): pl.pallas_call(kernel, out_shape=outs, in_specs=specs, out_specs=[VMEM] *...  12.3 us
  transfers between devices with their start and end apart: 23, of which 8 were waited for; matrix products, arithmetic and copies ran while one was open for 0% of the time, Pallas kernels for 12%

profile of v6, /device:TPU:0, one launch (start us, length us, event | category | flops | bytes accessed | tf_op | source)
XLA Modules:
  0.0 55.2 jit_solution(6869044223251996914)
XLA Ops:
  0.6 1.3 %shard_map.76 = (bf16[64,1024]{1,0:T(8,128)(2,1)S(1)}, bf16[64,1024]{1,0:T(8,128)(2,1)S(1)}, bf16[64,1024]{1,0:T(8,128)(2,1)S(1)}, bf16[64,1024]{1,0:T(8,128)(2,1)S(1)}) custom-call(s32[8,128]{1,0:T(8,128)} %bitcast.11, bf16[128,1024]{1,0:T(8,128)(2,1)} %bitcast.9), custom_call_target="tpu_custom_call" | custom-call | flops 67108864 | bytes 790528 | tf_op jit(solution)/shard_map/pallas_call | solution.py:122
  1.9 3.0 %collective-permute-start = (bf16[64,1024]{1,0:T(8,128)(2,1)S(1)}, bf16[64,1024]{1,0:T(8,128)(2,1)S(1)}, u32[]{:S(2)}, u32[]{:S(2)}) collective-permute-start(bf16[64,1024]{1,0:T(8,128)(2,1)S(1)} %get-tuple-element.68), channel_id=1, source_target_pairs={{0,8},{4,12},{8,0},{12,4},{16,24},{20,28},{24,16},{28,20},{1,9},{5... | collective-permute-start | bytes 393224 | tf_op jit(solution)/shard_map/ppermute | solution.py:399
  4.9 1.5 %collective-permute-start.1 = (bf16[64,1024]{1,0:T(8,128)(2,1)S(1)}, bf16[64,1024]{1,0:T(8,128)(2,1)S(1)}, u32[]{:S(2)}, u32[]{:S(2)}) collective-permute-start(bf16[64,1024]{1,0:T(8,128)(2,1)S(1)} %get-tuple-element.69), channel_id=1, source_target_pairs={{0,16},{4,20},{8,24},{12,28},{16,0},{20,4},{24,8},{28,12},{1,17},{... | collective-permute-start | bytes 393224 | tf_op jit(solution)/shard_map/ppermute | solution.py:399
  7.1 2.0 %shard_map.77 = (bf16[1024,1536]{1,0:T(8,128)(2,1)S(1)}, f32[256,512]{1,0:T(8,128)S(1)}, f32[256,128]{1,0:T(8,128)S(1)}, f32[8,256]{1,0:T(8,128)S(1)}, bf16[256,128]{1,0:T(8,128)(2,1)S(1)}) custom-call(s32[8,128]{1,0:T(8,128)} %bitcast.12, f32[1,512]{1,0:T(1,128)S(1)} %bitcast.6, bf16[1024,1536]{1,0:T(8,128)(2,1)} %w_hbm.1, bf16[256,512]{1,0:T(8,128)(2,1)} %bitcast.8), custom_call_target="tpu_custom_call" | custom-call | flops 16777216 | bytes 7288832 | tf_op jit(solution)/shard_map/pallas_call | solution.py:122
  9.2 3.5 %collective-permute-done.1.refs_2_ = bf16[64,1024]{1,0:T(8,128)(2,1)S(1)} collective-permute-done((bf16[64,1024]{1,0:T(8,128)(2,1)S(1)}, bf16[64,1024]{1,0:T(8,128)(2,1)S(1)}, u32[]{:S(2)}, u32[]{:S(2)}) %collective-permute-start.1) | collective-permute-done | bytes 131104 | tf_op jit(solution)/shard_map/ppermute | solution.py:399
  13.4 1.2 %collective-permute-done.4.near_part_ref = bf16[128,512]{1,0:T(8,128)(2,1)S(1)} collective-permute-done((bf16[128,512]{1,0:T(8,128)(2,1)S(1)}, bf16[128,512]{1,0:T(8,128)(2,1)S(1)}, u32[]{:S(2)}, u32[]{:S(2)}) %collective-permute-start.4) | collective-permute-done | bytes 131104 | tf_op jit(solution)/shard_map/ppermute | solution.py:399
  14.6 3.3 %shard_map.79 = (bf16[256,512]{1,0:T(8,128)(2,1)}, bf16[256,768]{1,0:T(8,128)(2,1)S(1)}, bf16[256,768]{1,0:T(8,128)(2,1)S(1)}, bf16[256,512]{1,0:T(8,128)(2,1)S(1)}) custom-call(f32[1,512]{1,0:T(1,128)S(1)} %bitcast.7, bf16[1024,1536]{1,0:T(8,128)(2,1)S(1)} %get-tuple-element.76.w_ref, f32[256,512]{1,0:T(8,128)S(1)} %get-tuple-element.77.grad, ...), custom_call_target="tpu_custom_call" | custom-call | flops 1275068416 | bytes 5646336 | tf_op jit(solution)/shard_map/pallas_call | solution.py:122
  20.4 1.6 %collective-permute-start.10 = (bf16[256,768]{1,0:T(8,128)(2,1)S(1)}, bf16[256,768]{1,0:T(8,128)(2,1)S(1)}, u32[]{:S(2)}, u32[]{:S(2)}) collective-permute-start(bf16[256,768]{1,0:T(8,128)(2,1)S(1)} %get-tuple-element.101), channel_id=1, source_target_pairs={{0,1},{1,0},{2,3},{3,2},{4,5},{5,4},{6,7},{7,6},{8,9},{9,8},{10,11... | collective-permute-start | bytes 1179656 | tf_op jit(solution)/shard_map/ppermute | solution.py:399
  22.4 1.3 %collective-permute-start.6 = (bf16[128,768]{1,0:T(8,128)(2,1)S(1)}, bf16[128,768]{1,0:T(8,128)(2,1)S(1)}, u32[]{:S(2)}, u32[]{:S(2)}) collective-permute-start(bf16[128,768]{1,0:T(8,128)(2,1)S(1)} %get-tuple-element.96), channel_id=1, source_target_pairs={{0,8},{4,12},{8,0},{12,4},{16,24},{20,28},{24,16},{28,20},{1,9},{5... | collective-permute-start | bytes 589832 | tf_op jit(solution)/shard_map/ppermute | solution.py:399
  24.5 1.4 %collective-permute-start.8 = (bf16[128,768]{1,0:T(8,128)(2,1)S(1)}, bf16[128,768]{1,0:T(8,128)(2,1)S(1)}, u32[]{:S(2)}, u32[]{:S(2)}) collective-permute-start(bf16[128,768]{1,0:T(8,128)(2,1)S(1)} %get-tuple-element.98), channel_id=1, source_target_pairs={{0,24},{4,28},{8,16},{12,20},{16,8},{20,12},{24,0},{28,4},{1,25},{... | collective-permute-start | bytes 589832 | tf_op jit(solution)/shard_map/ppermute | solution.py:399
  26.0 1.0 %shard_map.83 = (bf16[64,1024]{1,0:T(8,128)(2,1)S(1)}, bf16[64,1024]{1,0:T(8,128)(2,1)S(1)}, bf16[64,1024]{1,0:T(8,128)(2,1)S(1)}, bf16[64,1024]{1,0:T(8,128)(2,1)S(1)}) custom-call(bf16[1024,1536]{1,0:T(8,128)(2,1)S(1)} %get-tuple-element.76.w_ref, bf16[256,768]{1,0:T(8,128)(2,1)S(1)} %get-tuple-element.92.d_first_ref.refs_0_, ...), custom_call_target="tpu_custom_call" | custom-call | flops 805306368 | bytes 4456448 | tf_op jit(solution)/shard_map/pallas_call | solution.py:122
  27.0 4.6 %collective-permute-done.10.in_ref = bf16[256,768]{1,0:T(8,128)(2,1)S(1)} collective-permute-done((bf16[256,768]{1,0:T(8,128)(2,1)S(1)}, bf16[256,768]{1,0:T(8,128)(2,1)S(1)}, u32[]{:S(2)}, u32[]{:S(2)}) %collective-permute-start.10) | collective-permute-done | bytes 393248 | tf_op jit(solution)/shard_map/ppermute | solution.py:399
  31.7 1.3 %collective-permute-start.11 = (bf16[64,768]{1,0:T(8,128)(2,1)S(1)}, bf16[64,768]{1,0:T(8,128)(2,1)S(1)}, u32[]{:S(2)}, u32[]{:S(2)}) collective-permute-start(bf16[64,768]{1,0:T(8,128)(2,1)S(1)} %get-tuple-element.109), channel_id=1, source_target_pairs={{0,8},{4,12},{8,0},{12,4},{16,24},{20,28},{24,16},{28,20},{1,9},{5... | collective-permute-start | bytes 294920 | tf_op jit(solution)/shard_map/ppermute | solution.py:399
  33.8 1.5 %collective-permute-start.13 = (bf16[64,768]{1,0:T(8,128)(2,1)S(1)}, bf16[64,768]{1,0:T(8,128)(2,1)S(1)}, u32[]{:S(2)}, u32[]{:S(2)}) collective-permute-start(bf16[64,768]{1,0:T(8,128)(2,1)S(1)} %get-tuple-element.111), channel_id=1, source_target_pairs={{0,24},{4,28},{8,16},{12,20},{16,8},{20,12},{24,0},{28,4},{1,25},{... | collective-permute-start | bytes 294920 | tf_op jit(solution)/shard_map/ppermute | solution.py:399
  35.4 1.6 %collective-permute-start.20 = (bf16[64,768]{1,0:T(8,128)(2,1)S(1)}, bf16[64,768]{1,0:T(8,128)(2,1)S(1)}, u32[]{:S(2)}, u32[]{:S(2)}) collective-permute-start(bf16[64,768]{1,0:T(8,128)(2,1)S(1)} %get-tuple-element.129), channel_id=1, source_target_pairs={{0,1},{1,0},{2,3},{3,2},{4,5},{5,4},{6,7},{7,6},{8,9},{9,8},{10,11... | collective-permute-start | bytes 294920 | tf_op jit(solution)/shard_map/ppermute | solution.py:399
  37.0 1.2 %collective-permute-start.16 = (bf16[64,1024]{1,0:T(8,128)(2,1)S(1)}, bf16[64,1024]{1,0:T(8,128)(2,1)S(1)}, u32[]{:S(2)}, u32[]{:S(2)}) collective-permute-start(bf16[64,1024]{1,0:T(8,128)(2,1)S(1)} %get-tuple-element.123), channel_id=1, source_target_pairs={{0,8},{4,12},{8,0},{12,4},{16,24},{20,28},{24,16},{28,20},{1,9},{5... | collective-permute-start | bytes 393224 | tf_op jit(solution)/shard_map/ppermute | solution.py:399
  39.1 1.4 %collective-permute-start.18 = (bf16[64,1024]{1,0:T(8,128)(2,1)S(1)}, bf16[64,1024]{1,0:T(8,128)(2,1)S(1)}, u32[]{:S(2)}, u32[]{:S(2)}) collective-permute-start(bf16[64,1024]{1,0:T(8,128)(2,1)S(1)} %get-tuple-element.125), channel_id=1, source_target_pairs={{0,24},{4,28},{8,16},{12,20},{16,8},{20,12},{24,0},{28,4},{1,25},{... | collective-permute-start | bytes 393224 | tf_op jit(solution)/shard_map/ppermute | solution.py:399
  40.6 2.7 %collective-permute-start.14 = (bf16[64,768]{1,0:T(8,128)(2,1)S(1)}, bf16[64,768]{1,0:T(8,128)(2,1)S(1)}, u32[]{:S(2)}, u32[]{:S(2)}) collective-permute-start(bf16[64,768]{1,0:T(8,128)(2,1)S(1)} %add_convert_fusion.3), channel_id=1, source_target_pairs={{0,2},{1,3},{2,0},{3,1},{4,6},{5,7},{6,4},{7,5},{8,10},{9,11},{10,... | collective-permute-start | bytes 294920 | tf_op jit(solution)/shard_map/ppermute | solution.py:399
  43.7 1.3 %collective-permute-done.18.refs_3_ = bf16[64,1024]{1,0:T(8,128)(2,1)S(1)} collective-permute-done((bf16[64,1024]{1,0:T(8,128)(2,1)S(1)}, bf16[64,1024]{1,0:T(8,128)(2,1)S(1)}, u32[]{:S(2)}, u32[]{:S(2)}) %collective-permute-start.18) | collective-permute-done | bytes 131104 | tf_op jit(solution)/shard_map/ppermute | solution.py:399
  45.8 2.3 %collective-permute-done.14 = bf16[64,768]{1,0:T(8,128)(2,1)S(1)} collective-permute-done((bf16[64,768]{1,0:T(8,128)(2,1)S(1)}, bf16[64,768]{1,0:T(8,128)(2,1)S(1)}, u32[]{:S(2)}, u32[]{:S(2)}) %collective-permute-start.14) | collective-permute-done | bytes 98336 | tf_op jit(solution)/shard_map/ppermute | solution.py:399
  48.1 1.5 %collective-permute-start.15 = (bf16[64,768]{1,0:T(8,128)(2,1)S(1)}, bf16[64,768]{1,0:T(8,128)(2,1)S(1)}, u32[]{:S(2)}, u32[]{:S(2)}) collective-permute-start(bf16[64,768]{1,0:T(8,128)(2,1)S(1)} %add_convert_fusion.2.refs_2_), channel_id=1, source_target_pairs={{0,1},{1,0},{2,3},{3,2},{4,5},{5,4},{6,7},{7,6},{8,9},{9,8},{10,11... | collective-permute-start | bytes 294920 | tf_op jit(solution)/shard_map/ppermute | solution.py:399
  49.6 1.5 %collective-permute-start.22 = (bf16[64,768]{1,0:T(8,128)(2,1)S(1)}, bf16[64,768]{1,0:T(8,128)(2,1)S(1)}, u32[]{:S(2)}, u32[]{:S(2)}) collective-permute-start(bf16[64,768]{1,0:T(8,128)(2,1)S(1)} %add_convert_fusion.refs_0_), channel_id=1, source_target_pairs={{0,1},{1,0},{2,3},{3,2},{4,5},{5,4},{6,7},{7,6},{8,9},{9,8},{10,11... | collective-permute-start | bytes 294920 | tf_op jit(solution)/shard_map/ppermute | solution.py:399
  51.2 1.0 %shard_map.87 = bf16[128,1024]{1,0:T(8,128)(2,1)} custom-call(bf16[256,128]{1,0:T(8,128)(2,1)S(1)} %get-tuple-element.112.place_ref, bf16[128,1024]{1,0:T(8,128)(2,1)S(1)} %get-tuple-element.126.near_ref, bf16[128,1024]{1,0:T(8,128)(2,1)S(1)} %collective-permute-done.19.refs_0_), custom_call_target="tpu_custom_call" | custom-call | flops 67108864 | bytes 851968 | tf_op jit(solution)/shard_map/pallas_call | solution.py:122
  52.8 1.5 %collective-permute-done.22.refs_1_ = bf16[64,768]{1,0:T(8,128)(2,1)S(1)} collective-permute-done((bf16[64,768]{1,0:T(8,128)(2,1)S(1)}, bf16[64,768]{1,0:T(8,128)(2,1)S(1)}, u32[]{:S(2)}, u32[]{:S(2)}) %collective-permute-start.22) | collective-permute-done | bytes 98336 | tf_op jit(solution)/shard_map/ppermute | solution.py:399
  (41 shorter events, 9.8 us)
Async XLA Ops:
  1.9 7.3 %collective-permute-start = (bf16[64,1024]{1,0:T(8,128)(2,1)S(1)}, bf16[64,1024]{1,0:T(8,128)(2,1)S(1)}, u32[]{:S(2)}, u32[]{:S(2)}) collective-permute-start(bf16[64,1024]{1,0:T(8,128)(2,1)S(1)} %get-tuple-element.68), channel_id=1, source_target_pairs={{0,8},{4,12},{8,0},{12,4},{16,24},{20,28},{24,16},{28,20},{1,9},{5... | collective-permute-start | bytes 393224 | tf_op jit(solution)/shard_map/ppermute | solution.py:399
  4.9 7.8 %collective-permute-start.1 = (bf16[64,1024]{1,0:T(8,128)(2,1)S(1)}, bf16[64,1024]{1,0:T(8,128)(2,1)S(1)}, u32[]{:S(2)}, u32[]{:S(2)}) collective-permute-start(bf16[64,1024]{1,0:T(8,128)(2,1)S(1)} %get-tuple-element.69), channel_id=1, source_target_pairs={{0,16},{4,20},{8,24},{12,28},{16,0},{20,4},{24,8},{28,12},{1,17},{... | collective-permute-start | bytes 393224 | tf_op jit(solution)/shard_map/ppermute | solution.py:399
  6.4 6.3 %collective-permute-start.2 = (bf16[64,1024]{1,0:T(8,128)(2,1)S(1)}, bf16[64,1024]{1,0:T(8,128)(2,1)S(1)}, u32[]{:S(2)}, u32[]{:S(2)}) collective-permute-start(bf16[64,1024]{1,0:T(8,128)(2,1)S(1)} %get-tuple-element.70), channel_id=1, source_target_pairs={{0,24},{4,28},{8,16},{12,20},{16,8},{20,12},{24,0},{28,4},{1,25},{... | collective-permute-start | bytes 393224 | tf_op jit(solution)/shard_map/ppermute | solution.py:399
  6.5 0.7 %copy-start = (f32[512]{0:T(512)S(1)}, f32[512]{0:T(512)}, u32[]{:S(2)}) copy-start(f32[512]{0:T(512)} %param.8) | copy-start | bytes 6148
  12.8 1.8 %collective-permute-start.3 = (bf16[128,1024]{1,0:T(8,128)(2,1)S(1)}, bf16[128,1024]{1,0:T(8,128)(2,1)S(1)}, u32[]{:S(2)}, u32[]{:S(2)}) collective-permute-start(bf16[128,1024]{1,0:T(8,128)(2,1)S(1)} %get-tuple-element.85), channel_id=1, source_target_pairs={{0,4},{4,0},{8,12},{12,8},{16,20},{20,16},{24,28},{28,24},{1,5},{5... | collective-permute-start | bytes 786440 | tf_op jit(solution)/shard_map/ppermute | solution.py:399
  12.9 1.7 %collective-permute-start.4 = (bf16[128,512]{1,0:T(8,128)(2,1)S(1)}, bf16[128,512]{1,0:T(8,128)(2,1)S(1)}, u32[]{:S(2)}, u32[]{:S(2)}) collective-permute-start(bf16[128,512]{1,0:T(8,128)(2,1)S(1)} %get-tuple-element.86), channel_id=1, source_target_pairs={{0,4},{4,0},{8,12},{12,8},{16,20},{20,16},{24,28},{28,24},{1,5},{5... | collective-permute-start | bytes 393224 | tf_op jit(solution)/shard_map/ppermute | solution.py:399
  18.0 1.8 %collective-permute-start.9 = (bf16[256,768]{1,0:T(8,128)(2,1)S(1)}, bf16[256,768]{1,0:T(8,128)(2,1)S(1)}, u32[]{:S(2)}, u32[]{:S(2)}) collective-permute-start(bf16[256,768]{1,0:T(8,128)(2,1)S(1)} %get-tuple-element.93.d_second_ref.refs_1_), channel_id=1, source_target_pairs={{0,4},{4,0},{8,12},{12,8},{16,20},{20,16},{24,28},{28,24},{1,5},{5... | collective-permute-start | bytes 1179656 | tf_op jit(solution)/shard_map/ppermute | solution.py:399
  18.2 3.8 %collective-permute-start.5 = (bf16[256,768]{1,0:T(8,128)(2,1)S(1)}, bf16[256,768]{1,0:T(8,128)(2,1)S(1)}, u32[]{:S(2)}, u32[]{:S(2)}) collective-permute-start(bf16[256,768]{1,0:T(8,128)(2,1)S(1)} %get-tuple-element.92.d_first_ref.refs_0_), channel_id=1, source_target_pairs={{0,4},{4,0},{8,12},{12,8},{16,20},{20,16},{24,28},{28,24},{1,5},{5... | collective-permute-start | bytes 1179656 | tf_op jit(solution)/shard_map/ppermute | solution.py:399
  20.4 11.2 %collective-permute-start.10 = (bf16[256,768]{1,0:T(8,128)(2,1)S(1)}, bf16[256,768]{1,0:T(8,128)(2,1)S(1)}, u32[]{:S(2)}, u32[]{:S(2)}) collective-permute-start(bf16[256,768]{1,0:T(8,128)(2,1)S(1)} %get-tuple-element.101), channel_id=1, source_target_pairs={{0,1},{1,0},{2,3},{3,2},{4,5},{5,4},{6,7},{7,6},{8,9},{9,8},{10,11... | collective-permute-start | bytes 1179656 | tf_op jit(solution)/shard_map/ppermute | solution.py:399
  22.4 11.4 %collective-permute-start.6 = (bf16[128,768]{1,0:T(8,128)(2,1)S(1)}, bf16[128,768]{1,0:T(8,128)(2,1)S(1)}, u32[]{:S(2)}, u32[]{:S(2)}) collective-permute-start(bf16[128,768]{1,0:T(8,128)(2,1)S(1)} %get-tuple-element.96), channel_id=1, source_target_pairs={{0,8},{4,12},{8,0},{12,4},{16,24},{20,28},{24,16},{28,20},{1,9},{5... | collective-permute-start | bytes 589832 | tf_op jit(solution)/shard_map/ppermute | solution.py:399
  23.7 11.5 %collective-permute-start.7 = (bf16[128,768]{1,0:T(8,128)(2,1)S(1)}, bf16[128,768]{1,0:T(8,128)(2,1)S(1)}, u32[]{:S(2)}, u32[]{:S(2)}) collective-permute-start(bf16[128,768]{1,0:T(8,128)(2,1)S(1)} %get-tuple-element.97), channel_id=1, source_target_pairs={{0,16},{4,20},{8,24},{12,28},{16,0},{20,4},{24,8},{28,12},{1,17},{... | collective-permute-start | bytes 589832 | tf_op jit(solution)/shard_map/ppermute | solution.py:399
  24.5 10.7 %collective-permute-start.8 = (bf16[128,768]{1,0:T(8,128)(2,1)S(1)}, bf16[128,768]{1,0:T(8,128)(2,1)S(1)}, u32[]{:S(2)}, u32[]{:S(2)}) collective-permute-start(bf16[128,768]{1,0:T(8,128)(2,1)S(1)} %get-tuple-element.98), channel_id=1, source_target_pairs={{0,24},{4,28},{8,16},{12,20},{16,8},{20,12},{24,0},{28,4},{1,25},{... | collective-permute-start | bytes 589832 | tf_op jit(solution)/shard_map/ppermute | solution.py:399
  31.7 6.6 %collective-permute-start.11 = (bf16[64,768]{1,0:T(8,128)(2,1)S(1)}, bf16[64,768]{1,0:T(8,128)(2,1)S(1)}, u32[]{:S(2)}, u32[]{:S(2)}) collective-permute-start(bf16[64,768]{1,0:T(8,128)(2,1)S(1)} %get-tuple-element.109), channel_id=1, source_target_pairs={{0,8},{4,12},{8,0},{12,4},{16,24},{20,28},{24,16},{28,20},{1,9},{5... | collective-permute-start | bytes 294920 | tf_op jit(solution)/shard_map/ppermute | solution.py:399
  32.9 6.1 %collective-permute-start.12 = (bf16[64,768]{1,0:T(8,128)(2,1)S(1)}, bf16[64,768]{1,0:T(8,128)(2,1)S(1)}, u32[]{:S(2)}, u32[]{:S(2)}) collective-permute-start(bf16[64,768]{1,0:T(8,128)(2,1)S(1)} %get-tuple-element.110), channel_id=1, source_target_pairs={{0,16},{4,20},{8,24},{12,28},{16,0},{20,4},{24,8},{28,12},{1,17},{... | collective-permute-start | bytes 294920 | tf_op jit(solution)/shard_map/ppermute | solution.py:399
  33.8 6.8 %collective-permute-start.13 = (bf16[64,768]{1,0:T(8,128)(2,1)S(1)}, bf16[64,768]{1,0:T(8,128)(2,1)S(1)}, u32[]{:S(2)}, u32[]{:S(2)}) collective-permute-start(bf16[64,768]{1,0:T(8,128)(2,1)S(1)} %get-tuple-element.111), channel_id=1, source_target_pairs={{0,24},{4,28},{8,16},{12,20},{16,8},{20,12},{24,0},{28,4},{1,25},{... | collective-permute-start | bytes 294920 | tf_op jit(solution)/shard_map/ppermute | solution.py:399
  35.4 7.9 %collective-permute-start.20 = (bf16[64,768]{1,0:T(8,128)(2,1)S(1)}, bf16[64,768]{1,0:T(8,128)(2,1)S(1)}, u32[]{:S(2)}, u32[]{:S(2)}) collective-permute-start(bf16[64,768]{1,0:T(8,128)(2,1)S(1)} %get-tuple-element.129), channel_id=1, source_target_pairs={{0,1},{1,0},{2,3},{3,2},{4,5},{5,4},{6,7},{7,6},{8,9},{9,8},{10,11... | collective-permute-start | bytes 294920 | tf_op jit(solution)/shard_map/ppermute | solution.py:399
  37.0 6.6 %collective-permute-start.16 = (bf16[64,1024]{1,0:T(8,128)(2,1)S(1)}, bf16[64,1024]{1,0:T(8,128)(2,1)S(1)}, u32[]{:S(2)}, u32[]{:S(2)}) collective-permute-start(bf16[64,1024]{1,0:T(8,128)(2,1)S(1)} %get-tuple-element.123), channel_id=1, source_target_pairs={{0,8},{4,12},{8,0},{12,4},{16,24},{20,28},{24,16},{28,20},{1,9},{5... | collective-permute-start | bytes 393224 | tf_op jit(solution)/shard_map/ppermute | solution.py:399
  38.2 5.4 %collective-permute-start.17 = (bf16[64,1024]{1,0:T(8,128)(2,1)S(1)}, bf16[64,1024]{1,0:T(8,128)(2,1)S(1)}, u32[]{:S(2)}, u32[]{:S(2)}) collective-permute-start(bf16[64,1024]{1,0:T(8,128)(2,1)S(1)} %get-tuple-element.124), channel_id=1, source_target_pairs={{0,16},{4,20},{8,24},{12,28},{16,0},{20,4},{24,8},{28,12},{1,17},{... | collective-permute-start | bytes 393224 | tf_op jit(solution)/shard_map/ppermute | solution.py:399
  39.1 5.9 %collective-permute-start.18 = (bf16[64,1024]{1,0:T(8,128)(2,1)S(1)}, bf16[64,1024]{1,0:T(8,128)(2,1)S(1)}, u32[]{:S(2)}, u32[]{:S(2)}) collective-permute-start(bf16[64,1024]{1,0:T(8,128)(2,1)S(1)} %get-tuple-element.125), channel_id=1, source_target_pairs={{0,24},{4,28},{8,16},{12,20},{16,8},{20,12},{24,0},{28,4},{1,25},{... | collective-permute-start | bytes 393224 | tf_op jit(solution)/shard_map/ppermute | solution.py:399
  40.6 7.5 %collective-permute-start.14 = (bf16[64,768]{1,0:T(8,128)(2,1)S(1)}, bf16[64,768]{1,0:T(8,128)(2,1)S(1)}, u32[]{:S(2)}, u32[]{:S(2)}) collective-permute-start(bf16[64,768]{1,0:T(8,128)(2,1)S(1)} %add_convert_fusion.3), channel_id=1, source_target_pairs={{0,2},{1,3},{2,0},{3,1},{4,6},{5,7},{6,4},{7,5},{8,10},{9,11},{10,... | collective-permute-start | bytes 294920 | tf_op jit(solution)/shard_map/ppermute | solution.py:399
  43.3 6.3 %collective-permute-start.21 = (bf16[64,768]{1,0:T(8,128)(2,1)S(1)}, bf16[64,768]{1,0:T(8,128)(2,1)S(1)}, u32[]{:S(2)}, u32[]{:S(2)}) collective-permute-start(bf16[64,768]{1,0:T(8,128)(2,1)S(1)} %add_convert_fusion.1), channel_id=1, source_target_pairs={{0,2},{1,3},{2,0},{3,1},{4,6},{5,7},{6,4},{7,5},{8,10},{9,11},{10,... | collective-permute-start | bytes 294920 | tf_op jit(solution)/shard_map/ppermute | solution.py:399
  45.8 5.4 %collective-permute-start.19 = (bf16[128,1024]{1,0:T(8,128)(2,1)S(1)}, bf16[128,1024]{1,0:T(8,128)(2,1)S(1)}, u32[]{:S(2)}, u32[]{:S(2)}) collective-permute-start(bf16[128,1024]{1,0:T(8,128)(2,1)S(1)} %get-tuple-element.127), channel_id=1, source_target_pairs={{0,4},{4,0},{8,12},{12,8},{16,20},{20,16},{24,28},{28,24},{1,5},{5... | collective-permute-start | bytes 786440 | tf_op jit(solution)/shard_map/ppermute | solution.py:399
  48.1 4.7 %collective-permute-start.15 = (bf16[64,768]{1,0:T(8,128)(2,1)S(1)}, bf16[64,768]{1,0:T(8,128)(2,1)S(1)}, u32[]{:S(2)}, u32[]{:S(2)}) collective-permute-start(bf16[64,768]{1,0:T(8,128)(2,1)S(1)} %add_convert_fusion.2.refs_2_), channel_id=1, source_target_pairs={{0,1},{1,0},{2,3},{3,2},{4,5},{5,4},{6,7},{7,6},{8,9},{9,8},{10,11... | collective-permute-start | bytes 294920 | tf_op jit(solution)/shard_map/ppermute | solution.py:399
  49.6 4.7 %collective-permute-start.22 = (bf16[64,768]{1,0:T(8,128)(2,1)S(1)}, bf16[64,768]{1,0:T(8,128)(2,1)S(1)}, u32[]{:S(2)}, u32[]{:S(2)}) collective-permute-start(bf16[64,768]{1,0:T(8,128)(2,1)S(1)} %add_convert_fusion.refs_0_), channel_id=1, source_target_pairs={{0,1},{1,0},{2,3},{3,2},{4,5},{5,4},{6,7},{7,6},{8,9},{9,8},{10,11... | collective-permute-start | bytes 294920 | tf_op jit(solution)/shard_map/ppermute | solution.py:399
